TPU v7x, 32 devices: a whole 2x2x4 slice. The times are simulated.
32 devices in a mesh: ctx: 16 (over z, y, x), fsdp: 2 (over core).
Axes of the slice: x: 2, y: 2, z: 4, core: 2. Of those that a mesh axis runs over, the one named last changes fastest.
Arguments:
- hidden_in: bfloat16 [2, 2048, 2048], P('fsdp', 'ctx'), may hold values from -6 to 6
- teacher: bfloat16 [2, 2048, 2048], P('fsdp', 'ctx'), may hold values from -8 to 8
- doc_starts: int32 [2, 4], P('fsdp'), may hold values from 0 to 2047, as said below
- routes: int32 [2, 2048, 6], P('fsdp', 'ctx'), may hold values from 0 to 15, all different within a row; in each aligned block of 128 rows (0 to 127, 128 to 255, ..., all dimensions but the last counted through in order) at most 72 rows name the same one
- gate_logits: float32 [2, 2048, 6], P('fsdp', 'ctx'), may hold values from -3 to 3
- input_gain: bfloat16 [2048], P(('ctx', 'fsdp')), may hold values from 0.5 to 1.5
- query_weight: bfloat16 [2048, 3072], P(('ctx', 'fsdp')), may hold values from -0.125 to 0.125
- latent_weight: bfloat16 [2048, 576], P(('ctx', 'fsdp')), may hold values from -0.125 to 0.125
- latent_gain: bfloat16 [512], P(('ctx', 'fsdp')), may hold values from 0.5 to 1.5
- expand_weight: bfloat16 [512, 4096], P(('ctx', 'fsdp')), may hold values from -0.25 to 0.25
- output_weight: bfloat16 [2048, 2048], P(('ctx', 'fsdp')), may hold values from -1 to 1
- mixer_gain: bfloat16 [2048], P(('ctx', 'fsdp')), may hold values from 0.5 to 1.5
- shared_gate: bfloat16 [2048, 2816], P(('ctx', 'fsdp')), may hold values from -0.125 to 0.125
- shared_up: bfloat16 [2048, 2816], P(('ctx', 'fsdp')), may hold values from -0.125 to 0.125
- shared_down: bfloat16 [2816, 2048], P(('ctx', 'fsdp')), may hold values from -0.15625 to 0.15625
- expert_gate: bfloat16 [16, 2048, 1408], P('ctx', None, 'fsdp'), may hold values from -0.25 to 0.25
- expert_up: bfloat16 [16, 2048, 1408], P('ctx', None, 'fsdp'), may hold values from -0.25 to 0.25
- expert_down: bfloat16 [16, 1408, 2048], P('ctx', 'fsdp'), may hold values from -0.21875 to 0.21875
Outputs:
- layer_out: bfloat16 [2, 2048, 2048], P('fsdp', 'ctx')
- loss_value: float32 [], replicated
- grad_input: float32 [2, 2048, 2048], P('fsdp', 'ctx')
- grad_input_gain: float32 [2048], P(('ctx', 'fsdp'))
- grad_query_weight: float32 [2048, 3072], P(('ctx', 'fsdp'))
- grad_latent_weight: float32 [2048, 576], P(('ctx', 'fsdp'))
- grad_latent_gain: float32 [512], P(('ctx', 'fsdp'))
- grad_expand_weight: float32 [512, 4096], P(('ctx', 'fsdp'))
- grad_output_weight: float32 [2048, 2048], P(('ctx', 'fsdp'))
- grad_mixer_gain: float32 [2048], P(('ctx', 'fsdp'))
- grad_shared_gate: float32 [2048, 2816], P(('ctx', 'fsdp'))
- grad_shared_up: float32 [2048, 2816], P(('ctx', 'fsdp'))
- grad_shared_down: float32 [2816, 2048], P(('ctx', 'fsdp'))
- grad_expert_gate: float32 [16, 2048, 1408], P('ctx', None, 'fsdp')
- grad_expert_up: float32 [16, 2048, 1408], P('ctx', None, 'fsdp')
- grad_expert_down: float32 [16, 1408, 2048], P('ctx', 'fsdp')
Inputs may be any that keep to these rules, and one draw needn't show every extreme that they name: `doc_starts`: in each stream the 4 starts rise strictly and the first is 0; one document begins within the first 128 positions and ends within the last 128. `routes`: each row names 6 different experts; within the rows of one device no expert is named more than 72 times.
All inputs are finite; a program needn't handle non-finite values.
Results may differ from a plain program's by a relative error of at most 0.019.
Values may be sent and summed in bfloat16 or wider, within the bound.
A program may use at most 384 MiB of HBM per device.

v0:
```python
import math

import jax
import jax.numpy as jnp
from jax import lax
from jax.sharding import PartitionSpec as P

D = 2048
H = 16
DN = 128
DR = 64
DV = 128
KVR = 512
TOPK = 6


EPS = 1e-06
NEG = -1e30
HIGH = lax.Precision.HIGHEST


def norm_forward(rows, gain):
    factor = lax.rsqrt(jnp.mean(rows * rows, axis=-1, keepdims=True) + EPS)
    return (rows * factor * gain, factor)


def norm_back(rows, factor, gain, grad_out):
    scaled = grad_out * gain
    normed = rows * factor
    grad_gain = jnp.sum(grad_out * normed, axis=0)
    grad_rows = factor * (scaled - normed * jnp.mean(scaled * normed, axis=-1, keepdims=True))
    return (grad_rows, grad_gain)


def rotate(values, cosine, sine):
    half = values.shape[-1] // 2
    first = values[..., :half]
    second = values[..., half:]
    return jnp.concatenate(
        [first * cosine - second * sine, second * cosine + first * sine], axis=-1
    )


def doc_tables(starts, positions):
    inside = starts[None, :] <= positions[:, None]
    doc_ids = jnp.sum(inside.astype(jnp.int32), axis=1)
    first = jnp.max(jnp.where(inside, starts[None, :], 0), axis=1)
    return (doc_ids, positions - first)


def rope_tables(offsets):
    freqs = 10000.0 ** (-(jnp.arange(DR // 2, dtype=jnp.float32) * 2.0) / DR)
    angle = offsets.astype(jnp.float32)[:, None] * freqs[None, :]
    return (jnp.cos(angle), jnp.sin(angle))


def silu_grads(gate_val, up_val, grad_hidden):
    sigma = jax.nn.sigmoid(gate_val)
    grad_gate = grad_hidden * up_val * sigma * (1.0 + gate_val * (1.0 - sigma))
    grad_up = grad_hidden * gate_val * sigma
    return (grad_gate.astype(jnp.bfloat16), grad_up.astype(jnp.bfloat16))


def dot_first(left, right):
    return lax.dot_general(
        left, right, (((0,), (0,)), ((), ())), preferred_element_type=jnp.float32
    )


def dot_last(left, right):
    return lax.dot_general(
        left, right, (((1,), (1,)), ((), ())), preferred_element_type=jnp.float32
    )


def wide_first(left, right):
    return lax.dot_general(
        left, right, (((0,), (0,)), ((), ())), precision=HIGH, preferred_element_type=jnp.float32
    )


def block_scores(queries, block, rope_block):
    nope = jnp.einsum(
        "qhd,khd->hqk", queries[..., :DN], block[..., :DN], preferred_element_type=jnp.float32
    )
    return nope + jnp.einsum(
        "qhr,kr->hqk", queries[..., DN:], rope_block, preferred_element_type=jnp.float32
    )


def in_blocks(update, carry, pieces):
    count = pieces[0].shape[0]
    width = math.gcd(count, 512)
    splits = tuple((item.reshape((count // width, width) + item.shape[1:]) for item in pieces))
    offsets = width * jnp.arange(count // width, dtype=jnp.int32)

    def advance(state, inputs):
        return (update(state, inputs[0], inputs[1]), None)

    carry, ignored_value = lax.scan(advance, carry, (splits, offsets))
    return carry


def shards(
    hidden_in,
    teacher,
    doc_starts,
    routes,
    gate_logits,
    input_gain,
    query_weight,
    latent_weight,
    latent_gain,
    expand_weight,
    output_weight,
    mixer_gain,
    shared_gate,
    shared_up,
    shared_down,
    expert_gate,
    expert_up,
    expert_down,
):
    f32 = jnp.float32
    bf16 = jnp.bfloat16
    cycle = lax.axis_size("ctx")
    groups = lax.axis_size("fsdp")
    tokens = hidden_in.shape[1]
    length = tokens * cycle
    local = expert_gate.shape[0]
    experts_total = cycle * local
    capacity = min(tokens, 3 * tokens * TOPK // (2 * experts_total))
    scale = (DN + DR) ** (-0.5)
    dense = (
        input_gain,
        query_weight,
        latent_weight,
        latent_gain,
        expand_weight,
        output_weight,
        mixer_gain,
        shared_gate,
        shared_up,
        shared_down,
    )
    gathered = (
        lax.all_gather(dense[0], ("ctx", "fsdp"), axis=0, tiled=True),
        lax.all_gather(dense[1], ("ctx", "fsdp"), axis=0, tiled=True),
        lax.all_gather(dense[2], ("ctx", "fsdp"), axis=0, tiled=True),
        lax.all_gather(dense[3], ("ctx", "fsdp"), axis=0, tiled=True),
        lax.all_gather(dense[4], ("ctx", "fsdp"), axis=0, tiled=True),
        lax.all_gather(dense[5], ("ctx", "fsdp"), axis=0, tiled=True),
        lax.all_gather(dense[6], ("ctx", "fsdp"), axis=0, tiled=True),
        lax.all_gather(dense[7], ("ctx", "fsdp"), axis=0, tiled=True),
        lax.all_gather(dense[8], ("ctx", "fsdp"), axis=0, tiled=True),
        lax.all_gather(dense[9], ("ctx", "fsdp"), axis=0, tiled=True),
    )
    (
        first_norm_scale,
        query_project_weight,
        latent_project_weight,
        latent_norm_scale,
        latent_expand_weight,
        output_project_weight,
        second_norm_scale,
        w_gate,
        w_up,
        w_down,
    ) = gathered
    starts = doc_starts[0]
    positions = lax.axis_index("ctx") * tokens + jnp.arange(tokens, dtype=jnp.int32)
    query_doc, offsets = doc_tables(starts, positions)
    cosine, sine = rope_tables(offsets)

    def allowed_mask(start, count):
        key_pos = start + jnp.arange(count, dtype=jnp.int32)
        key_doc, ignored_value = doc_tables(starts, key_pos)
        return (
            (key_doc[None, :] == query_doc[:, None]) & (key_pos[None, :] <= positions[:, None])
        )[None]

    residual_stream = hidden_in[0].astype(f32)
    normed_one, factor_one = norm_forward(residual_stream, first_norm_scale.astype(f32))
    act_one = normed_one.astype(bf16)
    query_raw = jnp.dot(act_one, query_project_weight, preferred_element_type=f32).reshape(
        tokens, H, DN + DR
    )
    query_rope = rotate(query_raw[..., DN:], cosine[:, None, :], sine[:, None, :])
    queries = (jnp.concatenate([query_raw[..., :DN], query_rope], axis=-1) * scale).astype(bf16)
    latent_raw = jnp.dot(act_one, latent_project_weight, preferred_element_type=f32)
    latent_normed, factor_latent = norm_forward(latent_raw[:, :KVR], latent_norm_scale.astype(f32))
    latent = latent_normed.astype(bf16)
    key_rope = rotate(latent_raw[:, KVR:], cosine, sine).astype(bf16)
    expanded = jnp.dot(latent, latent_expand_weight, preferred_element_type=f32).astype(bf16)
    payload = (expanded, key_rope)

    def attend_piece(carry, pieces, start):
        top, grand_total, summed = carry
        block, rope_block = pieces
        count = block.shape[0]
        block = block.reshape(count, H, DN + DV)
        allowed = allowed_mask(start, count)
        scores = jnp.where(allowed, block_scores(queries, block, rope_block), NEG)
        new_top = jnp.maximum(top, jnp.max(scores, axis=-1))
        weights_now = jnp.where(allowed, jnp.exp(scores - new_top[..., None]), 0.0)
        shrink = jnp.exp(top - new_top)
        grand_total = grand_total * shrink + jnp.sum(weights_now, axis=-1)
        summed = summed * shrink[..., None] + jnp.einsum(
            "hqk,khv->hqv", weights_now.astype(bf16), block[..., DN:], preferred_element_type=f32
        )
        return (new_top, grand_total, summed)

    start_state = (
        jnp.full((H, tokens), NEG, f32),
        jnp.zeros((H, tokens), f32),
        jnp.zeros((H, tokens, DV), f32),
    )
    top, grand_total, summed = in_blocks(
        attend_piece,
        start_state,
        (
            lax.all_gather(payload[0], "ctx", axis=0, tiled=True),
            lax.all_gather(payload[1], "ctx", axis=0, tiled=True),
        ),
    )
    attended = jnp.transpose(summed / grand_total[..., None], (1, 0, 2))
    log_total = top + jnp.log(grand_total)
    attended_low = attended.reshape(tokens, H * DV).astype(bf16)
    mixed = residual_stream + jnp.dot(
        attended_low, output_project_weight, preferred_element_type=f32
    )
    normed_two, factor_two = norm_forward(mixed, second_norm_scale.astype(f32))
    act_two = normed_two.astype(bf16)
    gate_val = jnp.dot(act_two, w_gate, preferred_element_type=f32)
    up_val = jnp.dot(act_two, w_up, preferred_element_type=f32)
    hidden_shared = (jax.nn.silu(gate_val) * up_val).astype(bf16)
    shared_out = jnp.dot(hidden_shared, w_down, preferred_element_type=f32)
    route_flat = routes[0].reshape(-1)
    assigned = route_flat.shape[0]
    onehot = (route_flat[:, None] == jnp.arange(experts_total, dtype=jnp.int32)[None, :]).astype(
        jnp.int32
    )
    order = jnp.sum(jnp.cumsum(onehot, axis=0) * onehot, axis=1) - 1
    slot_of = route_flat * capacity + order
    table = (
        jnp.zeros((experts_total * capacity,), jnp.int32)
        .at[slot_of]
        .set(jnp.arange(assigned, dtype=jnp.int32) + 1)
    )
    filled = (table > 0)[:, None]
    entry = jnp.maximum(table - 1, 0)
    nothing = jnp.zeros((), bf16)
    full_gate, full_up, full_down = (
        lax.all_gather(expert_gate, "fsdp", axis=2, tiled=True),
        lax.all_gather(expert_up, "fsdp", axis=2, tiled=True),
        lax.all_gather(expert_down, "fsdp", axis=1, tiled=True),
    )
    outgoing = jnp.where(filled, act_two[entry // TOPK], nothing).reshape(
        cycle, local * capacity, D
    )
    arrived = lax.all_to_all(outgoing, "ctx", split_axis=0, concat_axis=0, tiled=True).reshape(
        cycle, local, capacity, D
    )
    slot = 0
    rows = arrived[:, slot].reshape(cycle * capacity, D)
    gate_e = jnp.dot(rows, full_gate[slot], preferred_element_type=f32)
    up_e = jnp.dot(rows, full_up[slot], preferred_element_type=f32)
    hidden_e = (jax.nn.silu(gate_e) * up_e).astype(bf16)
    kept = [(rows, gate_e, up_e, hidden_e)]
    outputs = (
        jnp.dot(hidden_e, full_down[slot], preferred_element_type=f32)
        .astype(bf16)
        .reshape(cycle, 1, capacity, D)
    )
    returned = lax.all_to_all(
        outputs.reshape(cycle, local * capacity, D), "ctx", split_axis=0, concat_axis=0, tiled=True
    )
    expert_out = returned.reshape(experts_total * capacity, D)
    probs = jax.nn.softmax(gate_logits[0], axis=-1)
    picked = expert_out[slot_of].reshape(tokens, TOPK, D)
    routed = jnp.sum(probs[..., None] * picked.astype(f32), axis=1)
    result = mixed + shared_out + routed
    diff = result - teacher[0].astype(f32)
    loss_value = lax.psum(0.5 * jnp.sum(diff * diff), ("ctx", "fsdp")) / (
        tokens * cycle * groups * D
    )
    grad_shared = diff.astype(bf16)
    grad_w_down = dot_first(hidden_shared, grad_shared)
    grad_gate_s, grad_up_s = silu_grads(gate_val, up_val, dot_last(grad_shared, w_down))
    grad_w_gate = dot_first(act_two, grad_gate_s)
    grad_w_up = dot_first(act_two, grad_up_s)
    grad_act_two = dot_last(grad_gate_s, w_gate) + dot_last(grad_up_s, w_up)
    grad_picked = (probs[..., None] * diff[:, None, :]).reshape(assigned, D).astype(bf16)
    outgoing = jnp.where(filled, grad_picked[entry], nothing).reshape(cycle, local * capacity, D)
    grads_in = lax.all_to_all(outgoing, "ctx", split_axis=0, concat_axis=0, tiled=True).reshape(
        cycle, local, capacity, D
    )
    slot = 0
    rows, gate_e, up_e, hidden_e = kept[slot]
    grad_y = grads_in[:, slot].reshape(cycle * capacity, D)
    grad_down_list = [dot_first(hidden_e, grad_y)]
    grad_gate_e, grad_up_e = silu_grads(gate_e, up_e, dot_last(grad_y, full_down[slot]))
    grad_gate_list = [dot_first(rows, grad_gate_e)]
    grad_up_list = [dot_first(rows, grad_up_e)]
    row_grad = dot_last(grad_gate_e, full_gate[slot]) + dot_last(grad_up_e, full_up[slot])
    backs = row_grad.reshape(cycle, 1, capacity, D)
    sent_back = lax.all_to_all(
        backs.reshape(cycle, local * capacity, D).astype(jnp.bfloat16),
        "ctx",
        split_axis=0,
        concat_axis=0,
        tiled=True,
    ).astype(jnp.float32)
    grad_rows = sent_back.reshape(experts_total * capacity, D)
    grad_act_two = grad_act_two + jnp.sum(grad_rows[slot_of].reshape(tokens, TOPK, D), axis=1)
    expert_shares = (
        lax.psum_scatter(
            jnp.stack(grad_gate_list).astype(jnp.bfloat16), "fsdp", scatter_dimension=2, tiled=True
        ).astype(jnp.float32),
        lax.psum_scatter(
            jnp.stack(grad_up_list).astype(jnp.bfloat16), "fsdp", scatter_dimension=2, tiled=True
        ).astype(jnp.float32),
        lax.psum_scatter(
            jnp.stack(grad_down_list).astype(jnp.bfloat16), "fsdp", scatter_dimension=1, tiled=True
        ).astype(jnp.float32),
    )
    grad_mixed_norm, grad_gain_two = norm_back(
        mixed, factor_two, second_norm_scale.astype(f32), grad_act_two
    )
    grad_mixed = diff + grad_mixed_norm
    grad_mixed_low = grad_mixed.astype(bf16)
    grad_w_output = dot_first(attended_low, grad_mixed_low)
    grad_attended = (
        dot_last(grad_mixed_low, output_project_weight).astype(bf16).reshape(tokens, H, DV)
    )
    delta = jnp.transpose(jnp.sum(grad_attended.astype(f32) * attended, axis=-1))
    w_expand_wide = latent_expand_weight.astype(f32)

    def key_piece(carry, pieces, start):
        grad_query = carry[0]
        block_in, rope_block = pieces
        block = block_in
        count = block.shape[0]
        block = block.reshape(count, H, DN + DV)
        allowed = allowed_mask(start, count)
        scores = jnp.where(allowed, block_scores(queries, block, rope_block), NEG)
        probs_now = jnp.where(allowed, jnp.exp(scores - log_total[..., None]), 0.0)
        grad_probs = jnp.einsum(
            "qhv,khv->hqk", grad_attended, block[..., DN:], preferred_element_type=f32
        )
        grad_scores = (probs_now * (grad_probs - delta[..., None])).astype(bf16)
        grad_values = jnp.einsum(
            "hqk,qhv->khv", probs_now.astype(bf16), grad_attended, preferred_element_type=f32
        )
        grad_nope = jnp.einsum(
            "hqk,qhd->khd", grad_scores, queries[..., :DN], preferred_element_type=f32
        )
        grad_rope = jnp.einsum(
            "hqk,qhr->kr", grad_scores, queries[..., DN:], preferred_element_type=f32
        )
        grad_query_nope = jnp.einsum(
            "hqk,khd->qhd", grad_scores, block[..., :DN], preferred_element_type=f32
        )
        grad_query_rope = jnp.einsum(
            "hqk,kr->qhr", grad_scores, rope_block, preferred_element_type=f32
        )
        grad_query = grad_query + jnp.concatenate([grad_query_nope, grad_query_rope], axis=-1)
        merged = jnp.concatenate([grad_nope, grad_values], axis=-1).reshape(count, H * (DN + DV))
        grad_rope_all = lax.dynamic_update_slice_in_dim(
            carry[2], lax.dynamic_slice_in_dim(carry[2], start, count, 0) + grad_rope, start, 0
        )
        grad_keys_all = lax.dynamic_update_slice_in_dim(
            carry[1], lax.dynamic_slice_in_dim(carry[1], start, count, 0) + merged, start, 0
        )
        return (grad_query, grad_keys_all, grad_rope_all)

    payload_back = (expanded, key_rope)
    back_state = (
        jnp.zeros((tokens, H, DN + DR), f32),
        jnp.zeros((length, H * (DN + DV)), f32),
        jnp.zeros((length, DR), f32),
    )
    folded = in_blocks(
        key_piece,
        back_state,
        (
            lax.all_gather(payload_back[0], "ctx", axis=0, tiled=True),
            lax.all_gather(payload_back[1], "ctx", axis=0, tiled=True),
        ),
    )
    grad_query = folded[0]
    grad_keys_mine, grad_rope_mine = (
        lax.psum_scatter(
            folded[1].astype(jnp.bfloat16), "ctx", scatter_dimension=0, tiled=True
        ).astype(jnp.float32),
        lax.psum_scatter(
            folded[2].astype(jnp.bfloat16), "ctx", scatter_dimension=0, tiled=True
        ).astype(jnp.float32),
    )
    grad_w_expand = wide_first(latent.astype(f32), grad_keys_mine)
    grad_latent_in = jnp.dot(grad_keys_mine, w_expand_wide.T, precision=HIGH)
    grad_latent_norm, grad_gain_latent = norm_back(
        latent_raw[:, :KVR], factor_latent, latent_norm_scale.astype(f32), grad_latent_in
    )
    grad_latent_all = jnp.concatenate(
        [grad_latent_norm, rotate(grad_rope_mine, cosine, -sine)], axis=-1
    ).astype(bf16)
    grad_w_latent = dot_first(act_one, grad_latent_all)
    grad_query = grad_query * scale
    grad_query = jnp.concatenate(
        [grad_query[..., :DN], rotate(grad_query[..., DN:], cosine[:, None, :], -sine[:, None, :])],
        axis=-1,
    )
    grad_query_low = grad_query.reshape(tokens, H * (DN + DR)).astype(bf16)
    grad_w_query = dot_first(act_one, grad_query_low)
    grad_act_one = dot_last(grad_query_low, query_project_weight) + dot_last(
        grad_latent_all, latent_project_weight
    )
    grad_stream_norm, grad_gain_one = norm_back(
        residual_stream, factor_one, first_norm_scale.astype(f32), grad_act_one
    )
    grad_input = (grad_mixed + grad_stream_norm)[None]
    shares = (
        lax.psum_scatter(grad_gain_one, ("ctx", "fsdp"), scatter_dimension=0, tiled=True),
        lax.psum_scatter(grad_w_query, ("ctx", "fsdp"), scatter_dimension=0, tiled=True),
        lax.psum_scatter(grad_w_latent, ("ctx", "fsdp"), scatter_dimension=0, tiled=True),
        lax.psum_scatter(grad_gain_latent, ("ctx", "fsdp"), scatter_dimension=0, tiled=True),
        lax.psum_scatter(grad_w_expand, ("ctx", "fsdp"), scatter_dimension=0, tiled=True),
        lax.psum_scatter(grad_w_output, ("ctx", "fsdp"), scatter_dimension=0, tiled=True),
        lax.psum_scatter(grad_gain_two, ("ctx", "fsdp"), scatter_dimension=0, tiled=True),
        lax.psum_scatter(grad_w_gate, ("ctx", "fsdp"), scatter_dimension=0, tiled=True),
        lax.psum_scatter(grad_w_up, ("ctx", "fsdp"), scatter_dimension=0, tiled=True),
        lax.psum_scatter(grad_w_down, ("ctx", "fsdp"), scatter_dimension=0, tiled=True),
    )
    return (
        result.astype(bf16)[None],
        loss_value,
        grad_input,
        shares[0],
        shares[1],
        shares[2],
        shares[3],
        shares[4],
        shares[5],
        shares[6],
        shares[7],
        shares[8],
        shares[9],
        expert_shares[0],
        expert_shares[1],
        expert_shares[2],
    )


def solution(mesh):
    in_specs = (
        P("fsdp", "ctx", None),
        P("fsdp", "ctx", None),
        P("fsdp", None),
        P("fsdp", "ctx", None),
        P("fsdp", "ctx", None),
        P(("ctx", "fsdp")),
        P(("ctx", "fsdp"), None),
        P(("ctx", "fsdp"), None),
        P(("ctx", "fsdp")),
        P(("ctx", "fsdp"), None),
        P(("ctx", "fsdp"), None),
        P(("ctx", "fsdp")),
        P(("ctx", "fsdp"), None),
        P(("ctx", "fsdp"), None),
        P(("ctx", "fsdp"), None),
        P("ctx", None, "fsdp"),
        P("ctx", None, "fsdp"),
        P("ctx", "fsdp", None),
    )
    out_specs = (
        P("fsdp", "ctx", None),
        P(),
        P("fsdp", "ctx", None),
        P(("ctx", "fsdp")),
        P(("ctx", "fsdp"), None),
        P(("ctx", "fsdp"), None),
        P(("ctx", "fsdp")),
        P(("ctx", "fsdp"), None),
        P(("ctx", "fsdp"), None),
        P(("ctx", "fsdp")),
        P(("ctx", "fsdp"), None),
        P(("ctx", "fsdp"), None),
        P(("ctx", "fsdp"), None),
        P("ctx", None, "fsdp"),
        P("ctx", None, "fsdp"),
        P("ctx", "fsdp", None),
    )
    return jax.shard_map(shards, mesh=mesh, in_specs=in_specs, out_specs=out_specs, check_vma=False)
```

profile of v0, /device:TPU:0, one launch (start us, length us, event | category | flops | bytes accessed | tf_op | source)
XLA Modules:
  0.0 3609.1 jit_solution(10332865758075537936)
XLA Ops:
  12.0 42.3 %all-reduce.7 = (bf16[2048]{0:T(1024)(128)(2,1)S(1)}, bf16[512]{0:T(512)(128)(2,1)S(1)}, bf16[2048]{0:T(1024)(128)(2,1)S(1)}) all-reduce(bf16[2048]{0:T(1024)(128)(2,1)S(1)} %dynamic-update-slice, bf16[512]{0:T(512)(128)(2,1)S(1)} %dynamic-update-slice.1, ...), channel_id=1, replica_groups=mesh['ctx'=16,'fsdp'=2] {'ctx','fsdp'}, use_global_device_ids=true, to_apply=%add | all-reduce | flops 4608 | bytes 18432
  55.5 16.0 all-gather.12.cloned.1.call-done
  74.7 60.7 %all-gather.14.cloned.1.call-done = bf16[512,4096]{1,0:T(8,128)(2,1)} async-done(((bf16[16,4096]{1,0:T(8,128)(2,1)}), bf16[512,4096]{1,0:T(8,128)(2,1)}) %all-gather.14.cloned.1.call-update) | async-done | bytes 4194320 | tf_op jit(solution)/shard_map/all_gather | solution.py:151
  151.1 40.9 %all_gather.53 = bf16[2048,64]{0,1:T(8,128)(2,1)S(1)} all-gather(bf16[128,64]{0,1:T(8,128)(2,1)S(1)} %pad_maximum_fusion.4), channel_id=1, replica_groups=mesh['ctx'=16,'fsdp'=2] {'ctx'}, dimensions={0}, use_global_device_ids=true | all-gather | bytes 278528 | tf_op jit(solution)/shard_map/all_gather | solution.py:223
  192.1 43.4 %all-gather.18.cloned.1.call-done = bf16[2048,3072]{1,0:T(8,128)(2,1)} async-done(((bf16[64,3072]{1,0:T(8,128)(2,1)}), bf16[2048,3072]{1,0:T(8,128)(2,1)}) %all-gather.18.cloned.1.call-update) | async-done | bytes 12582928 | tf_op jit(solution)/shard_map/all_gather | solution.py:148
  235.4 16.8 copy.146
  259.8 168.7 %all-gather.16.cloned.1.call-done = bf16[2048,4096]{1,0:T(8,128)(2,1)} async-done(((bf16[128,4096]{1,0:T(8,128)(2,1)}), bf16[2048,4096]{1,0:T(8,128)(2,1)}) %all-gather.16.cloned.1.call-update) | async-done | bytes 16777232 | tf_op jit(solution)/shard_map/all_gather | solution.py:222
  428.5 21.3 copy.147
  449.8 39.9 %while.30 = (s32[]{:T(128)}, f32[16,128]{1,0:T(8,128)S(1)}, f32[16,128]{1,0:T(8,128)S(1)}, f32[16,128,128]{2,1,0:T(8,128)}, s32[1,4]{1,0:T(1,128)S(1)}, /*index=...) while((s32[]{:T(128)}, f32[16,128]{1,0:T(8,128)S(1)}, ...), condition=%wide.region_8.9_spmd.clone, body=%wide.region_4.8_spmd.clone.sunk | while | flops 681525376 | bytes 46870256 | solution.py:100
  492.6 14.3 all-gather.20.cloned.1.call-done
  528.9 97.7 %all-to-all-done = bf16[16,72,2048]{2,1,0:T(8,128)(2,1)} async-done(((bf16[16,72,2048]{2,1,0:T(8,128)(2,1)}), bf16[16,72,2048]{2,1,0:T(8,128)(2,1)}, u32[]{:S(2)}, u32[]{:S(2)}) %all-to-all-start) | async-done | bytes 4718624 | tf_op jit(solution)/shard_map/all_to_all | solution.py:261
  626.6 12.8 fusion.63
  639.4 14.5 multiply_convert_fusion.2
  654.0 12.8 convolution_convert_fusion.3
  666.8 50.5 %all-to-all-start.1 = ((bf16[16,72,2048]{2,1,0:T(8,128)(2,1)}), bf16[16,72,2048]{2,1,0:T(8,128)(2,1)}, u32[]{:S(2)}, u32[]{:S(2)}) async-start(bf16[16,72,2048]{2,1,0:T(8,128)(2,1)} %bitcast.316), calls=%async_computation.1 | async-start | bytes 9437184 | tf_op jit(solution)/shard_map/all_to_all | solution.py:275
  725.3 131.6 %all-gather.24.cloned.1.call-done = bf16[2048,2816]{1,0:T(8,128)(2,1)} async-done(((bf16[64,2816]{1,0:T(8,128)(2,1)}), bf16[2048,2816]{1,0:T(8,128)(2,1)}) %all-gather.24.cloned.1.call-update) | async-done | bytes 11534352 | tf_op jit(solution)/shard_map/all_gather | solution.py:155
  889.7 62.8 %all-gather.26.cloned.1.call-done = bf16[2816,2048]{1,0:T(8,128)(2,1)} async-done(((bf16[88,2048]{1,0:T(8,128)(2,1)}), bf16[2816,2048]{1,0:T(8,128)(2,1)}) %all-gather.26.cloned.1.call-update) | async-done | bytes 11534352 | tf_op jit(solution)/shard_map/all_gather | solution.py:156
  985.5 109.6 %all_to_all.20 = bf16[16,72,2048]{2,1,0:T(8,128)(2,1)S(1)} all-to-all(bf16[16,72,2048]{2,1,0:T(8,128)(2,1)S(1)} %broadcast_select_fusion), channel_id=1, replica_groups=mesh['ctx'=16,'fsdp'=2] {'ctx'}, dimensions={0} | all-to-all | bytes 9437184 | tf_op jit(solution)/shard_map/all_to_all | solution.py:295
  1095.1 16.3 multiply_convert_fusion
  1121.2 11.6 add_convert_fusion
  1154.3 70.7 %all-to-all-done.3 = bf16[16,72,2048]{2,1,0:T(8,128)(2,1)} async-done(((bf16[16,72,2048]{2,1,0:T(8,128)(2,1)}), bf16[16,72,2048]{2,1,0:T(8,128)(2,1)}, u32[]{:S(2)}, u32[]{:S(2)}) %all-to-all-start.3) | async-done | bytes 4718624 | tf_op jit(solution)/shard_map/all_to_all | solution.py:307
  1272.5 11.3 broadcast_in_dim.147
  1283.9 322.1 %while.31 = (s32[]{:T(128)}, f32[128,16,192]{0,2,1:T(8,128)}, f32[2048,4096]{0,1:T(8,128)}, f32[2048,64]{0,1:T(8,128)}, bf16[4,512,4096]{1,2,0:T(8,128)(2,1)}, /...) while((s32[]{:T(128)}, f32[128,16,192]{0,2,1:T(8,128)}, ...), condition=%wide.region_24.25_spmd.clone, body=%wide.region_22.24_spmd.clone.sunk | while | flops 1758828672 | bytes 146569200 | solution.py:100
  1312.7 11.8 bitcast_add_fusion.4
  1324.6 40.0 %dynamic_update_slice.10 = f32[2048,4096]{0,1:T(8,128)} dynamic-update-slice(f32[2048,4096]{0,1:T(8,128)} %get-tuple-element.724, f32[512,4096]{0,1:T(8,128)} %bitcast_add_fusion.4, s32[]{:T(128)S(6)} %select_n.102, s32[]{:T(128)} %constant.37.clone.1..sunk.1) | dynamic-update-slice | bytes 16777220 | tf_op jit(solution)/shard_map/while/body/eval_jaxpr/dynamic_update_slice | solution.py:372
  1393.8 11.8 bitcast_add_fusion.4
  1405.6 40.0 %dynamic_update_slice.10 = f32[2048,4096]{0,1:T(8,128)} dynamic-update-slice(f32[2048,4096]{0,1:T(8,128)} %get-tuple-element.724, f32[512,4096]{0,1:T(8,128)} %bitcast_add_fusion.4, s32[]{:T(128)S(6)} %select_n.102, s32[]{:T(128)} %constant.37.clone.1..sunk.1) | dynamic-update-slice | bytes 16777220 | tf_op jit(solution)/shard_map/while/body/eval_jaxpr/dynamic_update_slice | solution.py:372
  1474.8 11.8 bitcast_add_fusion.4
  1486.6 40.0 %dynamic_update_slice.10 = f32[2048,4096]{0,1:T(8,128)} dynamic-update-slice(f32[2048,4096]{0,1:T(8,128)} %get-tuple-element.724, f32[512,4096]{0,1:T(8,128)} %bitcast_add_fusion.4, s32[]{:T(128)S(6)} %select_n.102, s32[]{:T(128)} %constant.37.clone.1..sunk.1) | dynamic-update-slice | bytes 16777220 | tf_op jit(solution)/shard_map/while/body/eval_jaxpr/dynamic_update_slice | solution.py:372
  1567.0 38.9 %dynamic_update_slice.10 = f32[2048,4096]{0,1:T(8,128)} dynamic-update-slice(f32[2048,4096]{0,1:T(8,128)} %get-tuple-element.724, f32[512,4096]{0,1:T(8,128)} %bitcast_add_fusion.4, s32[]{:T(128)S(6)} %select_n.102, s32[]{:T(128)} %constant.37.clone.1..sunk.1) | dynamic-update-slice | bytes 16777220 | tf_op jit(solution)/shard_map/while/body/eval_jaxpr/dynamic_update_slice | solution.py:372
  1608.1 17.5 convert_element_type.230
  1625.6 21.3 copy.178
  1648.8 12.5 fusion.52
  1661.3 27.9 copy.182
  1701.7 12.7 fusion.53
  1714.4 28.0 copy.184
  1823.4 222.0 %reduce-scatter.37.cloned.1.call-done = bf16[128,4096]{1,0:T(8,128)(2,1)} async-done(((bf16[2048,4096]{1,0:T(8,128)(2,1)}), bf16[128,4096]{1,0:T(8,128)(2,1)}) %reduce-scatter.37.cloned.1.call-update) | async-done | bytes 1048592
  2059.5 11.8 fusion.135
  2078.2 15.5 copy.183
  2106.0 15.3 copy.185
  2133.9 47.0 %all-reduce.6 = (f32[]{:T(128)}, f32[2048]{0:T(1024)S(1)}, f32[512]{0:T(512)S(1)}, f32[2048]{0:T(1024)S(1)}) all-reduce(f32[]{:T(128)S(6)} %mul_shard_map.3, f32[2048]{0:T(1024)S(1)} %get-tuple-element.408, f32[512]{0:T(512)S(1)} %get-tuple-element.410, f32[2048]{0:T(1024)S(1)} %copy-done.56), channel_id=1, replica_groups=mesh['ctx'=16,'fsdp'=2] {'ctx','fsdp'}, use_global_device_ids=true, to_apply=%region_18.19 | all-reduce | flops 4609 | bytes 36872 | tf_op jit(solution)/shard_map/psum | solution.py:284
  2185.9 168.6 %reduce-scatter.33.cloned.1.call-done = f32[88,2048]{1,0:T(8,128)} async-done(((f32[2816,2048]{1,0:T(8,128)}), f32[88,2048]{1,0:T(8,128)}) %reduce-scatter.33.cloned.1.call-update) | async-done | bytes 720912 | tf_op jit(solution)/shard_map/reduce_scatter | solution.py:433
  2354.5 254.2 %reduce-scatter.31.cloned.1.call-done = f32[64,2816]{1,0:T(8,128)} async-done(((f32[2048,2816]{1,0:T(8,128)}), f32[64,2816]{1,0:T(8,128)}) %reduce-scatter.31.cloned.1.call-update) | async-done | bytes 720912 | tf_op jit(solution)/shard_map/reduce_scatter | solution.py:432
  2608.7 254.3 %reduce-scatter.29.cloned.1.call-done = f32[64,2816]{1,0:T(8,128)} async-done(((f32[2048,2816]{1,0:T(8,128)}), f32[64,2816]{1,0:T(8,128)}) %reduce-scatter.29.cloned.1.call-update) | async-done | bytes 720912 | tf_op jit(solution)/shard_map/reduce_scatter | solution.py:431
  2863.0 190.8 %reduce-scatter.27.cloned.1.call-done = f32[64,2048]{1,0:T(8,128)} async-done(((f32[2048,2048]{1,0:T(8,128)}), f32[64,2048]{1,0:T(8,128)}) %reduce-scatter.27.cloned.1.call-update) | async-done | bytes 524304 | tf_op jit(solution)/shard_map/reduce_scatter | solution.py:429
  3053.8 254.1 %reduce-scatter.21.cloned.1.call-done = f32[64,3072]{1,0:T(8,128)} async-done(((f32[2048,3072]{1,0:T(8,128)}), f32[64,3072]{1,0:T(8,128)}) %reduce-scatter.21.cloned.1.call-update) | async-done | bytes 786448 | tf_op jit(solution)/shard_map/reduce_scatter | solution.py:425
  3307.9 145.5 %reduce-scatter.23.cloned.1.call-done = f32[64,576]{1,0:T(8,128)} async-done(((f32[2048,576]{1,0:T(8,128)}), f32[64,576]{1,0:T(8,128)}) %reduce-scatter.23.cloned.1.call-update) | async-done | bytes 147472 | tf_op jit(solution)/shard_map/reduce_scatter | solution.py:426
  3453.4 147.8 %reduce-scatter.25.cloned.1.call-done = f32[16,4096]{1,0:T(8,128)} async-done(((f32[512,4096]{1,0:T(8,128)}), f32[16,4096]{1,0:T(8,128)}) %reduce-scatter.25.cloned.1.call-update) | async-done | bytes 262160 | tf_op jit(solution)/shard_map/reduce_scatter | solution.py:428
  (526 shorter events, 514.7 us)
Async XLA Ops:
  7.2 64.4 %all-gather.12.cloned.1.call-start = ((), (), s32[]{:S(2)}) async-start(), calls=%async_computation.16 | async-start | bytes 2703360 | tf_op jit(solution)/shard_map/all_gather | solution.py:149
  7.9 127.5 %all-gather.14.cloned.1.call-start = ((), (), s32[]{:S(2)}) async-start(), calls=%async_computation.17 | async-start | bytes 4325376 | tf_op jit(solution)/shard_map/all_gather | solution.py:151
  8.7 226.8 %all-gather.18.cloned.1.call-start = ((), (), s32[]{:S(2)}) async-start(), calls=%async_computation.19 | async-start | bytes 12976128 | tf_op jit(solution)/shard_map/all_gather | solution.py:148
  9.4 419.1 %all-gather.16.cloned.1.call-start = ((), (), s32[]{:S(2)}) async-start(), calls=%async_computation.18 | async-start | bytes 17825792 | tf_op jit(solution)/shard_map/all_gather | solution.py:222
  54.3 85.1 %copy-start.49 = (f32[512]{0:T(512)}, f32[512]{0:T(512)S(1)}, u32[]{:S(2)}) copy-start(f32[512]{0:T(512)S(1)} %convert_element_type.196) | copy-start | bytes 6148
  54.3 197.9 %copy-start.40 = (f32[2048]{0:T(1024)}, f32[2048]{0:T(1024)S(1)}, u32[]{:S(2)}) copy-start(f32[2048]{0:T(1024)S(1)} %convert_element_type.194) | copy-start | bytes 24580
  55.5 196.7 %copy-start.57 = (f32[128]{0:T(128)}, f32[128]{0:T(128)S(1)}, u32[]{:S(2)}) copy-start(f32[128]{0:T(128)S(1)} %add_rsqrt_fusion.2) | copy-start | bytes 1540
  74.6 76.0 %copy-start.23 = (f32[128,576]{0,1:T(8,128)}, f32[128,576]{0,1:T(8,128)S(1)}, u32[]{:S(2)}) copy-start(f32[128,576]{0,1:T(8,128)S(1)} %fusion.100) | copy-start | bytes 884740
  74.7 65.9 %copy-start.61 = (f32[128]{0:T(128)}, f32[128]{0:T(128)S(1)}, u32[]{:S(2)}) copy-start(f32[128]{0:T(128)S(1)} %add_rsqrt_fusion.1) | copy-start | bytes 1540
  139.4 367.5 %all-gather.20.cloned.1.call-start = ((), (), s32[]{:S(2)}) async-start(), calls=%async_computation.20 | async-start | bytes 8650752 | tf_op jit(solution)/shard_map/all_gather | solution.py:152
  140.0 388.9 %all-gather.28.cloned.1.call-start = ((), (), s32[]{:S(2)}) async-start(), calls=%async_computation.24 | async-start | bytes 8650752 | tf_op jit(solution)/shard_map/all_gather | solution.py:254
  140.6 498.8 %all-gather.30.cloned.1.call-start = ((), (), s32[]{:S(2)}) async-start(), calls=%async_computation.25 | async-start | bytes 8650752 | tf_op jit(solution)/shard_map/all_gather | solution.py:255
  141.4 512.6 %all-gather.32.cloned.1.call-start = ((), (), s32[]{:S(2)}) async-start(), calls=%async_computation.26 | async-start | bytes 8650752 | tf_op jit(solution)/shard_map/all_gather | solution.py:256
  142.1 576.2 %all-gather.22.cloned.1.call-start = ((), (), s32[]{:S(2)}) async-start(), calls=%async_computation.21 | async-start | bytes 11894784 | tf_op jit(solution)/shard_map/all_gather | solution.py:154
  142.9 714.1 %all-gather.24.cloned.1.call-start = ((), (), s32[]{:S(2)}) async-start(), calls=%async_computation.22 | async-start | bytes 11894784 | tf_op jit(solution)/shard_map/all_gather | solution.py:155
  143.9 367.8 %copy-start.47 = (f32[2048]{0:T(1024)}, f32[2048]{0:T(1024)S(1)}, u32[]{:S(2)}) copy-start(f32[2048]{0:T(1024)S(1)} %convert_element_type.206) | copy-start | bytes 24580
  150.8 108.2 %copy-start.45 = (f32[128,32]{0,1:T(8,128)}, f32[128,32]{0,1:T(8,128)S(1)}, u32[]{:S(2)}) copy-start(f32[128,32]{0,1:T(8,128)S(1)} %get-tuple-element.494) | copy-start | bytes 49156
  511.7 440.8 %copy-start.11 = (f32[128,2048]{1,0:T(8,128)}, f32[128,2048]{1,0:T(8,128)S(1)}, u32[]{:S(2)}) copy-start(f32[128,2048]{1,0:T(8,128)S(1)} %get-tuple-element.496) | copy-start | bytes 3145732
  511.9 345.1 %copy-start = (bf16[128,2048]{1,0:T(8,128)(2,1)}, bf16[128,2048]{1,0:T(8,128)(2,1)S(1)}, u32[]{:S(2)}) copy-start(bf16[128,2048]{1,0:T(8,128)(2,1)S(1)} %multiply_convert_fusion.7) | copy-start | bytes 1572868
  523.6 103.0 %all-to-all-start = ((bf16[16,72,2048]{2,1,0:T(8,128)(2,1)}), bf16[16,72,2048]{2,1,0:T(8,128)(2,1)}, u32[]{:S(2)}, u32[]{:S(2)}) async-start(bf16[16,72,2048]{2,1,0:T(8,128)(2,1)} %broadcast_select_fusion.1), calls=%async_computation | async-start | bytes 9437184 | tf_op jit(solution)/shard_map/all_to_all | solution.py:261
  528.1 424.3 %all-gather.26.cloned.1.call-start = ((), (), s32[]{:S(2)}) async-start(), calls=%async_computation.23 | async-start | bytes 11894784 | tf_op jit(solution)/shard_map/all_gather | solution.py:156
  666.8 50.5 %copy-start.55 = (f32[1,128,6]{1,0,2:T(1,128)S(1)}, f32[1,128,6]{1,0,2:T(1,128)}, u32[]{:S(2)}) copy-start(f32[1,128,6]{1,0,2:T(1,128)} %param.26) | copy-start | bytes 9220
  666.8 198.0 %all-to-all-start.1 = ((bf16[16,72,2048]{2,1,0:T(8,128)(2,1)}), bf16[16,72,2048]{2,1,0:T(8,128)(2,1)}, u32[]{:S(2)}, u32[]{:S(2)}) async-start(bf16[16,72,2048]{2,1,0:T(8,128)(2,1)} %bitcast.316), calls=%async_computation.1 | async-start | bytes 9437184 | tf_op jit(solution)/shard_map/all_to_all | solution.py:275
  864.8 87.7 %copy-start.29 = (bf16[128,2816]{1,0:T(8,128)(2,1)}, bf16[128,2816]{1,0:T(8,128)(2,1)S(1)}, u32[]{:S(2)}) copy-start(bf16[128,2816]{1,0:T(8,128)(2,1)S(1)} %get-tuple-element.499) | copy-start | bytes 2162692
  882.1 70.4 %copy-start.44 = (bf16[1,128,2048]{2,1,0:T(8,128)(2,1)S(1)}, bf16[1,128,2048]{2,1,0:T(8,128)(2,1)}, u32[]{:S(2)}) copy-start(bf16[1,128,2048]{2,1,0:T(8,128)(2,1)} %param.23) | copy-start | bytes 1572868
  985.5 126.0 %slice-start.5 = ((s8[5767168]{0:T(1024)(128)(4,1)}), s8[4194304]{0:T(1024)(128)(4,1)S(1)}, s32[]{:S(2)}) async-start(s8[5767168]{0:T(1024)(128)(4,1)} %bitcast.324), calls=%async_computation.44 | async-start | bytes 8388608
  1132.9 92.1 %all-to-all-start.3 = ((bf16[16,72,2048]{2,1,0:T(8,128)(2,1)}), bf16[16,72,2048]{2,1,0:T(8,128)(2,1)}, u32[]{:S(2)}, u32[]{:S(2)}) async-start(bf16[16,72,2048]{2,1,0:T(8,128)(2,1)} %bitcast.317), calls=%async_computation.3 | async-start | bytes 9437184 | tf_op jit(solution)/shard_map/all_to_all | solution.py:307
  1137.7 673.0 %reduce-scatter.39.cloned.1.call-start = ((), (), s32[]{:S(2)}) async-start(), calls=%async_computation.36 | async-start | bytes 557056
  1324.6 40.0 %copy-start.53 = (s32[128]{0:T(128)S(1)}, s32[128]{0:T(128)}, u32[]{:S(2)}) copy-start(s32[128]{0:T(128)} %get-tuple-element.864) | copy-start | bytes 1540 | tf_op jit(solution)/shard_map/while
  1324.6 40.0 %copy-start.71 = (s32[4]{0:T(128)S(1)}, s32[4]{0:T(128)}, u32[]{:S(2)}) copy-start(s32[4]{0:T(128)} %get-tuple-element.896) | copy-start | bytes 52 | tf_op jit(solution)/shard_map/while
  1405.6 40.0 %copy-start.53 = (s32[128]{0:T(128)S(1)}, s32[128]{0:T(128)}, u32[]{:S(2)}) copy-start(s32[128]{0:T(128)} %get-tuple-element.864) | copy-start | bytes 1540 | tf_op jit(solution)/shard_map/while
  1405.6 40.0 %copy-start.71 = (s32[4]{0:T(128)S(1)}, s32[4]{0:T(128)}, u32[]{:S(2)}) copy-start(s32[4]{0:T(128)} %get-tuple-element.896) | copy-start | bytes 52 | tf_op jit(solution)/shard_map/while
  1486.6 40.0 %copy-start.53 = (s32[128]{0:T(128)S(1)}, s32[128]{0:T(128)}, u32[]{:S(2)}) copy-start(s32[128]{0:T(128)} %get-tuple-element.864) | copy-start | bytes 1540 | tf_op jit(solution)/shard_map/while
  1486.6 40.0 %copy-start.71 = (s32[4]{0:T(128)S(1)}, s32[4]{0:T(128)}, u32[]{:S(2)}) copy-start(s32[4]{0:T(128)} %get-tuple-element.896) | copy-start | bytes 52 | tf_op jit(solution)/shard_map/while
  1608.1 437.4 %reduce-scatter.37.cloned.1.call-start = ((), (), s32[]{:S(2)}) async-start(), calls=%async_computation.35 | async-start | bytes 17825792
  1646.9 424.4 %reduce-scatter.41.cloned.1.call-start = ((), (), s32[]{:S(2)}) async-start(), calls=%async_computation.37 | async-start | bytes 8650752
  1699.8 399.3 %reduce-scatter.43.cloned.1.call-start = ((), (), s32[]{:S(2)}) async-start(), calls=%async_computation.38 | async-start | bytes 8650752
  1752.9 373.7 %reduce-scatter.35.cloned.1.call-start = ((), (), s32[]{:S(2)}) async-start(), calls=%async_computation.34 | async-start | bytes 8650752 | tf_op jit(solution)/shard_map/reduce_scatter | solution.py:323
  1766.1 588.4 %reduce-scatter.33.cloned.1.call-start = ((), (), s32[]{:S(2)}) async-start(), calls=%async_computation.33 | async-start | bytes 23789568 | tf_op jit(solution)/shard_map/reduce_scatter | solution.py:433
  1776.9 831.8 %reduce-scatter.31.cloned.1.call-start = ((), (), s32[]{:S(2)}) async-start(), calls=%async_computation.32 | async-start | bytes 23789568 | tf_op jit(solution)/shard_map/reduce_scatter | solution.py:432
  1787.8 1075.2 %reduce-scatter.29.cloned.1.call-start = ((), (), s32[]{:S(2)}) async-start(), calls=%async_computation.31 | async-start | bytes 23789568 | tf_op jit(solution)/shard_map/reduce_scatter | solution.py:431
  1798.4 1255.5 %reduce-scatter.27.cloned.1.call-start = ((), (), s32[]{:S(2)}) async-start(), calls=%async_computation.30 | async-start | bytes 17301504 | tf_op jit(solution)/shard_map/reduce_scatter | solution.py:429
  1808.0 1499.9 %reduce-scatter.21.cloned.1.call-start = ((), (), s32[]{:S(2)}) async-start(), calls=%async_computation.27 | async-start | bytes 25952256 | tf_op jit(solution)/shard_map/reduce_scatter | solution.py:425
  1823.3 222.1 %copy-start.24 = (f32[128,576]{0,1:T(8,128)S(1)}, f32[128,576]{0,1:T(8,128)}, u32[]{:S(2)}) copy-start(f32[128,576]{0,1:T(8,128)} %copy-done.23) | copy-start | bytes 884740
  1823.4 222.1 %copy-start.50 = (f32[512]{0:T(512)S(1)}, f32[512]{0:T(512)}, u32[]{:S(2)}) copy-start(f32[512]{0:T(512)} %copy-done.49) | copy-start | bytes 6148
  1823.4 222.1 %copy-start.62 = (f32[128]{0:T(128)S(1)}, f32[128]{0:T(128)}, u32[]{:S(2)}) copy-start(f32[128]{0:T(128)} %copy-done.61) | copy-start | bytes 1540
  1823.4 1630.0 %reduce-scatter.23.cloned.1.call-start = ((), (), s32[]{:S(2)}) async-start(), calls=%async_computation.28 | async-start | bytes 5406720 | tf_op jit(solution)/shard_map/reduce_scatter | solution.py:426
  2052.8 1548.4 %reduce-scatter.25.cloned.1.call-start = ((), (), s32[]{:S(2)}) async-start(), calls=%async_computation.29 | async-start | bytes 8650752 | tf_op jit(solution)/shard_map/reduce_scatter | solution.py:428
  (82 other events, 493.9 us)
Sparse Core Ops, SparseCore 0:
  10.8 60.6 all-gather.11
  74.4 60.9 all-gather.13
  138.3 97.1 all-gather.17
  238.6 189.8 all-gather.15
  431.2 75.6 all-gather.19
  508.3 14.6 all-gather.27
  524.5 17.1 all-gather.29
  543.2 17.1 all-gather.31
  563.3 130.1 all-gather.21
  696.2 160.7 all-gather.23
  859.9 92.5 all-gather.25
  1608.2 92.0 reduce-scatter.38
  1702.7 342.7 reduce-scatter.36
  2048.3 19.3 reduce-scatter.40
  2070.5 15.0 reduce-scatter.42
  2087.8 15.0 reduce-scatter.34
  2105.6 248.8 reduce-scatter.32
  2357.2 251.4 reduce-scatter.30
  2611.6 251.4 reduce-scatter.28
  2865.7 188.0 reduce-scatter.26
  3060.8 247.0 reduce-scatter.20
  3310.8 142.5 reduce-scatter.22
  3456.4 144.7 reduce-scatter.24
where the time goes:
time: 3630 us; the launch traced here: 3610 us
  waiting for transfers between devices  2310 us (64%)
  local copies, waits for them, and re-layouts  503 us (14%)
  matrix products  311 us (9%)
  blocking collectives  240 us (7%)
  other arithmetic  157 us (4%)
  starting transfers between devices  61.7 us (2%)
    reduce_scatter x1, waiting for transfers between devices, shards(): lax.psum_scatter(grad_w_gate, ('ctx', 'fsdp'), scatter_dimension=0, tiled...  254 us
    reduce_scatter x1, waiting for transfers between devices, shards(): lax.psum_scatter(grad_w_up, ('ctx', 'fsdp'), scatter_dimension=0, tiled=T...  254 us
    reduce_scatter x1, waiting for transfers between devices, shards(): lax.psum_scatter(grad_w_query, ('ctx', 'fsdp'), scatter_dimension=0, tile...  254 us
    unnamed x27, waiting for transfers between devices  228 us
    unnamed x179, local copies, waits for them, and re-layouts  200 us
    reduce_scatter x1, waiting for transfers between devices, shards(): lax.psum_scatter(grad_w_output, ('ctx', 'fsdp'), scatter_dimension=0, til...  191 us
    all_gather x1, waiting for transfers between devices, shards(): lax.all_gather(payload[0], 'ctx', axis=0, tiled=True)  169 us
    reduce_scatter x1, waiting for transfers between devices, shards(): lax.psum_scatter(grad_w_down, ('ctx', 'fsdp'), scatter_dimension=0, tiled...  169 us
  transfers between devices with their start and end apart: 26, of which 17 were waited for; matrix products, arithmetic and copies ran while one was open for 14% of the time, Pallas kernels for 0%

commit v1 on v0

v1 whole, which is shorter than its diff:
```python
import functools
import math

import jax
import jax.numpy as jnp
from jax import lax
from jax.experimental import pallas as pl
from jax.experimental.pallas import tpu as pltpu
from jax.sharding import PartitionSpec as P

D = 2048
H = 16
DN = 128
DR = 64
DV = 128
KVR = 512
TOPK = 6

EPS = 1e-06
NEG = -1e30
MESH = pl.DeviceIdType.MESH
f32 = jnp.float32
bf16 = jnp.bfloat16


def norm_forward(rows, gain):
    factor = lax.rsqrt(jnp.mean(rows * rows, axis=-1, keepdims=True) + EPS)
    return (rows * factor * gain, factor)


def norm_back_rows(rows, factor, gain, grad_out):
    scaled = grad_out * gain
    normed = rows * factor
    return factor * (scaled - normed * jnp.mean(scaled * normed, axis=-1, keepdims=True))


def rotate(values, cosine, sine):
    half = values.shape[-1] // 2
    first = values[..., :half]
    second = values[..., half:]
    return jnp.concatenate(
        [first * cosine - second * sine, second * cosine + first * sine], axis=-1
    )


def rope_tables(offsets):
    freqs = 10000.0 ** (-(jnp.arange(DR // 2, dtype=f32) * 2.0) / DR)
    angle = offsets.astype(f32)[:, None] * freqs[None, :]
    return (jnp.cos(angle), jnp.sin(angle))


def silu_grads(gate_val, up_val, grad_hidden):
    sigma = jax.nn.sigmoid(gate_val)
    grad_gate = grad_hidden * up_val * sigma * (1.0 + gate_val * (1.0 - sigma))
    grad_up = grad_hidden * gate_val * sigma
    return (grad_gate.astype(bf16), grad_up.astype(bf16))


def dot(left, right):
    return jnp.dot(left, right, preferred_element_type=f32)


def dot_first(left, right):
    return lax.dot_general(left, right, (((0,), (0,)), ((), ())), preferred_element_type=f32)


def dot_last(left, right):
    return lax.dot_general(left, right, (((1,), (1,)), ((), ())), preferred_element_type=f32)


def flip(me, mask):
    out = me
    bit = 1
    while bit <= mask:
        if mask & bit:
            out = out + bit * (1 - 2 * ((me // bit) % 2))
        bit *= 2
    return out


def row_parts(rows, bits):
    low, high = [1, 2], [1 << k for k in range(bits - 1, 1, -1)]
    orders = (high + low, high + low[::-1], low + high)
    unit = rows // 8
    if unit % 16 and rows % 16 == 0:
        units = rows // 16
        first = -(-3 * units // 8)
        counts = [first * 16, min(first, units - first) * 16]
        counts.append(rows - sum(counts))
    else:
        counts = [3 * unit, 3 * unit, 2 * unit]
    parts, start = [], 0
    for count, order in zip(counts, orders):
        if count:
            parts.append((start, count, tuple(order)))
            start += count
    return tuple(parts)


def greet(bits):
    me = lax.axis_index("ctx")
    barrier = pltpu.get_barrier_semaphore()
    for k in range(bits):
        pl.semaphore_signal(
            barrier, inc=1, device_id={"ctx": flip(me, 1 << k)}, device_id_type=MESH
        )
    pl.semaphore_wait(barrier, bits)


def gather_events(parts, bits):
    events = []
    for p, (_, _, order) in enumerate(parts):
        for slot in range(1 << bits):
            hops = [k for k, b in enumerate(order) if slot & b]
            for k in range(hops[-1] + 1 if hops else 0, bits):
                events.append((len(hops), k, p, slot, order[k]))
    return tuple(sorted(events))


def gather_kernel(parts, bits, events, x_ref, o_ref, send_sem, recv_sem, own_sem):
    me = lax.axis_index("ctx")
    own = pltpu.make_async_copy(x_ref, o_ref.at[me], own_sem)
    own.start()
    greet(bits)

    def copy(p, slot, bit, index):
        start, count, _ = parts[p]
        rows = pl.ds(start, count)
        block = flip(me, slot)
        return pltpu.make_async_remote_copy(
            src_ref=x_ref.at[rows] if slot == 0 else o_ref.at[block, rows],
            dst_ref=o_ref.at[block, rows],
            send_sem=send_sem.at[index],
            recv_sem=recv_sem.at[p, slot ^ bit],
            device_id={"ctx": flip(me, bit)},
            device_id_type=MESH,
        )

    def arrived(p, slot):
        start, count, order = parts[p]
        rows = pl.ds(start, count)
        bit = [b for b in order if slot & b][-1]
        pltpu.make_async_remote_copy(
            src_ref=x_ref.at[rows],
            dst_ref=o_ref.at[flip(me, slot), rows],
            send_sem=send_sem.at[0],
            recv_sem=recv_sem.at[p, slot],
            device_id={"ctx": flip(me, bit)},
            device_id_type=MESH,
        ).wait_recv()

    seen = set()
    started = []
    for index, (_, _, p, slot, bit) in enumerate(events):
        if slot and (p, slot) not in seen:
            arrived(p, slot)
            seen.add((p, slot))
        sent = copy(p, slot, bit, index)
        sent.start()
        started.append(sent)
    for p in range(len(parts)):
        for slot in range(1, 1 << bits):
            if (p, slot) not in seen:
                arrived(p, slot)
    for sent in started:
        sent.wait_send()
    own.wait()


def gather_ctx(x, bits):
    rows, cols = x.shape
    parts = row_parts(rows, bits)
    events = gather_events(parts, bits)
    return pl.pallas_call(
        functools.partial(gather_kernel, parts, bits, events),
        name="gather_ctx",
        out_shape=jax.ShapeDtypeStruct((1 << bits, rows, cols), x.dtype),
        in_specs=[pl.BlockSpec(memory_space=pl.ANY)],
        out_specs=pl.BlockSpec(memory_space=pl.ANY),
        scratch_shapes=[
            pltpu.SemaphoreType.DMA((len(events),)),
            pltpu.SemaphoreType.DMA((len(parts), 1 << bits)),
            pltpu.SemaphoreType.DMA,
        ],
        compiler_params=pltpu.CompilerParams(collective_id=1, has_side_effects=True),
    )(x)


def scatter_kernel(parts, bits, x_ref, o_ref, recv, send, send_sem, recv_sem):
    me = lax.axis_index("ctx")
    greet(bits)

    def copy(p, slot, k, src):
        start, count, order = parts[p]
        return pltpu.make_async_remote_copy(
            src_ref=src,
            dst_ref=recv.at[slot - 1, pl.ds(start, count)],
            send_sem=send_sem.at[p, slot - 1],
            recv_sem=recv_sem.at[p, slot - 1],
            device_id={"ctx": flip(me, order[k])},
            device_id_type=MESH,
        )

    started = []
    for k in range(bits + 1):
        for j in range(1 << max(bits - 1 - k, 0)):
            for p, (start, count, order) in enumerate(parts):
                rows = pl.ds(start, count)
                slot = order[k] if k < bits else 0
                for q, b in enumerate(order[k + 1 :]):
                    if (j >> q) & 1:
                        slot |= b
                block = flip(me, slot)
                if k == 0:
                    sent = copy(p, slot, 0, x_ref.at[block, rows])
                    sent.start()
                    started.append(sent)
                    continue
                for e in range(k):
                    other = slot | order[e]
                    copy(p, other, e, recv.at[other - 1, rows]).wait_recv()
                target = send.at[slot - 1] if k < bits else o_ref

                @pl.loop(0, count // 16)
                def _(t, k=k, slot=slot, block=block, start=start, order=order, target=target):
                    part = pl.ds(pl.multiple_of(start + t * 16, 16), 16)
                    total = x_ref[block, part].astype(f32)
                    for e in range(k):
                        total = total + recv[(slot | order[e]) - 1, part].astype(f32)
                    target[part] = total.astype(target.dtype)

                if k < bits:
                    sent = copy(p, slot, k, send.at[slot - 1, rows])
                    sent.start()
                    started.append(sent)
    for sent in started:
        sent.wait_send()


def scatter_ctx(x, bits):
    _, rows, cols = x.shape
    parts = tuple((start, count, order[::-1]) for start, count, order in row_parts(rows, bits))
    others = (1 << bits) - 1
    return pl.pallas_call(
        functools.partial(scatter_kernel, parts, bits),
        name="scatter_ctx",
        out_shape=jax.ShapeDtypeStruct((rows, cols), f32),
        in_specs=[pl.BlockSpec(memory_space=pltpu.VMEM)],
        out_specs=pl.BlockSpec(memory_space=pltpu.VMEM),
        scratch_shapes=[
            pltpu.VMEM((others, rows, cols), bf16),
            pltpu.VMEM((others, rows, cols), bf16),
            pltpu.SemaphoreType.DMA((len(parts), others)),
            pltpu.SemaphoreType.DMA((len(parts), others)),
        ],
        compiler_params=pltpu.CompilerParams(
            collective_id=2, has_side_effects=True, vmem_limit_bytes=56 << 20
        ),
    )(x)


def attend_kernel(block, count, q_ref, k_ref, v_ref, first_ref, o_ref, log_ref):
    step = pl.program_id(0)
    for i in range(count):

        @pl.when(step == i)
        def _(i=i):
            extent = (i + 1) * block
            scores = dot_last(q_ref[...], k_ref[:extent, :])
            key_pos = lax.broadcasted_iota(jnp.int32, (block, extent), 1)
            query_pos = i * block + lax.broadcasted_iota(jnp.int32, (block, extent), 0)
            allowed = (key_pos >= first_ref[...]) & (key_pos <= query_pos)
            scores = jnp.where(allowed, scores, NEG)
            top = jnp.max(scores, axis=-1, keepdims=True)
            weights = jnp.exp(scores - top)
            total = jnp.sum(weights, axis=-1, keepdims=True)
            summed = dot(weights.astype(bf16), v_ref[:extent, :])
            o_ref[...] = summed / total
            log_ref[...] = top + jnp.log(total)


def attend(queries, keys, values, first):
    length = queries.shape[0]
    block = min(256, length)
    count = length // block
    return pl.pallas_call(
        functools.partial(attend_kernel, block, count),
        name="attend",
        grid=(count,),
        out_shape=(
            jax.ShapeDtypeStruct((length, DV), f32),
            jax.ShapeDtypeStruct((length, 1), f32),
        ),
        in_specs=[
            pl.BlockSpec((block, DN + DR), lambda i: (i, 0)),
            pl.BlockSpec((length, DN + DR), lambda i: (0, 0)),
            pl.BlockSpec((length, DV), lambda i: (0, 0)),
            pl.BlockSpec((block, 1), lambda i: (i, 0)),
        ],
        out_specs=(
            pl.BlockSpec((block, DV), lambda i: (i, 0)),
            pl.BlockSpec((block, 1), lambda i: (i, 0)),
        ),
        compiler_params=pltpu.CompilerParams(vmem_limit_bytes=56 << 20),
        cost_estimate=pl.CostEstimate(
            flops=length * length * (DN + DR + DV),
            bytes_accessed=length * 2000,
            transcendentals=length * length // 2,
        ),
    )(queries, keys, values, first)


def attend_back_kernel(
    block, count, q_ref, k_ref, v_ref, g_ref, first_ref, log_ref, delta_ref, dq_ref, dk_ref, dv_ref
):
    step = pl.program_id(0)

    @pl.when(step == 0)
    def _():
        dk_ref[...] = jnp.zeros_like(dk_ref)
        dv_ref[...] = jnp.zeros_like(dv_ref)

    for i in range(count):

        @pl.when(step == i)
        def _(i=i):
            extent = (i + 1) * block
            keys = k_ref[:extent, :]
            scores = dot_last(keys, q_ref[...])
            key_pos = lax.broadcasted_iota(jnp.int32, (extent, block), 0)
            query_pos = i * block + lax.broadcasted_iota(jnp.int32, (extent, block), 1)
            allowed = (key_pos >= first_ref[...]) & (key_pos <= query_pos)
            weights = jnp.where(allowed, jnp.exp(scores - log_ref[...]), 0.0)
            grad_weights = dot_last(v_ref[:extent, :], g_ref[...])
            grad_scores = (weights * (grad_weights - delta_ref[...])).astype(bf16)
            dv_ref[:extent, :] += dot(weights.astype(bf16), g_ref[...])
            dk_ref[:extent, :] += dot(grad_scores, q_ref[...])
            dq_ref[...] = dot_first(grad_scores, keys)


def attend_back(queries, keys, values, grad, first, log_total, delta):
    length = queries.shape[0]
    block = min(256, length)
    count = length // block
    row = lambda: pl.BlockSpec((1, block), lambda i: (0, i))
    whole = lambda width: pl.BlockSpec((length, width), lambda i: (0, 0))
    part = lambda width: pl.BlockSpec((block, width), lambda i: (i, 0))
    return pl.pallas_call(
        functools.partial(attend_back_kernel, block, count),
        name="attend_back",
        grid=(count,),
        out_shape=(
            jax.ShapeDtypeStruct((length, DN + DR), f32),
            jax.ShapeDtypeStruct((length, DN + DR), f32),
            jax.ShapeDtypeStruct((length, DV), f32),
        ),
        in_specs=[
            part(DN + DR),
            whole(DN + DR),
            whole(DV),
            part(DV),
            row(),
            row(),
            row(),
        ],
        out_specs=(part(DN + DR), whole(DN + DR), whole(DV)),
        compiler_params=pltpu.CompilerParams(vmem_limit_bytes=56 << 20),
        cost_estimate=pl.CostEstimate(
            flops=length * length * (3 * (DN + DR) + 2 * DV),
            bytes_accessed=length * 4000,
            transcendentals=length * length // 2,
        ),
    )(queries, keys, values, grad, first, log_total, delta)


def shift_fsdp(x, groups, by):
    return lax.ppermute(x, "fsdp", [(i, (i + by) % groups) for i in range(groups)])


def gather_fsdp(x, groups):
    if groups != 2:
        return lax.all_gather(x, "fsdp", axis=0)
    other = shift_fsdp(x, groups, 1)
    mine_first = lax.axis_index("fsdp") == 0
    return jnp.stack([jnp.where(mine_first, x, other), jnp.where(mine_first, other, x)])


def scatter_fsdp(x, groups):
    if groups != 2:
        return lax.psum_scatter(x.astype(bf16), "fsdp", scatter_dimension=0).astype(f32)
    me = lax.axis_index("fsdp")
    away = lax.dynamic_index_in_dim(x, 1 - me, 0, keepdims=False).astype(bf16)
    mine = lax.dynamic_index_in_dim(x, me, 0, keepdims=False).astype(f32)
    return mine + shift_fsdp(away, groups, 1).astype(f32)


def shards(
    hidden_in,
    teacher,
    doc_starts,
    routes,
    gate_logits,
    input_gain,
    query_weight,
    latent_weight,
    latent_gain,
    expand_weight,
    output_weight,
    mixer_gain,
    shared_gate,
    shared_up,
    shared_down,
    expert_gate,
    expert_up,
    expert_down,
):
    cycle = lax.axis_size("ctx")
    groups = lax.axis_size("fsdp")
    bits = cycle.bit_length() - 1
    tokens = hidden_in.shape[1]
    length = tokens * cycle
    everyone = ("ctx", "fsdp")
    capacity = min(tokens, 3 * tokens * TOPK // (2 * cycle))
    scale = (DN + DR) ** (-0.5)
    copies = max(1, cycle // H)
    ctx_index = lax.axis_index("ctx")
    copy_index = ctx_index % copies
    slab = query_weight.shape[0]
    slab_latent = expand_weight.shape[0]

    def columns(weight):
        rows, width = weight.shape
        pieces = jnp.transpose(weight.reshape(rows, cycle, width // cycle), (1, 0, 2))
        pieces = lax.all_to_all(pieces, "ctx", split_axis=0, concat_axis=0, tiled=True)
        pieces = jnp.transpose(gather_fsdp(pieces, groups), (1, 0, 2, 3))
        return pieces.reshape(cycle * groups * rows, width // cycle)

    def rows_back(grads):
        rows, width = grads.shape
        slab_rows = rows // (cycle * groups)
        pieces = jnp.transpose(grads.reshape(cycle, groups, slab_rows, width), (1, 0, 2, 3))
        pieces = scatter_fsdp(pieces, groups).astype(bf16)
        pieces = lax.all_to_all(pieces, "ctx", split_axis=0, concat_axis=0, tiled=True)
        return jnp.transpose(pieces, (1, 0, 2)).reshape(slab_rows, cycle * width).astype(f32)

    def same_head(part):
        if copies == 1:
            return part
        teams = [[i * copies + j for j in range(copies)] for i in range(H)]
        return lax.all_gather(part, "ctx", axis=1, tiled=True, axis_index_groups=teams)

    def own_part(full):
        if copies == 1:
            return full
        width = full.shape[1] // copies
        return lax.dynamic_slice_in_dim(full, copy_index * width, width, 1)

    spare = jnp.zeros((slab - slab_latent,), bf16)
    narrow = jnp.concatenate(
        [
            latent_weight,
            input_gain[:, None],
            mixer_gain[:, None],
            jnp.concatenate([latent_gain, spare])[:, None],
        ],
        axis=1,
    )
    narrow = lax.all_gather(narrow, everyone, axis=0, tiled=True)
    w_latent = narrow[:, : KVR + DR]
    gain_one = narrow[:, KVR + DR].astype(f32)
    gain_two = narrow[:, KVR + DR + 1].astype(f32)
    gain_latent = narrow[:, KVR + DR + 2].reshape(-1, slab)[:, :slab_latent].reshape(-1).astype(f32)
    w_query = same_head(columns(query_weight))
    w_expand = same_head(columns(expand_weight))
    probs = jax.nn.softmax(gate_logits[0], axis=-1)
    chosen = routes[0][:, :, None] == jnp.arange(cycle, dtype=jnp.int32)[None, None, :]
    dense_probs = jnp.sum(jnp.where(chosen, probs[:, :, None], 0.0), axis=1)
    all_probs = lax.all_gather(dense_probs, "ctx", axis=0, tiled=True)
    w_output = lax.all_gather(output_weight, everyone, axis=0, tiled=True)

    starts = doc_starts[0]
    positions = jnp.arange(length, dtype=jnp.int32)
    inside = starts[None, :] <= positions[:, None]
    first_pos = jnp.max(jnp.where(inside, starts[None, :], 0), axis=1)
    cosine, sine = rope_tables(positions - first_pos)
    residual = hidden_in[0].astype(f32)
    all_hidden = gather_ctx(hidden_in[0], bits).reshape(length, D).astype(f32)
    act_one, factor_all = norm_forward(all_hidden, gain_one)
    act_one = act_one.astype(bf16)
    query_raw = dot(act_one, w_query)
    queries = jnp.concatenate(
        [query_raw[:, :DN], rotate(query_raw[:, DN:], cosine, sine)], axis=-1
    )
    queries = (queries * scale).astype(bf16)
    latent_raw = dot(act_one, w_latent)
    latent, factor_latent = norm_forward(latent_raw[:, :KVR], gain_latent)
    latent = latent.astype(bf16)
    key_rope = rotate(latent_raw[:, KVR:], cosine, sine).astype(bf16)
    expanded = dot(latent, w_expand).astype(bf16)
    keys = jnp.concatenate([expanded[:, :DN], key_rope], axis=-1)
    values = expanded[:, DN:]
    attended, log_total = attend(queries, keys, values, first_pos[:, None])
    attended_low = attended.astype(bf16)
    attended_mine = lax.all_to_all(
        own_part(attended_low).reshape(cycle, tokens, DV // copies),
        "ctx",
        split_axis=0,
        concat_axis=0,
        tiled=True,
    )
    attended_mine = jnp.transpose(attended_mine, (1, 0, 2)).reshape(tokens, H * DV)
    mixed = residual + dot(attended_mine, w_output)

    normed_two, factor_two = norm_forward(mixed, gain_two)
    act_two = normed_two.astype(bf16)
    all_act = gather_ctx(act_two, bits)
    my_probs = lax.dynamic_index_in_dim(all_probs, ctx_index, 1, keepdims=False)
    my_probs = my_probs.reshape(cycle, tokens)
    used = my_probs > 0.0
    place = jnp.cumsum(used.astype(jnp.int32), axis=1) - 1
    slots = jnp.arange(capacity, dtype=jnp.int32)
    select = (place[:, None, :] == slots[None, :, None]) & used[:, None, :]
    slot_probs = jnp.sum(jnp.where(select, my_probs[:, None, :], 0.0), axis=-1).reshape(-1, 1)
    select = select.astype(bf16)

    def pick(blocks):
        return jnp.einsum("bst,btd->bsd", select, blocks, preferred_element_type=f32).reshape(
            cycle * capacity, D
        )

    def place_back(rows):
        return jnp.einsum(
            "bst,bsd->btd", select, rows.reshape(cycle, capacity, D), preferred_element_type=f32
        )

    w_gate = columns(shared_gate)
    w_up = columns(shared_up)
    w_down = gather_fsdp(shared_down, groups).reshape(-1, D)
    shares = [(expert_gate[0], expert_up[0], expert_down[0])]
    for r in range(1, groups):
        shares.append(tuple(shift_fsdp(item, groups, r) for item in shares[0]))
    flat_act = all_act.reshape(length, D)
    gate_s = dot(flat_act, w_gate)
    up_s = dot(flat_act, w_up)
    hidden_s = (jax.nn.silu(gate_s) * up_s).astype(bf16)
    rows = pick(all_act).astype(bf16)
    kept = []
    total = 0.0
    for part_gate, part_up, part_down in shares:
        gate_e = dot(rows, part_gate)
        up_e = dot(rows, part_up)
        hidden_e = (jax.nn.silu(gate_e) * up_e).astype(bf16)
        kept.append((gate_e, up_e, hidden_e))
        total = total + dot(hidden_e, part_down)
    outputs = (slot_probs * total).astype(bf16)
    partial = place_back(outputs) + dot(hidden_s, w_down).reshape(cycle, tokens, D)
    result = mixed + scatter_ctx(partial.astype(bf16), bits)
    diff = result - teacher[0].astype(f32)
    share = 0.5 * jnp.sum(diff * diff)
    loss_value = jnp.sum(lax.all_gather(share, everyone)) / (length * groups * D)

    all_diff = gather_ctx(diff.astype(bf16), bits)
    flat_diff = all_diff.reshape(length, D)
    grad_w_down = dot_first(hidden_s, flat_diff)
    grad_gate_s, grad_up_s = silu_grads(gate_s, up_s, dot_last(flat_diff, w_down))
    grad_rows = (slot_probs * pick(all_diff)).astype(bf16)
    row_grad = 0.0
    grad_shares = []
    for (part_gate, part_up, part_down), (gate_e, up_e, hidden_e) in zip(shares, kept):
        grad_gate_e, grad_up_e = silu_grads(gate_e, up_e, dot_last(grad_rows, part_down))
        row_grad = row_grad + dot_last(grad_gate_e, part_gate) + dot_last(grad_up_e, part_up)
        grad_shares.append((hidden_e, grad_gate_e, grad_up_e))
    partial = (
        place_back(row_grad.astype(bf16))
        + (dot_last(grad_gate_s, w_gate) + dot_last(grad_up_s, w_up)).reshape(cycle, tokens, D)
    )
    grad_act_two = scatter_ctx(partial.astype(bf16), bits)
    expert_grads = None
    for r, (hidden_e, grad_gate_e, grad_up_e) in enumerate(grad_shares):
        grads = (
            dot_first(rows, grad_gate_e),
            dot_first(rows, grad_up_e),
            dot_first(hidden_e, grad_rows),
        )
        if r:
            grads = tuple(
                total + shift_fsdp(item.astype(bf16), groups, -r).astype(f32)
                for total, item in zip(expert_grads, grads)
            )
        expert_grads = grads
    grad_w_gate = rows_back(dot_first(flat_act, grad_gate_s))
    grad_w_up = rows_back(dot_first(flat_act, grad_up_s))
    grad_w_down = scatter_fsdp(grad_w_down.reshape(groups, -1, D), groups)

    grad_gain_two = jnp.sum(grad_act_two * mixed * factor_two, axis=0)
    grad_mixed = diff + norm_back_rows(mixed, factor_two, gain_two, grad_act_two)
    grad_mixed_low = grad_mixed.astype(bf16)
    grad_w_output = lax.psum_scatter(
        dot_first(attended_mine, grad_mixed_low).astype(bf16),
        everyone,
        scatter_dimension=0,
        tiled=True,
    ).astype(f32)
    grad_attended = dot_last(grad_mixed_low, w_output).astype(bf16)
    grad_attended = lax.all_to_all(
        jnp.transpose(grad_attended.reshape(tokens, cycle, DV // copies), (1, 0, 2)),
        "ctx",
        split_axis=0,
        concat_axis=0,
        tiled=True,
    ).reshape(length, DV // copies)
    grad_attended = same_head(grad_attended)
    delta = jnp.sum(grad_attended.astype(f32) * attended, axis=-1)
    grad_query, grad_keys, grad_values = attend_back(
        queries,
        keys,
        values,
        grad_attended,
        first_pos[None, :],
        log_total.reshape(1, length),
        delta[None, :],
    )
    grad_expanded = jnp.concatenate([grad_keys[:, :DN], grad_values], axis=-1).astype(bf16)
    grad_w_expand = rows_back(own_part(dot_first(latent, grad_expanded)))
    grad_latent = dot_last(own_part(grad_expanded), own_part(w_expand))
    normed_latent = latent_raw[:, :KVR] * factor_latent
    grad_gain_latent = jnp.sum(grad_latent * normed_latent, axis=0)
    grad_latent = norm_back_rows(latent_raw[:, :KVR], factor_latent, gain_latent, grad_latent)
    grad_rope = rotate(grad_keys[:, DN:], cosine, -sine) / copies
    grad_latent_raw = jnp.concatenate([grad_latent, grad_rope], axis=-1).astype(bf16)
    grad_query = grad_query * scale
    grad_query = jnp.concatenate(
        [grad_query[:, :DN], rotate(grad_query[:, DN:], cosine, -sine)], axis=-1
    ).astype(bf16)
    partial = dot_last(own_part(grad_query), own_part(w_query)) + dot_last(
        grad_latent_raw, w_latent
    )
    grad_act_one = scatter_ctx(partial.astype(bf16).reshape(cycle, tokens, D), bits)
    grad_gain_one = jnp.sum(partial * (all_hidden * factor_all), axis=0)
    grad_w_query = rows_back(own_part(dot_first(act_one, grad_query)))
    spare = jnp.zeros((cycle * groups, slab - slab_latent), f32)
    grad_gain_latent = jnp.concatenate(
        [grad_gain_latent.reshape(cycle * groups, slab_latent), spare], axis=1
    ).reshape(-1)
    grad_narrow = jnp.concatenate(
        [
            dot_first(act_one, grad_latent_raw),
            grad_gain_one[:, None],
            grad_gain_two[:, None],
            grad_gain_latent[:, None],
        ],
        axis=1,
    )
    grad_narrow = lax.psum_scatter(
        grad_narrow.astype(bf16), everyone, scatter_dimension=0, tiled=True
    ).astype(f32)
    _, factor_one = norm_forward(residual, gain_one)
    grad_input = grad_mixed + norm_back_rows(residual, factor_one, gain_one, grad_act_one)
    return (
        result.astype(bf16)[None],
        loss_value,
        grad_input[None],
        grad_narrow[:, KVR + DR],
        grad_w_query,
        grad_narrow[:, : KVR + DR],
        grad_narrow[:slab_latent, KVR + DR + 2],
        grad_w_expand,
        grad_w_output,
        grad_narrow[:, KVR + DR + 1],
        grad_w_gate,
        grad_w_up,
        grad_w_down,
        expert_grads[0][None],
        expert_grads[1][None],
        expert_grads[2][None],
    )


def solution(mesh):
    tokens = P("fsdp", "ctx", None)
    rows = P(("ctx", "fsdp"), None)
    gain = P(("ctx", "fsdp"))
    wide = P("ctx", None, "fsdp")
    deep = P("ctx", "fsdp", None)
    in_specs = (
        tokens,
        tokens,
        P("fsdp", None),
        tokens,
        tokens,
        gain,
        rows,
        rows,
        gain,
        rows,
        rows,
        gain,
        rows,
        rows,
        rows,
        wide,
        wide,
        deep,
    )
    out_specs = (
        tokens,
        P(),
        tokens,
        gain,
        rows,
        rows,
        gain,
        rows,
        rows,
        gain,
        rows,
        rows,
        rows,
        wide,
        wide,
        deep,
    )
    return jax.shard_map(shards, mesh=mesh, in_specs=in_specs, out_specs=out_specs, check_vma=False)
```

time: 3630 us -> 1230 us (0.34)
  waiting for transfers between devices: 2310 us -> 71 us
  Pallas kernels: 0 us -> 534 us
  local copies, waits for them, and re-layouts: 503 us -> 71.7 us
  blocking collectives: 240 us -> 78.8 us
  other arithmetic: 157 us -> 94 us
    reduce_scatter x8 -> x1, waiting for transfers between devices: 1420 us -> 0.01 us  [shards(): lax.psum_scatter(dot_first(attended_mine, grad_mixed_low).astype(bf16), e...]
    pallas_call x0 -> x8, Pallas kernels: none -> 534 us  [the longest x3 303 us: scatter_ctx(): pl.pallas_call(functools.partial(scatter_kernel, parts, bits), name='scat...]
    all_gather x11 -> x2, waiting for transfers between devices: 498 us -> 0.02 us  [the longest x1 0.02 us: shards(): narrow = lax.all_gather(narrow, everyone, axis=0, tiled=True)]
    unnamed x27 -> x5, waiting for transfers between devices: 228 us -> 0.75 us
    unnamed x179 -> x205, local copies, waits for them, and re-layouts: 200 us -> 15.6 us
    dynamic_update_slice x8 -> x0, local copies, waits for them, and re-layouts: 165 us -> none  [the longest x4 159 us: key_piece(): lax.dynamic_update_slice_in_dim(carry[1], lax.dynamic_slice_in_dim(carry[...]
    all_to_all x1 -> x0, blocking collectives: 110 us -> none  [shards(): lax.all_to_all(outgoing, 'ctx', split_axis=0, concat_axis=0, tiled=True)]
    all_to_all x3 -> x10, waiting for transfers between devices: 168 us -> 69.9 us  [the longest x4 28.5 us: rows_back(): lax.all_to_all(pieces, 'ctx', split_axis=0, concat_axis=0, tiled=True)]
  transfers between devices with their start and end apart: 26 -> 30, of which waited for: 17 -> 8; matrix products, arithmetic and copies ran while one was open for 14% -> 20% of each run, Pallas kernels for 0% -> 24%
where the time goes in v1:
time: 1230 us; the launch traced here: 1220 us
  Pallas kernels  534 us (43%)
  matrix products  297 us (24%)
  other arithmetic  94 us (8%)
  blocking collectives  78.8 us (6%)
  local copies, waits for them, and re-layouts  71.7 us (6%)
  waiting for transfers between devices  71 us (6%)
  starting transfers between devices  59.7 us (5%)
  between operations  18.4 us (1%)
    pallas_call x3, Pallas kernels, scatter_ctx(): pl.pallas_call(functools.partial(scatter_kernel, parts, bits), name='scat...  303 us
    pallas_call x3, Pallas kernels, gather_ctx(): pl.pallas_call(functools.partial(gather_kernel, parts, bits, events), nam...  207 us
    dot_general x13, matrix products, dot_last(): lax.dot_general(left, right, (((1,), (1,)), ((), ())), preferred_element_...  106 us
    dot_general x13, matrix products, dot_first(): lax.dot_general(left, right, (((0,), (0,)), ((), ())), preferred_element_...  80.7 us
    dot_general x13, matrix products, dot(): return jnp.dot(left, right, preferred_element_type=f32)  80.3 us
    all_gather x1, blocking collectives, shards(): all_probs = lax.all_gather(dense_probs, 'ctx', axis=0, tiled=True)  39.9 us
    unnamed x1, blocking collectives  38.9 us
    all_to_all x4, waiting for transfers between devices, rows_back(): lax.all_to_all(pieces, 'ctx', split_axis=0, concat_axis=0, tiled=True)  28.5 us
  transfers between devices with their start and end apart: 30, of which 8 were waited for; matrix products, arithmetic and copies ran while one was open for 20% of the time, Pallas kernels for 24%

profile of v1, /device:TPU:0, one launch (start us, length us, event | category | flops | bytes accessed | tf_op | source)
XLA Modules:
  0.0 1224.6 jit_solution(2804809729571284662)
XLA Ops:
  13.5 8.3 all-to-all-start.1
  23.0 77.6 %gather_ctx.3 = bf16[16,128,2048]{2,1,0:T(8,128)(2,1)} custom-call(bf16[128,2048]{1,0:T(8,128)(2,1)} %bitcast.336), custom_call_target="tpu_custom_call" | custom-call | tf_op jit(solution)/shard_map/gather_ctx/pallas_call | solution.py:174
  100.6 39.9 %all_gather.17 = f32[2048,16]{0,1:T(8,128)S(1)} all-gather(f32[128,16]{0,1:T(8,128)S(1)} %select_reduce_fusion.1), channel_id=1, replica_groups=mesh['ctx'=16,'fsdp'=2] {'ctx'}, dimensions={0}, use_global_device_ids=true | all-gather | bytes 139264 | tf_op jit(solution)/shard_map/all_gather | solution.py:478
  140.6 6.3 multiply_reduce_fusion.1
  160.0 13.5 %all-to-all-done = bf16[16,64,192]{2,1,0:T(8,128)(2,1)S(1)} async-done(((bf16[16,64,192]{2,1,0:T(8,128)(2,1)}), bf16[16,64,192]{2,1,0:T(8,128)(2,1)S(1)}, u32[]{:S(2)}, u32[]{:S(2)}) %all-to-all-start) | async-done | bytes 393248 | tf_op jit(solution)/shard_map/all_to_all | solution.py:434
  173.5 8.0 all-to-all-start.3
  183.1 9.2 all-to-all-done.3
  200.1 8.7 multiply_convert_fusion
  208.9 8.2 fusion.3
  230.3 8.6 multiply_convert_fusion.1
  252.9 10.6 attend.1
  265.8 7.2 all-to-all-start.2
  278.3 10.1 all-to-all-done.2
  294.4 66.9 %gather_ctx.4 = bf16[16,128,2048]{2,1,0:T(8,128)(2,1)} custom-call(bf16[128,2048]{1,0:T(8,128)(2,1)} %multiply_convert_fusion.15.x_ref), custom_call_target="tpu_custom_call" | custom-call | tf_op jit(solution)/shard_map/gather_ctx/pallas_call | solution.py:174
  376.0 6.6 fusion.98
  388.5 8.7 multiply_convert_fusion.10
  397.2 8.4 multiply_convert_fusion.3
  405.6 8.2 fusion.68
  420.9 12.1 add_convert_fusion.1.x_ref
  433.0 84.0 %scatter_ctx.3 = f32[128,2048]{1,0:T(8,128)} custom-call(bf16[16,128,2048]{2,1,0:T(8,128)(2,1)} %add_convert_fusion.1.x_ref), custom_call_target="tpu_custom_call" | custom-call | tf_op jit(solution)/shard_map/scatter_ctx/pallas_call | solution.py:244
  519.2 62.4 %gather_ctx.5 = bf16[16,128,2048]{2,1,0:T(8,128)(2,1)} custom-call(bf16[128,2048]{1,0:T(8,128)(2,1)} %fusion.109.x_ref), custom_call_target="tpu_custom_call" | custom-call | tf_op jit(solution)/shard_map/gather_ctx/pallas_call | solution.py:174
  589.2 8.5 multiply_convert_fusion.8
  597.7 6.4 fusion.100
  604.2 6.6 fusion.104
  617.4 9.8 convolution_add_fusion.1
  627.2 10.9 multiply_convert_fusion.7
  638.0 8.9 fusion.116
  647.0 15.1 %add_convert_fusion.2 = bf16[1152,2048]{1,0:T(8,128)(2,1)S(1)} fusion(f32[1152,2048]{1,0:T(8,128)} %fusion.116, f32[1152,2048]{1,0:T(8,128)} %fusion.104, f32[1152,2048]{1,0:T(8,128)} %fusion.100, bf16[1152,704]{0,1:T(8,128)(2,1)} %get-tuple-element.136, bf16[2048,704]{0,1:T(8,128)(2,1)} %collective-permute-done.3), kind=kOutput, calls=%fused_computation.9 | convolution fusion | flops 3331325952 | bytes 37535744 | tf_op jit(solution)/shard_map/dot_general | solution.py:68
  662.1 11.7 add_convert_fusion.x_ref
  673.8 82.6 %scatter_ctx.4 = f32[128,2048]{1,0:T(8,128)} custom-call(bf16[16,128,2048]{2,1,0:T(8,128)(2,1)} %add_convert_fusion.x_ref), custom_call_target="tpu_custom_call" | custom-call | tf_op jit(solution)/shard_map/scatter_ctx/pallas_call | solution.py:244
  760.2 6.3 fusion.29
  775.1 8.6 all-to-all-done.5
  784.7 13.3 %attend_back.1 = (f32[2048,192]{1,0:T(8,128)}, f32[2048,192]{1,0:T(8,128)}, f32[2048,128]{1,0:T(8,128)}) custom-call(bf16[2048,192]{1,0:T(8,128)(2,1)} %fusion.5.q_ref, bf16[2048,192]{1,0:T(8,128)(2,1)} %pad_maximum_fusion.3.k_ref, bf16[2048,128]{1,0:T(8,128)(2,1)} %get-tuple-element.155.v_ref, bf16[2048,128]{1,0:T(8,128)(2,1)} %bitcast.352, ...), custom_call_target="tpu_custom_call" | custom-call | flops 3489660928 | bytes 8192000 | tf_op jit(solution)/shard_map/attend_back/pallas_call | solution.py:348
  801.7 6.1 fusion.36
  817.3 11.0 convolution_convert_fusion.5
  828.3 10.3 fusion.1
  838.6 13.7 %multiply_reduce_fusion = (bf16[2048]{0:T(1024)(128)(2,1)S(1)}, bf16[2048,2048]{1,0:T(8,128)(2,1)}) fusion(bf16[16,128,2048]{2,1,0:T(8,128)(2,1)} %gather_ctx.3, f32[2048]{0:T(1024)S(1)} %copy-done.57, f32[2048,2048]{1,0:T(8,128)} %fusion.1, bf16[2048,192]{1,0:T(8,128)(2,1)S(1)} %bitcast.349, bf16[2048,32]{1,0:T(8,128)(2,1)S(1)} %get-tuple-element.142, ...), kind=kOutput, calls=%fused_computation.1 | convolution fusion | flops 1638135808 | bytes 35139584 | tf_op jit(solution)/shard_map/dot_general | solution.py:68
  867.5 12.4 %copy.206 = bf16[2048,2048]{1,0:T(8,128)(2,1)} copy(bf16[2048,2048]{0,1:T(8,128)(2,1)} %bitcast.318) | data formatting | bytes 16777216 | tf_op jit(solution)/shard_map/dot_general | solution.py:64
  879.9 8.5 convolution_convert_fusion.4
  899.4 12.6 %copy.210 = bf16[2048,2048]{1,0:T(8,128)(2,1)} copy(bf16[2048,2048]{0,1:T(8,128)(2,1)} %bitcast.306) | data formatting | bytes 16777216 | tf_op jit(solution)/shard_map/dot_general | solution.py:64
  912.0 6.0 fusion.57
  929.1 38.9 %all-reduce.2 = f32[32]{0:T(128)S(1)} all-reduce(f32[32]{0:T(128)S(1)} %dynamic-update-slice), channel_id=1, replica_groups=mesh['ctx'=16,'fsdp'=2] {'ctx','fsdp'}, use_global_device_ids=true, to_apply=%add.2 | all-reduce | flops 32 | bytes 256
  994.0 136.9 %scatter_ctx.5 = f32[128,2048]{1,0:T(8,128)} custom-call(bf16[16,128,2048]{2,1,0:T(8,128)(2,1)} %bitcast.319), custom_call_target="tpu_custom_call" | custom-call | tf_op jit(solution)/shard_map/scatter_ctx/pallas_call | solution.py:244
  1141.9 14.7 %all-to-all-done.8 = bf16[16,64,176]{2,1,0:T(8,128)(2,1)S(1)} async-done(((bf16[16,64,176]{2,1,0:T(8,128)(2,1)}), bf16[16,64,176]{2,1,0:T(8,128)(2,1)S(1)}, u32[]{:S(2)}, u32[]{:S(2)}) %all-to-all-start.8) | async-done | bytes 360480 | tf_op jit(solution)/shard_map/all_to_all | solution.py:443
  1176.9 8.3 all-to-all-done.6
  1187.2 10.3 add_bitcast_fusion
  1197.5 7.1 add_bitcast_fusion.1
  1204.7 7.0 add_bitcast_fusion.2
  (396 shorter events, 240.4 us)
Async XLA Ops:
  7.2 190.0 %all-gather.3.cloned.1.call-start = ((), (), s32[]{:S(2)}) async-start(), calls=%async_computation.12 | async-start | bytes 2703360 | tf_op jit(solution)/shard_map/all_gather | solution.py:468
  11.2 277.3 %all-gather.5.cloned.1.call-start = ((), (), s32[]{:S(2)}) async-start(), calls=%async_computation.13 | async-start | bytes 8650752 | tf_op jit(solution)/shard_map/all_gather | solution.py:479
  13.5 135.1 %all-to-all-start.1 = ((bf16[16,16,256]{2,1,0:T(8,128)(2,1)}), bf16[16,16,256]{2,1,0:T(8,128)(2,1)S(1)}, u32[]{:S(2)}, u32[]{:S(2)}) async-start(bf16[16,16,256]{2,1,0:T(8,128)(2,1)} %copy.191), calls=%async_computation.1 | async-start | bytes 262144 | tf_op jit(solution)/shard_map/all_to_all | solution.py:434
  21.9 360.8 %collective-permute-start.2 = (bf16[2048,704]{0,1:T(8,128)(2,1)}, bf16[2048,704]{0,1:T(8,128)(2,1)}, u32[]{:S(2)}, u32[]{:S(2)}) collective-permute-start(bf16[2048,704]{0,1:T(8,128)(2,1)} %bitcast.374), channel_id=1, source_target_pairs={{0,1},{1,0},{2,3},{3,2},{4,5},{5,4},{6,7},{7,6},{8,9},{9,8},{10,11... | collective-permute-start | bytes 8650760 | tf_op jit(solution)/shard_map/ppermute | solution.py:377
  21.9 366.5 %collective-permute-start.3 = (bf16[2048,704]{0,1:T(8,128)(2,1)}, bf16[2048,704]{0,1:T(8,128)(2,1)}, u32[]{:S(2)}, u32[]{:S(2)}) collective-permute-start(bf16[2048,704]{0,1:T(8,128)(2,1)} %bitcast.373), channel_id=1, source_target_pairs={{0,1},{1,0},{2,3},{3,2},{4,5},{5,4},{6,7},{7,6},{8,9},{9,8},{10,11... | collective-permute-start | bytes 8650760 | tf_op jit(solution)/shard_map/ppermute | solution.py:377
  22.4 374.7 %collective-permute-start.4 = (bf16[704,2048]{1,0:T(8,128)(2,1)}, bf16[704,2048]{1,0:T(8,128)(2,1)}, u32[]{:S(2)}, u32[]{:S(2)}) collective-permute-start(bf16[704,2048]{1,0:T(8,128)(2,1)} %bitcast.372), channel_id=1, source_target_pairs={{0,1},{1,0},{2,3},{3,2},{4,5},{5,4},{6,7},{7,6},{8,9},{9,8},{10,11... | collective-permute-start | bytes 8650760 | tf_op jit(solution)/shard_map/ppermute | solution.py:377
  22.5 158.9 %collective-permute-start.7 = (bf16[88,2048]{1,0:T(8,128)(2,1)}, bf16[88,2048]{1,0:T(8,128)(2,1)S(1)}, u32[]{:S(2)}, u32[]{:S(2)}) collective-permute-start(bf16[88,2048]{1,0:T(8,128)(2,1)} %param.32), channel_id=1, source_target_pairs={{0,1},{1,0},{2,3},{3,2},{4,5},{5,4},{6,7},{7,6},{8,9},{9,8},{10,11... | collective-permute-start | bytes 1081352 | tf_op jit(solution)/shard_map/ppermute | solution.py:377
  23.0 77.6 %copy-start.67 = (s32[1,128,6]{1,0,2:T(1,128)S(1)}, s32[1,128,6]{1,0,2:T(1,128)}, u32[]{:S(2)}) copy-start(s32[1,128,6]{1,0,2:T(1,128)} %param.21) | copy-start | bytes 9220
  23.0 77.6 %copy-start.62 = (f32[1,128,6]{1,0,2:T(1,128)S(1)}, f32[1,128,6]{1,0,2:T(1,128)}, u32[]{:S(2)}) copy-start(f32[1,128,6]{1,0,2:T(1,128)} %param.22) | copy-start | bytes 9220
  148.6 24.9 %all-to-all-start = ((bf16[16,64,192]{2,1,0:T(8,128)(2,1)}), bf16[16,64,192]{2,1,0:T(8,128)(2,1)S(1)}, u32[]{:S(2)}, u32[]{:S(2)}) async-start(bf16[16,64,192]{2,1,0:T(8,128)(2,1)} %bitcast.304), calls=%async_computation | async-start | bytes 1048576 | tf_op jit(solution)/shard_map/all_to_all | solution.py:434
  152.2 29.4 %copy-start.44 = (bf16[88,2048]{1,0:T(8,128)(2,1)S(1)}, bf16[88,2048]{1,0:T(8,128)(2,1)}, u32[]{:S(2)}) copy-start(bf16[88,2048]{1,0:T(8,128)(2,1)} %param.32) | copy-start | bytes 1081348
  152.2 92.6 %copy-start.53 = (f32[2048]{0:T(1024)}, f32[2048]{0:T(1024)S(1)}, u32[]{:S(2)}) copy-start(f32[2048]{0:T(1024)S(1)} %subtract_convert_fusion) | copy-start | bytes 24580
  160.0 40.2 %copy-start.56 = (f32[2048]{0:T(1024)}, f32[2048]{0:T(1024)S(1)}, u32[]{:S(2)}) copy-start(f32[2048]{0:T(1024)S(1)} %get-tuple-element.169) | copy-start | bytes 24580
  160.0 22.4 %collective-permute-start.1 = (bf16[16,16,256]{2,1,0:T(8,128)(2,1)S(1)}, bf16[16,16,256]{2,1,0:T(8,128)(2,1)S(1)}, u32[]{:S(2)}, u32[]{:S(2)}) collective-permute-start(bf16[16,16,256]{2,1,0:T(8,128)(2,1)S(1)} %all-to-all-done.1), channel_id=1, source_target_pairs={{0,1},{1,0},{2,3},{3,2},{4,5},{5,4},{6,7},{7,6},{8,9},{9,8},{10,11... | collective-permute-start | bytes 393224 | tf_op jit(solution)/shard_map/ppermute | solution.py:377
  173.5 18.8 %all-to-all-start.3 = ((bf16[16,64,176]{2,1,0:T(8,128)(2,1)}), bf16[16,64,176]{2,1,0:T(8,128)(2,1)}, u32[]{:S(2)}, u32[]{:S(2)}) async-start(bf16[16,64,176]{2,1,0:T(8,128)(2,1)} %bitcast.303), calls=%async_computation.3 | async-start | bytes 1048576 | tf_op jit(solution)/shard_map/all_to_all | solution.py:434
  181.5 15.5 %collective-permute-start = (bf16[16,64,192]{2,1,0:T(8,128)(2,1)S(1)}, bf16[16,64,192]{2,1,0:T(8,128)(2,1)S(1)}, u32[]{:S(2)}, u32[]{:S(2)}) collective-permute-start(bf16[16,64,192]{2,1,0:T(8,128)(2,1)S(1)} %all-to-all-done), channel_id=1, source_target_pairs={{0,1},{1,0},{2,3},{3,2},{4,5},{5,4},{6,7},{7,6},{8,9},{9,8},{10,11... | collective-permute-start | bytes 1179656 | tf_op jit(solution)/shard_map/ppermute | solution.py:377
  192.3 73.5 %all-to-all-start.4 = ((bf16[16,64,176]{2,1,0:T(8,128)(2,1)}), bf16[16,64,176]{2,1,0:T(8,128)(2,1)}, u32[]{:S(2)}, u32[]{:S(2)}) async-start(bf16[16,64,176]{2,1,0:T(8,128)(2,1)} %bitcast.302), calls=%async_computation.4 | async-start | bytes 1048576 | tf_op jit(solution)/shard_map/all_to_all | solution.py:434
  196.8 77.3 %collective-permute-start.5 = (bf16[16,64,176]{2,1,0:T(8,128)(2,1)}, bf16[16,64,176]{2,1,0:T(8,128)(2,1)}, u32[]{:S(2)}, u32[]{:S(2)}) collective-permute-start(bf16[16,64,176]{2,1,0:T(8,128)(2,1)} %all-to-all-done.3), channel_id=1, source_target_pairs={{0,1},{1,0},{2,3},{3,2},{4,5},{5,4},{6,7},{7,6},{8,9},{9,8},{10,11... | collective-permute-start | bytes 1081352 | tf_op jit(solution)/shard_map/ppermute | solution.py:377
  197.2 41.7 %copy-start.16 = (bf16[2,16,64,192]{3,2,0,1:T(8,128)(2,1)}, bf16[2,16,64,192]{3,2,0,1:T(8,128)(2,1)S(1)}, u32[]{:S(2)}) copy-start(bf16[2,16,64,192]{3,2,0,1:T(8,128)(2,1)S(1)} %pad_maximum_fusion.2) | copy-start | bytes 2359300
  200.1 30.2 %copy-start.49 = (f32[2048]{0:T(1024)}, f32[2048]{0:T(1024)S(1)}, u32[]{:S(2)}) copy-start(f32[2048]{0:T(1024)S(1)} %get-tuple-element.125) | copy-start | bytes 24580
  265.8 22.7 %all-to-all-start.2 = ((bf16[16,128,128]{1,2,0:T(8,128)(2,1)}), bf16[16,128,128]{1,2,0:T(8,128)(2,1)S(1)}, u32[]{:S(2)}, u32[]{:S(2)}) async-start(bf16[16,128,128]{1,2,0:T(8,128)(2,1)} %copy.197), calls=%async_computation.2 | async-start | bytes 1048576 | tf_op jit(solution)/shard_map/all_to_all | solution.py:504
  273.9 2.1 collective-permute-start.6
  293.4 67.9 %copy-start.65 = (f32[128]{0:T(128)}, f32[128]{0:T(128)S(1)}, u32[]{:S(2)}) copy-start(f32[128]{0:T(128)S(1)} %add_rsqrt_fusion.3) | copy-start | bytes 1540
  366.3 22.2 %copy-start.2 = (bf16[16,72,2048]{2,1,0:T(8,128)(2,1)}, bf16[16,72,2048]{2,1,0:T(8,128)(2,1)S(1)}, u32[]{:S(2)}) copy-start(bf16[16,72,2048]{2,1,0:T(8,128)(2,1)S(1)} %convolution_convert_fusion.1) | copy-start | bytes 14155780
  388.5 25.4 %slice-start = ((s8[8388608]{0:T(1024)(128)(4,1)}), s8[4194304]{0:T(1024)(128)(4,1)S(1)}, s32[]{:S(2)}) async-start(s8[8388608]{0:T(1024)(128)(4,1)} %bitcast.307), calls=%async_computation.16 | async-start | bytes 8388608
  433.0 84.0 %copy-start.12 = (bf16[1,128,2048]{2,1,0:T(8,128)(2,1)S(1)}, bf16[1,128,2048]{2,1,0:T(8,128)(2,1)}, u32[]{:S(2)}) copy-start(bf16[1,128,2048]{2,1,0:T(8,128)(2,1)} %param.19) | copy-start | bytes 1572868
  673.8 82.6 %copy-start.1 = (f32[128,2048]{1,0:T(8,128)S(1)}, f32[128,2048]{1,0:T(8,128)}, u32[]{:S(2)}) copy-start(f32[128,2048]{1,0:T(8,128)} %scatter_ctx.3) | copy-start | bytes 3145732
  673.8 82.6 %copy-start.52 = (f32[2048]{0:T(1024)S(1)}, f32[2048]{0:T(1024)}, u32[]{:S(2)}) copy-start(f32[2048]{0:T(1024)} %get-tuple-element.124) | copy-start | bytes 24580
  673.8 82.6 %copy-start.66 = (f32[128]{0:T(128)S(1)}, f32[128]{0:T(128)}, u32[]{:S(2)}) copy-start(f32[128]{0:T(128)} %copy-done.65) | copy-start | bytes 1540
  767.4 16.2 %all-to-all-start.5 = ((bf16[16,128,128]{2,1,0:T(8,128)(2,1)}), bf16[16,128,128]{2,1,0:T(8,128)(2,1)S(1)}, u32[]{:S(2)}, u32[]{:S(2)}) async-start(bf16[16,128,128]{2,1,0:T(8,128)(2,1)} %bitcast.301), calls=%async_computation.5 | async-start | bytes 1048576 | tf_op jit(solution)/shard_map/all_to_all | solution.py:605
  772.9 438.8 %reduce-scatter.7.cloned.1.call-start = ((), (), s32[]{:S(2)}) async-start(), calls=%async_computation.15 | async-start | bytes 2703360
  784.7 23.4 %slice-start.6 = ((s8[4718592]{0:T(1024)(128)(4,1)}), s8[524288]{0:T(1024)(128)(4,1)S(1)}, s32[]{:S(2)}) async-start(s8[4718592]{0:T(1024)(128)(4,1)} %bitcast.321), calls=%async_computation.22 | async-start | bytes 1048576
  807.9 30.8 %copy-start.21 = (bf16[2048,32]{1,0:T(8,128)(2,1)}, bf16[2048,32]{1,0:T(8,128)(2,1)S(1)}, u32[]{:S(2)}) copy-start(bf16[2048,32]{1,0:T(8,128)(2,1)S(1)} %get-tuple-element.142) | copy-start | bytes 393220
  808.0 30.7 %copy-start.23 = (bf16[2048,128]{1,0:T(8,128)(2,1)}, bf16[2048,128]{1,0:T(8,128)(2,1)S(1)}, u32[]{:S(2)}) copy-start(bf16[2048,128]{1,0:T(8,128)(2,1)S(1)} %slice.167) | copy-start | bytes 1572868
  860.3 354.3 %reduce-scatter.5.cloned.1.call-start = ((), (), s32[]{:S(2)}) async-start(), calls=%async_computation.14 | async-start | bytes 8650752 | tf_op jit(solution)/shard_map/reduce_scatter | solution.py:598
  888.4 298.8 %collective-permute-start.15 = (bf16[704,2048]{1,0:T(8,128)(2,1)}, bf16[704,2048]{1,0:T(8,128)(2,1)}, u32[]{:S(2)}, u32[]{:S(2)}) collective-permute-start(bf16[704,2048]{1,0:T(8,128)(2,1)} %convolution_convert_fusion.4), channel_id=1, source_target_pairs={{0,1},{1,0},{2,3},{3,2},{4,5},{5,4},{6,7},{7,6},{8,9},{9,8},{10,11... | collective-permute-start | bytes 8650760 | tf_op jit(solution)/shard_map/ppermute | solution.py:377
  893.6 303.9 %collective-permute-start.14 = (bf16[2048,704]{0,1:T(8,128)(2,1)}, bf16[2048,704]{0,1:T(8,128)(2,1)}, u32[]{:S(2)}, u32[]{:S(2)}) collective-permute-start(bf16[2048,704]{0,1:T(8,128)(2,1)} %convolution_convert_fusion.2), channel_id=1, source_target_pairs={{0,1},{1,0},{2,3},{3,2},{4,5},{5,4},{6,7},{7,6},{8,9},{9,8},{10,11... | collective-permute-start | bytes 8650760 | tf_op jit(solution)/shard_map/ppermute | solution.py:377
  899.3 305.3 %collective-permute-start.13 = (bf16[2048,704]{0,1:T(8,128)(2,1)}, bf16[2048,704]{0,1:T(8,128)(2,1)}, u32[]{:S(2)}, u32[]{:S(2)}) collective-permute-start(bf16[2048,704]{0,1:T(8,128)(2,1)} %convolution_convert_fusion.3), channel_id=1, source_target_pairs={{0,1},{1,0},{2,3},{3,2},{4,5},{5,4},{6,7},{7,6},{8,9},{9,8},{10,11... | collective-permute-start | bytes 8650760 | tf_op jit(solution)/shard_map/ppermute | solution.py:377
  920.2 49.0 %collective-permute-start.11 = (bf16[16,64,176]{2,1,0:T(8,128)(2,1)}, bf16[16,64,176]{2,1,0:T(8,128)(2,1)S(1)}, u32[]{:S(2)}, u32[]{:S(2)}) collective-permute-start(bf16[16,64,176]{2,1,0:T(8,128)(2,1)} %fusion.73), channel_id=1, source_target_pairs={{0,1},{1,0},{2,3},{3,2},{4,5},{5,4},{6,7},{7,6},{8,9},{9,8},{10,11... | collective-permute-start | bytes 1081352 | tf_op jit(solution)/shard_map/ppermute | solution.py:377
  924.1 53.0 %collective-permute-start.10 = (bf16[16,64,176]{2,1,0:T(8,128)(2,1)}, bf16[16,64,176]{2,1,0:T(8,128)(2,1)}, u32[]{:S(2)}, u32[]{:S(2)}) collective-permute-start(bf16[16,64,176]{2,1,0:T(8,128)(2,1)} %fusion.72), channel_id=1, source_target_pairs={{0,1},{1,0},{2,3},{3,2},{4,5},{5,4},{6,7},{7,6},{8,9},{9,8},{10,11... | collective-permute-start | bytes 1081352 | tf_op jit(solution)/shard_map/ppermute | solution.py:377
  969.2 10.3 collective-permute-start.12
  971.4 161.1 %all-to-all-start.9 = ((bf16[16,64,176]{2,1,0:T(8,128)(2,1)}), bf16[16,64,176]{2,1,0:T(8,128)(2,1)S(1)}, u32[]{:S(2)}, u32[]{:S(2)}) async-start(bf16[16,64,176]{2,1,0:T(8,128)(2,1)} %fusion.50), calls=%async_computation.10 | async-start | bytes 1048576 | tf_op jit(solution)/shard_map/all_to_all | solution.py:443
  984.9 156.3 %collective-permute-start.9 = (bf16[16,16,256]{2,1,0:T(8,128)(2,1)S(1)}, bf16[16,16,256]{2,1,0:T(8,128)(2,1)S(1)}, u32[]{:S(2)}, u32[]{:S(2)}) collective-permute-start(bf16[16,16,256]{2,1,0:T(8,128)(2,1)S(1)} %fusion.86), channel_id=1, source_target_pairs={{0,1},{1,0},{2,3},{3,2},{4,5},{5,4},{6,7},{7,6},{8,9},{9,8},{10,11... | collective-permute-start | bytes 393224 | tf_op jit(solution)/shard_map/ppermute | solution.py:377
  993.8 166.5 %collective-permute-start.8 = (bf16[16,64,192]{2,1,0:T(8,128)(2,1)}, bf16[16,64,192]{2,1,0:T(8,128)(2,1)S(1)}, u32[]{:S(2)}, u32[]{:S(2)}) collective-permute-start(bf16[16,64,192]{2,1,0:T(8,128)(2,1)} %fusion.71), channel_id=1, source_target_pairs={{0,1},{1,0},{2,3},{3,2},{4,5},{5,4},{6,7},{7,6},{8,9},{9,8},{10,11... | collective-permute-start | bytes 1179656 | tf_op jit(solution)/shard_map/ppermute | solution.py:377
  994.0 136.9 %copy-start.50 = (f32[2048]{0:T(1024)S(1)}, f32[2048]{0:T(1024)}, u32[]{:S(2)}) copy-start(f32[2048]{0:T(1024)} %copy-done.49) | copy-start | bytes 24580
  1132.5 24.1 %all-to-all-start.8 = ((bf16[16,64,176]{2,1,0:T(8,128)(2,1)}), bf16[16,64,176]{2,1,0:T(8,128)(2,1)S(1)}, u32[]{:S(2)}, u32[]{:S(2)}) async-start(bf16[16,64,176]{2,1,0:T(8,128)(2,1)} %fusion.51), calls=%async_computation.9 | async-start | bytes 1048576 | tf_op jit(solution)/shard_map/all_to_all | solution.py:443
  1156.6 11.5 all-to-all-start.7
  1168.0 17.2 %all-to-all-start.6 = ((bf16[16,64,192]{2,1,0:T(8,128)(2,1)}), bf16[16,64,192]{2,1,0:T(8,128)(2,1)S(1)}, u32[]{:S(2)}, u32[]{:S(2)}) async-start(bf16[16,64,192]{2,1,0:T(8,128)(2,1)} %fusion.52), calls=%async_computation.6 | async-start | bytes 1048576 | tf_op jit(solution)/shard_map/all_to_all | solution.py:443
  (81 other events, 559.6 us)
Sparse Core Ops, SparseCore 0:
  11.4 78.6 all-gather.2
  93.0 90.9 all-gather.4
  860.5 137.0 reduce-scatter.6
  999.7 168.6 reduce-scatter.4

commit v2 on v1

v2 whole, which is shorter than its diff:
```python
import functools
import math

import jax
import jax.numpy as jnp
from jax import lax
from jax.experimental import pallas as pl
from jax.experimental.pallas import tpu as pltpu
from jax.sharding import PartitionSpec as P

D = 2048
H = 16
DN = 128
DR = 64
DV = 128
KVR = 512
TOPK = 6
WIDE = 256

EPS = 1e-06
NEG = -1e30
MESH = pl.DeviceIdType.MESH
f32 = jnp.float32
bf16 = jnp.bfloat16


def norm_forward(rows, gain):
    factor = lax.rsqrt(jnp.mean(rows * rows, axis=-1, keepdims=True) + EPS)
    return (rows * factor * gain, factor)


def norm_back_rows(rows, factor, gain, grad_out):
    scaled = grad_out * gain
    normed = rows * factor
    return factor * (scaled - normed * jnp.mean(scaled * normed, axis=-1, keepdims=True))


def rotate(values, cosine, sine):
    half = values.shape[-1] // 2
    first = values[..., :half]
    second = values[..., half:]
    return jnp.concatenate(
        [first * cosine - second * sine, second * cosine + first * sine], axis=-1
    )


def rope_tables(offsets):
    freqs = 10000.0 ** (-(jnp.arange(DR // 2, dtype=f32) * 2.0) / DR)
    angle = offsets.astype(f32)[:, None] * freqs[None, :]
    return (jnp.cos(angle), jnp.sin(angle))


def silu_grads(gate_val, up_val, grad_hidden):
    sigma = jax.nn.sigmoid(gate_val)
    grad_gate = grad_hidden * up_val * sigma * (1.0 + gate_val * (1.0 - sigma))
    grad_up = grad_hidden * gate_val * sigma
    return (grad_gate.astype(bf16), grad_up.astype(bf16))


def dot(left, right):
    return jnp.dot(left, right, preferred_element_type=f32)


def dot_first(left, right):
    return lax.dot_general(left, right, (((0,), (0,)), ((), ())), preferred_element_type=f32)


def dot_last(left, right):
    return lax.dot_general(left, right, (((1,), (1,)), ((), ())), preferred_element_type=f32)


def flip(me, mask):
    out = me
    bit = 1
    while bit <= mask:
        if mask & bit:
            out = out + bit * (1 - 2 * ((me // bit) % 2))
        bit *= 2
    return out


def row_parts(rows, bits):
    low, high = [1, 2], [1 << k for k in range(bits - 1, 1, -1)]
    orders = (high + low, high + low[::-1], low + high)
    units = rows // 16
    if units < 3:
        return ((0, rows, tuple(orders[0])),)
    third = max(1, units // 4)
    first = (units - third) // 2
    counts = (first * 16, (units - third - first) * 16, third * 16)
    parts, start = [], 0
    for count, order in zip(counts, orders):
        parts.append((start, count, tuple(order)))
        start += count
    return tuple(parts)


def all_parts(shapes, bits):
    return tuple(
        (a,) + part for a, shape in enumerate(shapes) for part in row_parts(shape[-2], bits)
    )


def greet(bits):
    me = lax.axis_index("ctx")
    barrier = pltpu.get_barrier_semaphore()
    for k in range(bits):
        pl.semaphore_signal(
            barrier, inc=1, device_id={"ctx": flip(me, 1 << k)}, device_id_type=MESH
        )
    pl.semaphore_wait(barrier, bits)


def gather_events(parts, bits):
    events = []
    for p, (_, _, _, order) in enumerate(parts):
        for slot in range(1 << bits):
            hops = [k for k, b in enumerate(order) if slot & b]
            for k in range(hops[-1] + 1 if hops else 0, bits):
                events.append((len(hops), k, p, slot, order[k]))
    return tuple(sorted(events))


def gather_kernel(parts, bits, events, count, *refs):
    x_refs, o_refs = refs[:count], refs[count : 2 * count]
    send_sem, recv_sem, own_sem = refs[2 * count :]
    me = lax.axis_index("ctx")
    own = [
        pltpu.make_async_copy(x_refs[a], o_refs[a].at[me], own_sem.at[a]) for a in range(count)
    ]
    for item in own:
        item.start()
    greet(bits)

    def copy(p, slot, bit, index):
        a, start, size, _ = parts[p]
        rows = pl.ds(start, size)
        block = flip(me, slot)
        return pltpu.make_async_remote_copy(
            src_ref=x_refs[a].at[rows] if slot == 0 else o_refs[a].at[block, rows],
            dst_ref=o_refs[a].at[block, rows],
            send_sem=send_sem.at[index],
            recv_sem=recv_sem.at[p, slot ^ bit],
            device_id={"ctx": flip(me, bit)},
            device_id_type=MESH,
        )

    def arrived(p, slot):
        a, start, size, order = parts[p]
        rows = pl.ds(start, size)
        bit = [b for b in order if slot & b][-1]
        pltpu.make_async_remote_copy(
            src_ref=x_refs[a].at[rows],
            dst_ref=o_refs[a].at[flip(me, slot), rows],
            send_sem=send_sem.at[0],
            recv_sem=recv_sem.at[p, slot],
            device_id={"ctx": flip(me, bit)},
            device_id_type=MESH,
        ).wait_recv()

    seen = set()
    started = []
    for index, (_, _, p, slot, bit) in enumerate(events):
        if slot and (p, slot) not in seen:
            arrived(p, slot)
            seen.add((p, slot))
        sent = copy(p, slot, bit, index)
        sent.start()
        started.append(sent)
    for p in range(len(parts)):
        for slot in range(1, 1 << bits):
            if (p, slot) not in seen:
                arrived(p, slot)
    for sent in started:
        sent.wait_send()
    for item in own:
        item.wait()


def gather_ctx(arrays, bits, collective):
    parts = all_parts([item.shape for item in arrays], bits)
    events = gather_events(parts, bits)
    count = len(arrays)
    return pl.pallas_call(
        functools.partial(gather_kernel, parts, bits, events, count),
        name="gather_ctx",
        out_shape=[jax.ShapeDtypeStruct((1 << bits,) + item.shape, item.dtype) for item in arrays],
        in_specs=[pl.BlockSpec(memory_space=pl.ANY)] * count,
        out_specs=[pl.BlockSpec(memory_space=pl.ANY)] * count,
        scratch_shapes=[
            pltpu.SemaphoreType.DMA((len(events),)),
            pltpu.SemaphoreType.DMA((len(parts), 1 << bits)),
            pltpu.SemaphoreType.DMA((count,)),
        ],
        compiler_params=pltpu.CompilerParams(collective_id=collective, has_side_effects=True),
    )(*arrays)


def gather_multiply_kernel(
    parts, bits, events, shares, tile, x_ref, rows_ref, dy_ref, *refs
):
    lefts, refs = refs[: 3 * shares], refs[3 * shares :]
    o_ref, outs, refs = refs[0], refs[1:4], refs[4:]
    rows, dy, left, sent, got, stage = refs[:6]
    send_sem, recv_sem, own_sem, load_sem, out_sem, far_sem, near_sem = refs[6:]
    me, place = lax.axis_index("ctx"), lax.axis_index("fsdp")
    half, width = left.shape[2], rows.shape[1]
    tiles = width // tile
    loads = [pltpu.make_async_copy(rows_ref, rows, load_sem.at[3 * shares])]
    loads.append(pltpu.make_async_copy(dy_ref, dy, load_sem.at[3 * shares + 1]))
    order = list(range(3, 3 * shares)) + [0, 1, 2]
    for i in range(3 * shares):
        loads.append(pltpu.make_async_copy(lefts[i], left.at[i], load_sem.at[i]))
    own = pltpu.make_async_copy(x_ref, o_ref.at[me], own_sem)
    own.start()
    barrier = pltpu.get_barrier_semaphore()
    for k in range(bits):
        pl.semaphore_signal(
            barrier, inc=1, device_id={"ctx": flip(me, 1 << k)}, device_id_type=MESH
        )
    for r in range(1, shares):
        pl.semaphore_signal(
            barrier, inc=1, device_id={"fsdp": (place + r) % shares}, device_id_type=MESH
        )
    pl.semaphore_wait(barrier, bits + shares - 1)
    for i in [0, 2 + 3 % (3 * shares), 1] if shares > 1 else [0, 2, 1]:
        loads[i].start()
    for i in range(2, len(loads)):
        if i != 2 + 3 % (3 * shares):
            loads[i].start()
    ready = set()

    def need(i):
        if i not in ready:
            loads[i].wait()
            ready.add(i)

    def copy(p, slot, bit, index):
        _, start, size, _ = parts[p]
        part = pl.ds(start, size)
        block = flip(me, slot)
        return pltpu.make_async_remote_copy(
            src_ref=x_ref.at[part] if slot == 0 else o_ref.at[block, part],
            dst_ref=o_ref.at[block, part],
            send_sem=send_sem.at[index],
            recv_sem=recv_sem.at[p, slot ^ bit],
            device_id={"ctx": flip(me, bit)},
            device_id_type=MESH,
        )

    def arrived(p, slot):
        _, start, size, path = parts[p]
        part = pl.ds(start, size)
        bit = [b for b in path if slot & b][-1]
        pltpu.make_async_remote_copy(
            src_ref=x_ref.at[part],
            dst_ref=o_ref.at[flip(me, slot), part],
            send_sem=send_sem.at[0],
            recv_sem=recv_sem.at[p, slot],
            device_id={"ctx": flip(me, bit)},
            device_id_type=MESH,
        ).wait_recv()

    def far(i, t):
        spot = (i - 3, slice(None), pl.ds(t * tile, tile))
        return pltpu.make_async_remote_copy(
            src_ref=sent.at[spot],
            dst_ref=got.at[spot],
            send_sem=far_sem.at[i - 3, t],
            recv_sem=near_sem.at[i - 3, t],
            device_id={"fsdp": (place + shares - i // 3) % shares},
            device_id_type=MESH,
        )

    def store(i, t):
        buffer = (i * tiles + t) % 2
        return pltpu.make_async_copy(
            stage.at[buffer], outs[i].at[:, pl.ds(t * tile, tile)], out_sem.at[i, t]
        )

    def multiply(i, t):
        need(2 + i)
        need(1 if i % 3 == 2 else 0)
        right = dy if i % 3 == 2 else rows
        total = dot_first(left[i], right[:, t * tile : (t + 1) * tile])
        if i >= 3:
            sent[i - 3, :, t * tile : (t + 1) * tile] = total.astype(bf16)
            far(i, t).start()
            return
        for r in range(1, shares):
            far(i + 3 * r, t).wait_recv()
            total = total + got[i + 3 * r - 3, :, t * tile : (t + 1) * tile].astype(f32)
        last = i * tiles + t - 2
        if last >= 0:
            store(last // tiles, last % tiles).wait()
        stage[(i * tiles + t) % 2] = total.astype(bf16)
        store(i, t).start()

    work = [(i, t) for i in order for t in range(tiles)]
    done = 0
    seen = set()
    started = []
    for index, (_, _, p, slot, bit) in enumerate(events):
        if slot and (p, slot) not in seen:
            arrived(p, slot)
            seen.add((p, slot))
        item = copy(p, slot, bit, index)
        item.start()
        started.append(item)
        first = bits * len(parts)
        if index >= first:
            while done < len(work) * (index - first + 1) // (len(events) - first):
                multiply(*work[done])
                done += 1
    for p in range(len(parts)):
        for slot in range(1, 1 << bits):
            if (p, slot) not in seen:
                arrived(p, slot)
    for item in started:
        item.wait_send()
    own.wait()
    for i in range(3, 3 * shares):
        for t in range(tiles):
            far(i, t).wait_send()
    for last in range(max(0, 3 * tiles - 2), 3 * tiles):
        store(last // tiles, last % tiles).wait()


def gather_multiply(x, rows, dy, lefts, bits, collective):
    parts = all_parts([x.shape], bits)
    events = gather_events(parts, bits)
    shares = len(lefts) // 3
    count, half = lefts[0].shape
    width = rows.shape[1]
    tile = width // 2
    anywhere = pl.BlockSpec(memory_space=pl.ANY)
    others = max(1, 3 * shares - 3)
    return pl.pallas_call(
        functools.partial(gather_multiply_kernel, parts, bits, events, shares, tile),
        name="gather_multiply",
        out_shape=[jax.ShapeDtypeStruct((1 << bits,) + x.shape, x.dtype)]
        + [jax.ShapeDtypeStruct((half, width), bf16)] * 3,
        in_specs=[anywhere] * (3 + 3 * shares),
        out_specs=[anywhere] * 4,
        scratch_shapes=[
            pltpu.VMEM((count, width), bf16),
            pltpu.VMEM((count, width), bf16),
            pltpu.VMEM((3 * shares, count, half), bf16),
            pltpu.VMEM((others, half, width), bf16),
            pltpu.VMEM((others, half, width), bf16),
            pltpu.VMEM((2, half, tile), bf16),
            pltpu.SemaphoreType.DMA((len(events),)),
            pltpu.SemaphoreType.DMA((len(parts), 1 << bits)),
            pltpu.SemaphoreType.DMA,
            pltpu.SemaphoreType.DMA((3 * shares + 2,)),
            pltpu.SemaphoreType.DMA((3, width // tile)),
            pltpu.SemaphoreType.DMA((others, width // tile)),
            pltpu.SemaphoreType.DMA((others, width // tile)),
        ],
        compiler_params=pltpu.CompilerParams(
            collective_id=collective, has_side_effects=True, vmem_limit_bytes=60 << 20
        ),
    )(x, rows, dy, *lefts)


def scatter_events(parts, bits):
    events = []
    for p, (_, _, _, order) in enumerate(parts):
        for slot in range(1, 1 << bits):
            k = [i for i, b in enumerate(order) if slot & b][0]
            later = tuple(-int(bool(slot & b)) for b in order[k + 1 :])
            events.append((k, later, p, slot))
    return tuple((k, p, slot) for k, _, p, slot in sorted(events))


def scatter_kernel(parts, bits, events, count, *refs):
    x_refs, o_refs = refs[:count], refs[count : 2 * count]
    recvs, sends, owns = (refs[(2 + i) * count : (3 + i) * count] for i in range(3))
    send_sem, recv_sem, own_sem = refs[5 * count :]
    me = lax.axis_index("ctx")
    later = [sorted({s for k, p, s in events if k and parts[p][0] == a}) for a in range(count)]

    def load(a, slot):
        place = later[a].index(slot) + 1 if slot else 0
        return pltpu.make_async_copy(
            x_refs[a].at[flip(me, slot)], owns[a].at[place], own_sem.at[a, place]
        )

    greet(bits)

    def copy(p, slot, k, src):
        a, start, size, order = parts[p]
        return pltpu.make_async_remote_copy(
            src_ref=src,
            dst_ref=recvs[a].at[slot - 1, pl.ds(start, size)],
            send_sem=send_sem.at[p, slot - 1],
            recv_sem=recv_sem.at[p, slot - 1],
            device_id={"ctx": flip(me, order[k])},
            device_id_type=MESH,
        )

    loaded = set()

    def add_up(p, slot, k):
        a, start, size, order = parts[p]
        place = later[a].index(slot) + 1 if slot else 0
        if (a, slot) not in loaded:
            load(a, slot).wait()
            loaded.add((a, slot))
        for e in range(k):
            other = slot | order[e]
            copy(p, other, e, recvs[a].at[other - 1, pl.ds(start, size)]).wait_recv()
        target = sends[a].at[place - 1] if slot else o_refs[a]

        @pl.loop(0, size // 16)
        def _(t):
            part = pl.ds(pl.multiple_of(start + t * 16, 16), 16)
            total = owns[a][place, part].astype(f32)
            for e in range(k):
                total = total + recvs[a][(slot | order[e]) - 1, part].astype(f32)
            target[part] = total.astype(target.dtype)

    started = []
    first = [event for event in events if event[0] == 0]
    for index, (k, p, slot) in enumerate(events):
        a, start, size, order = parts[p]
        rows = pl.ds(start, size)
        if k == 0:
            src = x_refs[a].at[flip(me, slot), rows]
        else:
            add_up(p, slot, k)
            src = sends[a].at[later[a].index(slot), rows]
        sent = copy(p, slot, k, src)
        sent.start()
        started.append(sent)
        if index == len(first) // 2:
            for a in range(count):
                for own in [0] + later[a]:
                    load(a, own).start()
    for p in range(len(parts)):
        add_up(p, 0, bits)
    for sent in started:
        sent.wait_send()


def scatter_ctx(arrays, bits, collective):
    shapes = [item.shape[1:] for item in arrays]
    parts = all_parts(shapes, bits)
    parts = tuple((a, start, size, order[::-1]) for a, start, size, order in parts)
    events = scatter_events(parts, bits)
    count = len(arrays)
    others = (1 << bits) - 1
    held = [
        1 + len({s for k, p, s in events if k and parts[p][0] == a}) for a in range(count)
    ]
    return pl.pallas_call(
        functools.partial(scatter_kernel, parts, bits, events, count),
        name="scatter_ctx",
        out_shape=[jax.ShapeDtypeStruct(shape, f32) for shape in shapes],
        in_specs=[pl.BlockSpec(memory_space=pl.ANY)] * count,
        out_specs=[pl.BlockSpec(memory_space=pltpu.VMEM)] * count,
        scratch_shapes=[pltpu.VMEM((others,) + shape, bf16) for shape in shapes]
        + [pltpu.VMEM((n - 1,) + shape, bf16) for n, shape in zip(held, shapes)]
        + [pltpu.VMEM((n,) + shape, bf16) for n, shape in zip(held, shapes)]
        + [
            pltpu.SemaphoreType.DMA((len(parts), others)),
            pltpu.SemaphoreType.DMA((len(parts), others)),
            pltpu.SemaphoreType.DMA((count, max(held))),
        ],
        compiler_params=pltpu.CompilerParams(
            collective_id=collective, has_side_effects=True, vmem_limit_bytes=58 << 20
        ),
    )(*arrays)


def attend_kernel(block, count, q_ref, k_ref, v_ref, first_ref, wo_ref, o_ref, log_ref, part_ref):
    step = pl.program_id(0)
    for i in range(count):

        @pl.when(step == i)
        def _(i=i):
            extent = (i + 1) * block
            scores = dot_last(q_ref[...], k_ref[:extent, :])
            key_pos = lax.broadcasted_iota(jnp.int32, (block, extent), 1)
            query_pos = i * block + lax.broadcasted_iota(jnp.int32, (block, extent), 0)
            allowed = (key_pos >= first_ref[...]) & (key_pos <= query_pos)
            scores = jnp.where(allowed, scores, NEG)
            top = jnp.max(scores, axis=-1, keepdims=True)
            weights = jnp.exp(scores - top)
            total = jnp.sum(weights, axis=-1, keepdims=True)
            summed = dot(weights.astype(bf16), v_ref[:extent, :])
            o_ref[...] = summed / total
            log_ref[...] = top + jnp.log(total)
            part_ref[...] = dot((summed / total).astype(bf16), wo_ref[...]).astype(bf16)


def attend(queries, keys, values, first, w_output):
    length = queries.shape[0]
    block = min(256, length)
    count = length // block
    return pl.pallas_call(
        functools.partial(attend_kernel, block, count),
        name="attend",
        grid=(count,),
        out_shape=(
            jax.ShapeDtypeStruct((length, DV), f32),
            jax.ShapeDtypeStruct((length, 1), f32),
            jax.ShapeDtypeStruct((length, D), bf16),
        ),
        in_specs=[
            pl.BlockSpec((block, WIDE), lambda i: (i, 0)),
            pl.BlockSpec((length, WIDE), lambda i: (0, 0)),
            pl.BlockSpec((length, DV), lambda i: (0, 0)),
            pl.BlockSpec((block, 1), lambda i: (i, 0)),
            pl.BlockSpec((DV, D), lambda i: (0, 0)),
        ],
        out_specs=(
            pl.BlockSpec((block, DV), lambda i: (i, 0)),
            pl.BlockSpec((block, 1), lambda i: (i, 0)),
            pl.BlockSpec((block, D), lambda i: (i, 0)),
        ),
        compiler_params=pltpu.CompilerParams(vmem_limit_bytes=56 << 20),
        cost_estimate=pl.CostEstimate(
            flops=length * length * (DN + DR + DV),
            bytes_accessed=length * 2000,
            transcendentals=length * length // 2,
        ),
    )(queries, keys, values, first, w_output)


def attend_back_kernel(
    block, count, q_ref, k_ref, v_ref, m_ref, att_ref, wo_ref, first_ref, log_ref,
    dq_ref, dk_ref, dv_ref, gwo_ref,
):
    step = pl.program_id(0)

    @pl.when(step == 0)
    def _():
        dk_ref[...] = jnp.zeros_like(dk_ref)
        dv_ref[...] = jnp.zeros_like(dv_ref)
        gwo_ref[...] = jnp.zeros_like(gwo_ref)

    grad = dot_last(m_ref[...], wo_ref[...]).astype(bf16)
    gwo_ref[...] += dot_first(att_ref[...].astype(bf16), m_ref[...])
    delta = jnp.sum((grad.astype(f32) * att_ref[...]).T, axis=0, keepdims=True)
    for i in range(count):

        @pl.when(step == i)
        def _(i=i):
            extent = (i + 1) * block
            keys = k_ref[:extent, :]
            scores = dot_last(keys, q_ref[...])
            key_pos = lax.broadcasted_iota(jnp.int32, (extent, block), 0)
            query_pos = i * block + lax.broadcasted_iota(jnp.int32, (extent, block), 1)
            allowed = (key_pos >= first_ref[...]) & (key_pos <= query_pos)
            weights = jnp.where(allowed, jnp.exp(scores - log_ref[...]), 0.0)
            grad_weights = dot_last(v_ref[:extent, :], grad)
            grad_scores = (weights * (grad_weights - delta)).astype(bf16)
            dv_ref[:extent, :] += dot(weights.astype(bf16), grad)
            dk_ref[:extent, :] += dot(grad_scores, q_ref[...])
            dq_ref[...] = dot_first(grad_scores, keys)


def attend_back(queries, keys, values, grad_mixed, attended, w_output, first, log_total):
    length = queries.shape[0]
    block = min(256, length)
    count = length // block
    row = lambda: pl.BlockSpec((1, block), lambda i: (0, i))
    whole = lambda height, width: pl.BlockSpec((height, width), lambda i: (0, 0))
    part = lambda width: pl.BlockSpec((block, width), lambda i: (i, 0))
    return pl.pallas_call(
        functools.partial(attend_back_kernel, block, count),
        name="attend_back",
        grid=(count,),
        out_shape=(
            jax.ShapeDtypeStruct((length, WIDE), f32),
            jax.ShapeDtypeStruct((length, WIDE), f32),
            jax.ShapeDtypeStruct((length, DV), f32),
            jax.ShapeDtypeStruct((DV, D), f32),
        ),
        in_specs=[
            part(WIDE),
            whole(length, WIDE),
            whole(length, DV),
            part(D),
            part(DV),
            whole(DV, D),
            row(),
            row(),
        ],
        out_specs=(part(WIDE), whole(length, WIDE), whole(length, DV), whole(DV, D)),
        compiler_params=pltpu.CompilerParams(vmem_limit_bytes=56 << 20),
        cost_estimate=pl.CostEstimate(
            flops=length * length * (3 * (DN + DR) + 2 * DV),
            bytes_accessed=length * 4000,
            transcendentals=length * length // 2,
        ),
    )(queries, keys, values, grad_mixed, attended, w_output, first, log_total)


def lanes_of(value):
    return lax.broadcasted_iota(jnp.int32, value.shape, len(value.shape) - 1)


def swap_lanes(ropes):
    return jnp.where(
        lanes_of(ropes) % DR < DR // 2, -pltpu.roll(ropes, 96, 1), pltpu.roll(ropes, 32, 1)
    )


def assemble_kernel(
    cycle, slab, mine_ref, other_ref, mine_n_ref, other_n_ref,
    w_ref, we_ref, gains_ref, narrow_ref, expand_ref,
):
    me = lax.axis_index("fsdp")
    for f, (pack_ref, slim_ref) in enumerate(((mine_ref, mine_n_ref), (other_ref, other_n_ref))):
        owner = me if f == 0 else 1 - me

        @pl.loop(0, cycle)
        def _(c):
            rows = pl.ds(pl.multiple_of((c * 2 + owner) * slab, slab), slab)
            w_ref[rows, :DN] = pack_ref[c, :, :DN]
            w_ref[rows, 3 * DN :] = slim_ref[c, :, :KVR]
            tail = pack_ref[c, :, DN:256].astype(f32)
            slim = slim_ref[c, :, KVR:].astype(f32)
            ropes = jnp.where(lanes_of(tail) < DR, tail, pltpu.roll(slim, DR, 1))
            w_ref[rows, DN : 2 * DN] = ropes.astype(bf16)
            w_ref[rows, 2 * DN : 3 * DN] = swap_lanes(ropes).astype(bf16)
            narrow_ref[rows, :] = slim
            quarter = slab // 4
            for q in range(2):
                left = tail[2 * q * quarter : (2 * q + 1) * quarter]
                right = tail[(2 * q + 1) * quarter : (2 * q + 2) * quarter]
                both = jnp.where(lanes_of(left) < DR, pltpu.roll(left, DR, 1), right)
                spot = pl.ds(pl.multiple_of((c * 2 + owner) * quarter, quarter), quarter)
                expand_ref[spot, q * DN : (q + 1) * DN] = both

    we_ref[...] = expand_ref[...].astype(bf16)
    gains_ref[...] = narrow_ref[...].T[DR : DR + 8, :]


def assemble(mine, other, mine_n, other_n):
    cycle, slab, _ = mine.shape
    return pl.pallas_call(
        functools.partial(assemble_kernel, cycle, slab),
        name="assemble",
        out_shape=(
            jax.ShapeDtypeStruct((D, 3 * DN + KVR), bf16),
            jax.ShapeDtypeStruct((KVR, DN + DV), bf16),
            jax.ShapeDtypeStruct((8, D), f32),
        ),
        scratch_shapes=[pltpu.VMEM((D, DN), f32), pltpu.VMEM((KVR, DN + DV), f32)],
        compiler_params=pltpu.CompilerParams(vmem_limit_bytes=40 << 20),
    )(mine, other, mine_n, other_n)


def finish_kernel(cycle, slab, gw_ref, gwe_ref, w_ref, we_ref, extra_ref, first_ref, slim_ref):
    quarter = slab // 4
    turned = gw_ref[:, 2 * DN : 3 * DN]
    ropes = gw_ref[:, DN : 2 * DN] - swap_lanes(turned)
    gain_one = jnp.sum(gw_ref[...] * w_ref[...].astype(f32), axis=1, keepdims=True)
    gain_latent = jnp.sum(gwe_ref[...] * we_ref[...].astype(f32), axis=1, keepdims=True)
    lanes = lanes_of(ropes)
    first_ref[:, :DN] = gw_ref[:, :DN].astype(bf16)
    slim_ref[:, :KVR] = gw_ref[:, 3 * DN :].astype(bf16)
    tail = jnp.where(lanes < DR, pltpu.roll(ropes, DR, 1), 0.0)
    tail = jnp.where(lanes == DR, gain_one, tail)
    tail = jnp.where(lanes == DR + 1, extra_ref[...], tail)
    for part in range(cycle * 2):
        rows = slice(part * slab, (part + 1) * slab)
        some = slice(part * quarter, (part + 1) * quarter)
        expand = gwe_ref[some, :]
        pieces = [
            pltpu.roll(expand[:, :DN], DR, 1),
            expand[:, :DN],
            pltpu.roll(expand[:, DN:], DR, 1),
            expand[:, DN:],
        ]
        pieces = jnp.concatenate(pieces, axis=0)
        first_ref[rows, DN:] = jnp.where(lanes[rows] < DR, ropes[rows], pieces).astype(bf16)
        column = jnp.concatenate(
            [gain_latent[some], jnp.zeros((slab - quarter, 1), f32)], axis=0
        )
        slim_ref[rows, KVR:] = jnp.where(lanes[rows] == DR + 2, column, tail[rows]).astype(bf16)


def finish(grad_w, grad_we, w_cat, w_expand, extra, cycle, slab):
    return pl.pallas_call(
        functools.partial(finish_kernel, cycle, slab),
        name="finish",
        out_shape=(
            jax.ShapeDtypeStruct((D, 256), bf16),
            jax.ShapeDtypeStruct((D, KVR + DN), bf16),
        ),
        compiler_params=pltpu.CompilerParams(vmem_limit_bytes=56 << 20),
    )(grad_w, grad_we, w_cat, w_expand, extra)


def place_lanes(out_ref, pieces, width):
    total = width * len(pieces)
    for start in range(0, total, DN):
        tile = None
        for c in range(start // width, min(len(pieces), -(-(start + DN) // width))):
            moved = pieces[c]
            shift = (c * width - start) % 256
            if shift:
                moved = pltpu.roll(moved, shift, 1)
            moved = moved[:, :DN]
            lanes = lanes_of(moved) + start
            inside = (lanes >= c * width) & (lanes < (c + 1) * width)
            tile = jnp.where(inside, moved, 0.0 if tile is None else tile)
        out_ref[:, start : start + DN] = tile


def spread_kernel(cycle, slab, pack_ref, pack_s_ref, gq_ref, gwe_ref, gg_ref, gu_ref):
    quarter = slab // 4
    for ref, out_ref, start in (
        (pack_ref, gq_ref, 0),
        (pack_s_ref, gg_ref, 0),
        (pack_s_ref, gu_ref, 256),
    ):
        pieces = [ref[c, :, start : start + 256].astype(f32) for c in range(cycle)]
        place_lanes(out_ref, pieces, out_ref.shape[1] // cycle)
    for c in range(cycle):
        tail = pack_ref[c, :, DN:256].astype(f32)
        for q in range(2):
            left = tail[2 * q * quarter : (2 * q + 1) * quarter]
            right = tail[(2 * q + 1) * quarter : (2 * q + 2) * quarter]
            both = jnp.where(lanes_of(left) < DR, pltpu.roll(left, DR, 1), right)
            at = c * 2 * DN + q * DN
            gwe_ref[:, at : at + DN] = both


def spread(packed, packed_s, widths):
    cycle, slab, _ = packed.shape
    return pl.pallas_call(
        functools.partial(spread_kernel, cycle, slab),
        name="spread",
        out_shape=(
            jax.ShapeDtypeStruct((slab, widths[0]), f32),
            jax.ShapeDtypeStruct((slab // 4, widths[1]), f32),
            jax.ShapeDtypeStruct((slab, widths[2]), f32),
            jax.ShapeDtypeStruct((slab, widths[3]), f32),
        ),
        compiler_params=pltpu.CompilerParams(vmem_limit_bytes=40 << 20),
    )(packed, packed_s)


def fixed(shape):
    return pl.BlockSpec(shape, lambda i: (0,) * len(shape), pipeline_mode=pl.Buffered(1))


def second(shape):
    return pl.BlockSpec(shape, lambda i: (0, 1), pipeline_mode=pl.Buffered(1))


def by_rows(rows, cols):
    return pl.BlockSpec((rows, cols), lambda i: (i, 0))


def project_kernel(
    scale, x_ref, gain_ref, w_ref, gain_l_ref, we_ref, cos_ref, sin_ref,
    act_ref, q_ref, k_ref, v_ref, latent_ref, raw_ref,
):
    act = norm_forward(x_ref[...].astype(f32), gain_ref[...])[0].astype(bf16)
    act_ref[...] = act
    raw = dot(act, w_ref[...])
    turned = raw[:, DN : 2 * DN] * cos_ref[...] + raw[:, 2 * DN : 3 * DN] * sin_ref[...]
    low = lax.broadcasted_iota(jnp.int32, turned.shape, 1) < DR
    q_ref[:, :DN] = (raw[:, :DN] * scale).astype(bf16)
    q_ref[:, DN:] = jnp.where(low, turned * scale, 0.0).astype(bf16)
    raw_latent = raw[:, 3 * DN :]
    raw_ref[...] = raw_latent
    latent = norm_forward(raw_latent, gain_l_ref[...])[0].astype(bf16)
    latent_ref[...] = latent
    expanded = dot(latent, we_ref[...]).astype(bf16)
    k_ref[:, :DN] = expanded[:, :DN]
    k_ref[:, DN:] = jnp.where(low, pltpu.roll(turned, DR, 1), 0.0).astype(bf16)
    v_ref[...] = expanded[:, DN:]


def project(x, gain, w_cat, gain_latent, w_expand, cosine, sine, scale):
    length = x.shape[0]
    block = min(256, length)
    width = w_cat.shape[1]
    return pl.pallas_call(
        functools.partial(project_kernel, scale),
        name="project",
        grid=(length // block,),
        out_shape=(
            jax.ShapeDtypeStruct((length, D), bf16),
            jax.ShapeDtypeStruct((length, WIDE), bf16),
            jax.ShapeDtypeStruct((length, WIDE), bf16),
            jax.ShapeDtypeStruct((length, DV), bf16),
            jax.ShapeDtypeStruct((length, KVR), bf16),
            jax.ShapeDtypeStruct((length, KVR), f32),
        ),
        in_specs=[
            by_rows(block, D),
            fixed((1, D)),
            fixed((D, width)),
            fixed((1, KVR)),
            fixed((KVR, DN + DV)),
            by_rows(block, DN),
            by_rows(block, DN),
        ],
        out_specs=(
            by_rows(block, D),
            by_rows(block, WIDE),
            by_rows(block, WIDE),
            by_rows(block, DV),
            by_rows(block, KVR),
            by_rows(block, KVR),
        ),
        compiler_params=pltpu.CompilerParams(vmem_limit_bytes=40 << 20),
        cost_estimate=pl.CostEstimate(
            flops=2 * length * D * width, bytes_accessed=length * D * 6, transcendentals=0
        ),
    )(x, gain[None, :], w_cat, gain_latent[None, :], w_expand, cosine, sine)


def project_back_kernel(
    scale, copies, dq_ref, dk_ref, dv_ref, raw_ref, latent_ref, act_ref, cos_ref, sin_ref,
    w_ref, we_ref, gain_l_ref, keep_q_ref, keep_e_ref, part_ref, gw_ref, gwe_ref,
):
    @pl.when(pl.program_id(0) == 0)
    def _():
        gw_ref[...] = jnp.zeros_like(gw_ref)
        gwe_ref[...] = jnp.zeros_like(gwe_ref)

    grad_q = dq_ref[...] * scale
    grad_k = dk_ref[:, :DN]
    grad_v = dv_ref[...]
    if copies > 1:
        grad_q = grad_q * keep_q_ref[...]
        grad_k = grad_k * keep_e_ref[:, :DN]
        grad_v = grad_v * keep_e_ref[:, DN:]
    rope_q = grad_q[:, DN:]
    low = lax.broadcasted_iota(jnp.int32, rope_q.shape, 1) < DR
    rope_k = jnp.where(low, dk_ref[:, DN:] * (1.0 / copies), 0.0)
    ropes = jnp.where(low, rope_q, pltpu.roll(rope_k, DR, 1))
    expanded = jnp.concatenate([grad_k, grad_v], axis=-1).astype(bf16)
    grad_latent = dot_last(expanded, we_ref[...])
    raw = raw_ref[...]
    factor = lax.rsqrt(jnp.mean(raw * raw, axis=-1, keepdims=True) + EPS)
    grad_latent = norm_back_rows(raw, factor, gain_l_ref[...], grad_latent)
    grads = jnp.concatenate(
        [
            grad_q[:, :DN].astype(bf16),
            (ropes * cos_ref[...]).astype(bf16),
            (ropes * sin_ref[...]).astype(bf16),
            grad_latent.astype(bf16),
        ],
        axis=-1,
    )
    part_ref[...] = dot_last(grads, w_ref[...]).astype(bf16)
    gw_ref[...] += dot_first(act_ref[...], grads)
    gwe_ref[...] += dot_first(latent_ref[...], expanded)


def project_back(
    grad_q, grad_k, grad_v, raw, latent, act, cosine, sine, w_cat, w_expand, gain_latent, keep_q,
    keep_e, scale, copies,
):
    length = act.shape[0]
    block = min(256, length)
    width = w_cat.shape[1]
    return pl.pallas_call(
        functools.partial(project_back_kernel, scale, copies),
        name="project_back",
        grid=(length // block,),
        out_shape=(
            jax.ShapeDtypeStruct((length, D), bf16),
            jax.ShapeDtypeStruct((D, width), f32),
            jax.ShapeDtypeStruct((KVR, DN + DV), f32),
        ),
        in_specs=[
            by_rows(block, WIDE),
            by_rows(block, WIDE),
            by_rows(block, DV),
            by_rows(block, KVR),
            by_rows(block, KVR),
            by_rows(block, D),
            by_rows(block, DN),
            by_rows(block, DN),
            fixed((D, width)),
            fixed((KVR, DN + DV)),
            fixed((1, KVR)),
            fixed((1, WIDE)),
            fixed((1, DN + DV)),
        ],
        out_specs=(
            by_rows(block, D),
            pl.BlockSpec((D, width), lambda i: (0, 0)),
            pl.BlockSpec((KVR, DN + DV), lambda i: (0, 0)),
        ),
        compiler_params=pltpu.CompilerParams(vmem_limit_bytes=56 << 20),
        cost_estimate=pl.CostEstimate(
            flops=4 * length * D * width, bytes_accessed=length * D * 6, transcendentals=0
        ),
    )(
        grad_q, grad_k, grad_v, raw, latent, act, cosine, sine, w_cat, w_expand,
        gain_latent[None, :], keep_q, keep_e,
    )


def choose(shape, dim, place):
    return (lax.broadcasted_iota(jnp.int32, shape, dim) == place).astype(f32).astype(bf16)


def experts_kernel(shares, unit, capacity, tokens, *refs):
    x_ref, row_ref, col_ref, prob_ref = refs[:4]
    weights = refs[4 : 4 + 3 * shares]
    wgs_ref, wus_ref, wds_ref = refs[4 + 3 * shares : 7 + 3 * shares]
    outs = refs[7 + 3 * shares :]
    part_ref, rows_ref, gs_ref, us_ref, hs_ref = outs[:5]
    kept = outs[5:]
    tall, short = unit * tokens, unit * capacity
    count = x_ref.shape[0] // tall
    for j in range(count):
        inside = slice(j * tall, (j + 1) * tall)
        pick = choose((short, tall), 0, row_ref[:, inside])
        rows_ref[j * short : (j + 1) * short, :] = dot(pick, x_ref[inside, :]).astype(bf16)
    rows = rows_ref[...]
    total = 0.0
    for s in range(shares):
        wg_ref, wu_ref, wd_ref = weights[3 * s : 3 * s + 3]
        gate = dot_last(rows, wg_ref[...])
        up = dot_last(rows, wu_ref[...])
        hidden = (gate * jax.nn.sigmoid(gate) * up).astype(bf16)
        for ref, value in zip(kept[3 * s : 3 * s + 3], (gate, up, hidden)):
            ref[...] = value.astype(bf16)
        total = total + dot(hidden, wd_ref[...])
    total = (total * prob_ref[...]).astype(bf16)
    gate = dot(x_ref[...], wgs_ref[...])
    up = dot(x_ref[...], wus_ref[...])
    hidden = (gate * jax.nn.sigmoid(gate) * up).astype(bf16)
    gs_ref[...] = gate.astype(bf16)
    us_ref[...] = up.astype(bf16)
    hs_ref[...] = hidden
    for j in range(count):
        inside = slice(j * tall, (j + 1) * tall)
        put = choose((tall, short), 1, col_ref[inside, :])
        part_ref[inside, :] = (
            dot(put, total[j * short : (j + 1) * short, :])
            + dot(hidden[inside, :], wds_ref[...])
        ).astype(bf16)


def expert_sizes(capacity, tokens, length):
    unit = 1
    while unit * capacity % 16:
        unit *= 2
    blocks = max(4, unit)
    return unit, blocks * tokens, blocks * capacity, length // (blocks * tokens)


def experts(x, place_row, place_col, prob, weights, shared, capacity, tokens):
    length = x.shape[0]
    unit, tall, short, steps = expert_sizes(capacity, tokens, length)
    shares = len(weights) // 3
    half = weights[0].shape[0]
    width = shared[2].shape[0]
    wide = [fixed((half, D))] * (3 * shares)
    return pl.pallas_call(
        functools.partial(experts_kernel, shares, unit, capacity, tokens),
        name="experts",
        grid=(steps,),
        out_shape=[
            jax.ShapeDtypeStruct((length, D), bf16),
            jax.ShapeDtypeStruct((steps * short, D), bf16),
        ]
        + [jax.ShapeDtypeStruct((length, width), bf16)] * 3
        + [jax.ShapeDtypeStruct((steps * short, half), bf16)] * (3 * shares),
        in_specs=[
            by_rows(tall, D),
            pl.BlockSpec((1, tall), lambda i: (0, i)),
            by_rows(tall, 1),
            by_rows(short, 1),
        ]
        + wide
        + [fixed((D, width)), second((D, width)), fixed((width, D))],
        out_specs=[by_rows(tall, D), by_rows(short, D)]
        + [by_rows(tall, width)] * 3
        + [by_rows(short, half)] * (3 * shares),
        compiler_params=pltpu.CompilerParams(vmem_limit_bytes=58 << 20),
        cost_estimate=pl.CostEstimate(
            flops=6 * D * (steps * short * half * shares + length * width),
            bytes_accessed=30 << 20,
            transcendentals=0,
        ),
    )(x, place_row, place_col, prob, *weights, *shared)


def experts_back_kernel(shares, unit, capacity, tokens, *refs):
    d_ref, x_ref, row_ref, col_ref, prob_ref, gs_ref, us_ref, hs_ref = refs[:8]
    refs = refs[8:]
    kept, refs = refs[: 2 * shares], refs[2 * shares :]
    weights, refs = refs[: 3 * shares], refs[3 * shares :]
    wgs_ref, wus_ref, wds_ref = refs[:3]
    part_ref, dy_ref, gws_ref, gwd_ref = refs[3:7]
    grads, (gwg_ref, gwu_ref) = refs[7:-2], refs[-2:]

    @pl.when(pl.program_id(0) == 0)
    def _():
        for ref in (gwg_ref, gwu_ref, gwd_ref):
            ref[...] = jnp.zeros_like(ref)

    tall, short = unit * tokens, unit * capacity
    count = x_ref.shape[0] // tall
    for j in range(count):
        inside = slice(j * tall, (j + 1) * tall)
        taken = slice(j * short, (j + 1) * short)
        pick = choose((short, tall), 0, row_ref[:, inside])
        dy_ref[taken, :] = (dot(pick, d_ref[inside, :]) * prob_ref[taken, :]).astype(bf16)
    total = 0.0
    for s in range(shares):
        wg_ref, wu_ref, wd_ref = weights[3 * s : 3 * s + 3]
        grad_hidden = dot_last(dy_ref[...], wd_ref[...])
        gate, up = (ref[...].astype(f32) for ref in kept[2 * s : 2 * s + 2])
        grad_gate, grad_up = silu_grads(gate, up, grad_hidden)
        grads[2 * s][...] = grad_gate
        grads[2 * s + 1][...] = grad_up
        total = total + dot(grad_gate, wg_ref[...]) + dot(grad_up, wu_ref[...])
    total = total.astype(bf16)
    grad_hidden = dot_last(d_ref[...], wds_ref[...])
    grad_gate, grad_up = silu_grads(
        gs_ref[...].astype(f32), us_ref[...].astype(f32), grad_hidden
    )
    gwg_ref[...] += dot_first(grad_gate, x_ref[...])
    gwu_ref[...] += dot_first(grad_up, x_ref[...])
    gwd_ref[...] += dot_first(hs_ref[...], d_ref[...])
    for j in range(count):
        inside = slice(j * tall, (j + 1) * tall)
        put = choose((tall, short), 1, col_ref[inside, :])
        part_ref[inside, :] = (
            dot(put, total[j * short : (j + 1) * short, :])
            + dot_last(grad_gate[inside, :], wgs_ref[...])
            + dot_last(grad_up[inside, :], wus_ref[...])
        ).astype(bf16)

    @pl.when(pl.program_id(0) == pl.num_programs(0) - 1)
    def _():
        width = gwg_ref.shape[0]
        gws_ref[:, :width] = gwg_ref[...].T.astype(bf16)
        gws_ref[:, width:] = gwu_ref[...].T.astype(bf16)


def experts_back(d, x, place_row, place_col, prob, saved, kept, weights, shared, capacity, tokens):
    length = x.shape[0]
    unit, tall, short, steps = expert_sizes(capacity, tokens, length)
    shares = len(weights) // 3
    half = weights[0].shape[0]
    width = shared[2].shape[0]
    wide = [fixed((half, D))] * (3 * shares)
    return pl.pallas_call(
        functools.partial(experts_back_kernel, shares, unit, capacity, tokens),
        name="experts_back",
        grid=(steps,),
        out_shape=[
            jax.ShapeDtypeStruct((length, D), bf16),
            jax.ShapeDtypeStruct((steps * short, D), bf16),
        ]
        + [jax.ShapeDtypeStruct((D, 2 * width), bf16), jax.ShapeDtypeStruct((width, D), f32)]
        + [jax.ShapeDtypeStruct((steps * short, half), bf16)] * (2 * shares),
        in_specs=[
            by_rows(tall, D),
            by_rows(tall, D),
            pl.BlockSpec((1, tall), lambda i: (0, i)),
            by_rows(tall, 1),
            by_rows(short, 1),
        ]
        + [by_rows(tall, width)] * 3
        + [by_rows(short, half)] * (2 * shares)
        + wide
        + [fixed((D, width)), second((D, width)), fixed((width, D))],
        out_specs=[by_rows(tall, D), by_rows(short, D)]
        + [fixed((D, 2 * width)), fixed((width, D))]
        + [by_rows(short, half)] * (2 * shares),
        scratch_shapes=[pltpu.VMEM((width, D), f32)] * 2,
        compiler_params=pltpu.CompilerParams(vmem_limit_bytes=60 << 20),
        cost_estimate=pl.CostEstimate(
            flops=6 * D * (steps * short * half * shares + 2 * length * width),
            bytes_accessed=50 << 20,
            transcendentals=0,
        ),
    )(d, x, place_row, place_col, prob, *saved, *kept, *weights, *shared)


def shift_fsdp(x, groups, by):
    return lax.ppermute(x, "fsdp", [(i, (i + by) % groups) for i in range(groups)])


def gather_fsdp(x, groups):
    if groups != 2:
        return lax.all_gather(x, "fsdp", axis=0)
    other = shift_fsdp(x, groups, 1)
    mine_first = lax.axis_index("fsdp") == 0
    return jnp.stack([jnp.where(mine_first, x, other), jnp.where(mine_first, other, x)])


def scatter_fsdp(x, groups):
    if groups != 2:
        return lax.psum_scatter(x.astype(bf16), "fsdp", scatter_dimension=0).astype(f32)
    me = lax.axis_index("fsdp")
    away = lax.dynamic_index_in_dim(x, 1 - me, 0, keepdims=False).astype(bf16)
    mine = lax.dynamic_index_in_dim(x, me, 0, keepdims=False).astype(f32)
    return mine + shift_fsdp(away, groups, 1).astype(f32)


def shards(
    hidden_in,
    teacher,
    doc_starts,
    routes,
    gate_logits,
    input_gain,
    query_weight,
    latent_weight,
    latent_gain,
    expand_weight,
    output_weight,
    mixer_gain,
    shared_gate,
    shared_up,
    shared_down,
    expert_gate,
    expert_up,
    expert_down,
):
    cycle = lax.axis_size("ctx")
    groups = lax.axis_size("fsdp")
    bits = cycle.bit_length() - 1
    tokens = hidden_in.shape[1]
    length = tokens * cycle
    capacity = min(tokens, 3 * tokens * TOPK // (2 * cycle))
    scale = (DN + DR) ** (-0.5)
    copies = max(1, cycle // H)
    ctx_index = lax.axis_index("ctx")
    copy_index = ctx_index % copies
    slab = query_weight.shape[0]
    slab_latent = expand_weight.shape[0]

    def pieces(weight):
        rows, width = weight.shape
        return jnp.transpose(weight.reshape(rows, cycle, width // cycle), (1, 0, 2))

    def padded(item, width):
        return jnp.pad(item, ((0, 0), (0, 0), (0, width - item.shape[2])))

    def exchange(packed):
        return lax.all_to_all(packed, "ctx", split_axis=0, concat_axis=0, tiled=True)

    def same_head(part, axis):
        if copies == 1:
            return part
        teams = [[i * copies + j for j in range(copies)] for i in range(H)]
        return lax.all_gather(part, "ctx", axis=axis, tiled=True, axis_index_groups=teams)

    def own_part(full, axis=1):
        if copies == 1:
            return full
        width = full.shape[axis] // copies
        return lax.dynamic_slice_in_dim(full, copy_index * width, width, axis)

    def swap(pair):
        half = pair.shape[1] // 2
        return jnp.concatenate([-pair[:, half:], pair[:, :half]], axis=1)

    def all_rows(item):
        both = jnp.transpose(gather_fsdp(item, groups), (1, 0, 2, 3))
        return both.reshape(-1, item.shape[2])

    fast = copies == 1 and groups == 2 and cycle * groups * slab == D and slab == 64
    part_q, part_e = H * (DN + DR) // cycle, H * (DN + DV) // cycle
    part_s = shared_gate.shape[1] // cycle
    shared_width = -(-part_s // 128) * 128

    probs = jax.nn.softmax(gate_logits[0], axis=-1)
    chosen = routes[0][:, :, None] == jnp.arange(cycle, dtype=jnp.int32)[None, None, :]
    dense_probs = jnp.sum(jnp.where(chosen, probs[:, :, None], 0.0), axis=1).T
    high = lax.reduce_precision(dense_probs, 8, 7)
    dense_probs = jnp.concatenate([high, dense_probs - high], axis=1).astype(bf16)
    prob_width = 2 * tokens // slab
    dense_probs = dense_probs.reshape(cycle, slab, prob_width)
    expand_pieces = pieces(expand_weight)
    if fast:
        quarter = part_e // 4
        expand_pieces = jnp.concatenate(
            [expand_pieces[:, :, q * quarter : (q + 1) * quarter] for q in range(4)], axis=1
        )
    else:
        expand_pieces = expand_pieces.reshape(cycle, slab, -1)
    block_q = -(-(part_q + expand_pieces.shape[2]) // 128) * 128
    block_s = -(-(part_s + prob_width) // 128) * 128
    packed = padded(jnp.concatenate([pieces(query_weight), expand_pieces], axis=2), block_q)
    packed = exchange(packed)
    packed_s = jnp.concatenate(
        [
            padded(jnp.concatenate([pieces(shared_gate), dense_probs], axis=2), block_s),
            padded(pieces(shared_up), block_s),
        ],
        axis=2,
    )
    narrow = jnp.concatenate(
        [
            latent_weight,
            input_gain[:, None],
            mixer_gain[:, None],
            jnp.concatenate([latent_gain, jnp.zeros((slab - slab_latent,), bf16)])[:, None],
            jnp.zeros((slab, -(KVR + DR + 3) % 128), bf16),
        ],
        axis=1,
    )
    w_down_s = gather_fsdp(shared_down, groups).reshape(-1, D)
    w_down_s = jnp.pad(w_down_s, ((0, shared_width - w_down_s.shape[0]), (0, 0)))
    w_output = gather_fsdp(output_weight, groups).reshape(-1, D)
    if copies > 1:
        rows_o = w_output.shape[0]
        own_output = lax.dynamic_update_slice_in_dim(
            jnp.zeros((DV, D), bf16), w_output, copy_index * rows_o, 0
        )
        w_output = same_head(w_output, 0)
    else:
        own_output = w_output
    weights = [expert_gate[0].T, expert_up[0].T, expert_down[0]]
    for r in range(1, groups):
        weights += [shift_fsdp(item, groups, r) for item in weights[:3]]
    starts = doc_starts[0]
    positions = jnp.arange(length, dtype=jnp.int32)
    inside = starts[None, :] <= positions[:, None]
    first_pos = jnp.max(jnp.where(inside, starts[None, :], 0), axis=1)
    cosine, sine = rope_tables(positions - first_pos)
    cosine = jnp.tile(cosine, (1, 4))
    sine = jnp.tile(sine, (1, 4))

    all_hidden, narrow = gather_ctx([hidden_in[0], narrow], bits, 1)
    packed_s, _ = lax.optimization_barrier((packed_s, all_hidden))
    packed_s = exchange(packed_s)
    my_probs = packed_s[:, :, part_s : part_s + prob_width]
    my_probs = my_probs.reshape(cycle, 2, tokens).astype(f32)
    my_probs = my_probs[:, 0] + my_probs[:, 1]
    if fast:
        w_cat, w_expand, gains = assemble(
            packed, shift_fsdp(packed, groups, 1), narrow, shift_fsdp(narrow, groups, 1)
        )
        gain_one, gain_two = gains[0], gains[1]
        gain_latent = gains[2].reshape(-1, slab)[:, :slab_latent].reshape(-1)
    else:
        narrow, packed = all_rows(narrow), all_rows(packed)
        gain_one = narrow[:, KVR + DR].astype(f32)
        gain_two = narrow[:, KVR + DR + 1].astype(f32)
        gain_latent = narrow[:, KVR + DR + 2].reshape(-1, slab)[:, :slab_latent]
        gain_latent = gain_latent.reshape(-1).astype(f32)
        w_query = same_head(packed[:, :part_q], 1)
        w_expand = packed[:, part_q : part_q + expand_pieces.shape[2]].reshape(KVR, part_e)
        w_expand = same_head(w_expand, 1)
        rope_k = narrow[:, KVR : KVR + DR]
        w_cat = jnp.concatenate(
            [w_query, rope_k, swap(w_query[:, DN:]), swap(rope_k), narrow[:, :KVR]], axis=1
        )

    w_both_s = all_rows(packed_s)

    residual = hidden_in[0].astype(f32)
    act_one, queries, keys, values, latent, latent_raw = project(
        all_hidden.reshape(length, D), gain_one, w_cat, gain_latent, w_expand, cosine, sine, scale
    )
    attended, log_total, partial = attend(
        queries, keys, values, first_pos[:, None], own_output
    )
    (mixing,) = scatter_ctx([partial.reshape(cycle, tokens, D)], bits, 3)
    mixed = residual + mixing

    normed_two, factor_two = norm_forward(mixed, gain_two)
    (all_act,) = gather_ctx([normed_two.astype(bf16)], bits, 2)
    all_act = all_act.reshape(length, D)
    used = my_probs > 0.0
    place = jnp.cumsum(used.astype(jnp.int32), axis=1) - 1
    slots = jnp.arange(capacity, dtype=jnp.int32)
    select = (place[:, None, :] == slots[None, :, None]) & used[:, None, :]
    slot_probs = jnp.sum(jnp.where(select, my_probs[:, None, :], 0.0), axis=-1).reshape(-1, 1)
    unit = expert_sizes(capacity, tokens, length)[0]
    turn = jnp.arange(cycle, dtype=jnp.int32)[:, None] % unit
    place = jnp.where(used, place + capacity * turn, -1).reshape(-1)
    routing = (place[None, :], place[:, None], slot_probs)
    shared = [w_both_s, w_both_s, w_down_s]
    partial, rows, gate_s, up_s, hidden_s, *kept = experts(
        all_act, *routing, weights, shared, capacity, tokens
    )
    (routed,) = scatter_ctx([partial.reshape(cycle, tokens, D)], bits, 3)
    result = mixed + routed
    diff = result - teacher[0].astype(f32)
    share = jnp.sum(gather_fsdp(0.5 * jnp.sum(diff * diff, keepdims=True), groups))

    (all_diff,) = gather_ctx([diff.astype(bf16)], bits, 2)
    gates = [item for s in range(groups) for item in kept[3 * s : 3 * s + 2]]
    partial, grad_rows, grad_shared, grad_w_down, *grads = experts_back(
        all_diff.reshape(length, D),
        all_act,
        *routing,
        [gate_s, up_s, hidden_s],
        gates,
        weights,
        shared,
        capacity,
        tokens,
    )
    (grad_act_two,) = scatter_ctx([partial.reshape(cycle, tokens, D)], bits, 3)
    grad_w_down = scatter_fsdp(grad_w_down[:part_s].reshape(groups, -1, D), groups)

    grad_gain_two = jnp.sum(grad_act_two * mixed * factor_two, axis=0)
    grad_mixed = diff + norm_back_rows(mixed, factor_two, gain_two, grad_act_two)
    lefts = []
    for r in range(groups):
        lefts += [grads[2 * r], grads[2 * r + 1], kept[3 * r + 2]]
    all_mixed, *expert_grads = gather_multiply(
        grad_mixed.astype(bf16), rows, grad_rows, lefts, bits, 5
    )
    def by_owner(grad):
        cut = jnp.transpose(grad.reshape(cycle, groups, slab, -1), (1, 0, 2, 3))
        return scatter_fsdp(cut, groups).astype(bf16)

    grad_shared, _ = lax.optimization_barrier((grad_shared, all_mixed))
    grad_shared = by_owner(grad_shared)
    high = lax.reduce_precision(share, 8, 7)
    mid = lax.reduce_precision(share - high, 8, 7)
    loss_parts = jnp.stack([high, mid, share - high - mid]).astype(bf16)
    spot = jnp.arange(grad_shared.shape[2], dtype=jnp.int32) - part_s
    loss_row = sum(jnp.where(spot == i, loss_parts[i], bf16(0)) for i in range(3))
    grad_shared = jnp.where(((spot >= 0) & (spot < 3))[None, None, :], loss_row, grad_shared)
    packed_s = exchange(grad_shared)
    loss_parts = packed_s[:, 0, part_s : part_s + 3].astype(f32)
    loss_value = jnp.sum(loss_parts) / (length * groups * D)
    grad_query, grad_keys, grad_values, grad_w_output = attend_back(
        queries,
        keys,
        values,
        all_mixed.reshape(length, D),
        attended,
        w_output,
        first_pos[None, :],
        log_total.reshape(1, length),
    )
    grad_query, packed_s = lax.optimization_barrier((grad_query, packed_s))
    grad_w_output = own_part(grad_w_output, 0).reshape(groups, slab, D)
    grad_w_output = scatter_fsdp(grad_w_output, groups)
    lanes = jnp.arange(WIDE, dtype=jnp.int32)
    keep_q = (lanes // ((DN + DR) // copies) == copy_index).astype(f32)[None, :]
    keep_e = (lanes // ((DN + DV) // copies) == copy_index).astype(f32)[None, :]
    partial, grad_w_cat, grad_w_expand = project_back(
        grad_query,
        grad_keys,
        grad_values,
        latent_raw,
        latent,
        act_one,
        cosine,
        sine,
        w_cat,
        w_expand,
        gain_latent,
        keep_q,
        keep_e,
        scale,
        copies,
    )
    if fast:
        first, slim = finish(
            grad_w_cat, grad_w_expand, w_cat, w_expand, grad_gain_two[:, None], cycle, slab
        )
    else:
        grad_gain_one = jnp.sum(grad_w_cat * w_cat.astype(f32), axis=1)
        grad_gain_latent = jnp.sum(grad_w_expand * w_expand.astype(f32), axis=1)
        turned = grad_w_cat[:, 2 * DN : 3 * DN]
        grad_ropes = grad_w_cat[:, DN : 2 * DN] - jnp.concatenate(
            [swap(turned[:, :DR]), swap(turned[:, DR:])], axis=1
        )
        grad_w_query = jnp.concatenate([grad_w_cat[:, :DN], grad_ropes[:, :DR]], axis=1)
        grad_we = own_part(grad_w_expand).reshape(cycle * groups, slab_latent, part_e)
        first = jnp.concatenate(
            [own_part(grad_w_query), grad_we.reshape(D, -1)], axis=1
        ).astype(bf16)
        spare = jnp.zeros((cycle * groups, slab - slab_latent), f32)
        grad_gain_latent = jnp.concatenate(
            [grad_gain_latent.reshape(cycle * groups, slab_latent), spare], axis=1
        ).reshape(-1)
        slim = jnp.concatenate(
            [
                grad_w_cat[:, 3 * DN :],
                grad_ropes[:, DR:],
                grad_gain_one[:, None],
                grad_gain_two[:, None],
                grad_gain_latent[:, None],
                jnp.zeros((D, -(KVR + DR + 3) % 128), f32),
            ],
            axis=1,
        ).astype(bf16)

    slim = by_owner(slim)
    first = padded(by_owner(first), block_q)
    packed = exchange(first)
    grad_act_one, grad_narrow = scatter_ctx(
        [partial.reshape(cycle, tokens, D), slim], bits, 4
    )
    if fast:
        own_grads = spread(
            packed,
            packed_s,
            [w.shape[1] for w in (query_weight, expand_weight, shared_gate, shared_up)],
        )
    else:
        spots = (
            (packed, 0, part_q, query_weight),
            (packed, part_q, expand_pieces.shape[2], expand_weight),
            (packed_s, 0, part_s, shared_gate),
            (packed_s, shared_width, part_s, shared_up),
        )
        own_grads = []
        for item, start, width, like in spots:
            item = item[:, :, start : start + width].reshape(cycle, like.shape[0], -1)
            own_grads.append(jnp.transpose(item, (1, 0, 2)).reshape(like.shape).astype(f32))
    _, factor_one = norm_forward(residual, gain_one)
    grad_input = grad_mixed + norm_back_rows(residual, factor_one, gain_one, grad_act_one)
    return (
        result.astype(bf16)[None],
        loss_value,
        grad_input[None],
        grad_narrow[:, KVR + DR] / input_gain.astype(f32),
        own_grads[0],
        grad_narrow[:, : KVR + DR],
        grad_narrow[:slab_latent, KVR + DR + 2] / latent_gain.astype(f32),
        own_grads[1],
        grad_w_output,
        grad_narrow[:, KVR + DR + 1],
        own_grads[2],
        own_grads[3],
        grad_w_down,
        expert_grads[0].astype(f32).T[None],
        expert_grads[1].astype(f32).T[None],
        expert_grads[2].astype(f32)[None],
    )


def solution(mesh):
    tokens = P("fsdp", "ctx", None)
    rows = P(("ctx", "fsdp"), None)
    gain = P(("ctx", "fsdp"))
    wide = P("ctx", None, "fsdp")
    deep = P("ctx", "fsdp", None)
    in_specs = (
        tokens,
        tokens,
        P("fsdp", None),
        tokens,
        tokens,
        gain,
        rows,
        rows,
        gain,
        rows,
        rows,
        gain,
        rows,
        rows,
        rows,
        wide,
        wide,
        deep,
    )
    out_specs = (
        tokens,
        P(),
        tokens,
        gain,
        rows,
        rows,
        gain,
        rows,
        rows,
        gain,
        rows,
        rows,
        rows,
        wide,
        wide,
        deep,
    )
    return jax.shard_map(shards, mesh=mesh, in_specs=in_specs, out_specs=out_specs, check_vma=False)
```

time: 1230 us -> 924 us (0.75)
  matrix products: 297 us -> 0 us
  Pallas kernels: 534 us -> 787 us
  blocking collectives: 78.8 us -> 0 us
  waiting for transfers between devices: 71 us -> 0.05 us
  other arithmetic: 94 us -> 48.8 us
  starting transfers between devices: 59.7 us -> 29.8 us
  local copies, waits for them, and re-layouts: 71.7 us -> 42.4 us
    dot_general x43 -> x0, matrix products: 297 us -> none  [the longest x13 106 us: dot_last(): lax.dot_general(left, right, (((1,), (1,)), ((), ())), preferred_element_...]
    pallas_call x6 -> x15, Pallas kernels: 510 us -> 754 us  [the longest x4 298 us: scatter_ctx(): pl.pallas_call(functools.partial(scatter_kernel, parts, bits, events, cou...]
    all_to_all x10 -> x4, waiting for transfers between devices: 69.9 us -> 0.01 us  [exchange(): lax.all_to_all(packed, 'ctx', split_axis=0, concat_axis=0, tiled=True)]
    all_gather x1 -> x0, blocking collectives: 39.9 us -> none  [shards(): all_probs = lax.all_gather(dense_probs, 'ctx', axis=0, tiled=True)]
    unnamed x1 -> x0, blocking collectives: 38.9 us -> none
    all_to_all x10 -> x4, starting transfers between devices: 56.3 us -> 25.9 us  [exchange(): lax.all_to_all(packed, 'ctx', split_axis=0, concat_axis=0, tiled=True)]
    convert_element_type x18 -> x6, other arithmetic: 38.8 us -> 10.7 us  [the longest x2 5.21 us: by_owner(): return scatter_fsdp(cut, groups).astype(bf16)]
    dot_general x2 -> x0, local copies, waits for them, and re-layouts: 25 us -> none  [dot_first(): lax.dot_general(left, right, (((0,), (0,)), ((), ())), preferred_element_...]
  transfers between devices with their start and end apart: 30 -> 18, of which waited for: 8 -> 0; matrix products, arithmetic and copies ran while one was open for 20% -> 8% of each run, Pallas kernels for 24% -> 44%
where the time goes in v2:
time: 924 us; the launch traced here: 917 us
  Pallas kernels  787 us (85%)
  other arithmetic  48.8 us (5%)
  local copies, waits for them, and re-layouts  42.4 us (5%)
  starting transfers between devices  29.8 us (3%)
    pallas_call x4, Pallas kernels, scatter_ctx(): pl.pallas_call(functools.partial(scatter_kernel, parts, bits, events, cou...  298 us
    pallas_call x3, Pallas kernels, gather_ctx(): pl.pallas_call(functools.partial(gather_kernel, parts, bits, events, coun...  218 us
    pallas_call x1, Pallas kernels, gather_multiply(): pl.pallas_call(functools.partial(gather_multiply_kernel, parts, bits, eve...  70.9 us
    pallas_call x1, Pallas kernels, experts_back(): pl.pallas_call(functools.partial(experts_back_kernel, shares, unit, capac...  61.2 us
    pallas_call x1, Pallas kernels, experts(): pl.pallas_call(functools.partial(experts_kernel, shares, unit, capacity,...  42.1 us
    pallas_call x1, Pallas kernels, project_back(): pl.pallas_call(functools.partial(project_back_kernel, scale, copies), nam...  31.5 us
    all_to_all x4, starting transfers between devices, exchange(): lax.all_to_all(packed, 'ctx', split_axis=0, concat_axis=0, tiled=True)  25.9 us
    pallas_call x1, Pallas kernels, attend_back(): pl.pallas_call(functools.partial(attend_back_kernel, block, count), name=...  19.4 us
  transfers between devices with their start and end apart: 18, of which 0 were waited for; matrix products, arithmetic and copies ran while one was open for 8% of the time, Pallas kernels for 44%

profile of v2, /device:TPU:0, one launch (start us, length us, event | category | flops | bytes accessed | tf_op | source)
XLA Modules:
  0.0 917.1 jit_solution(14151511986218566837)
XLA Ops:
  2.3 1.6 reshape.481
  5.1 8.3 all-to-all-start
  19.3 1.4 copy.168.sin_ref
  20.8 1.3 copy.167.cos_ref
  22.1 1.3 copy.169.first_ref
  24.2 79.0 %gather_ctx.3 = (bf16[16,128,2048]{2,1,0:T(8,128)(2,1)}, bf16[16,64,640]{2,1,0:T(8,128)(2,1)}) custom-call(bf16[128,2048]{1,0:T(8,128)(2,1)} %bitcast.171, bf16[64,640]{1,0:T(8,128)(2,1)} %concatenate.28.refs_1_), custom_call_target="tpu_custom_call" | custom-call | tf_op jit(solution)/shard_map/gather_ctx/pallas_call | solution.py:184
  107.0 5.8 all-to-all-start.1
  115.3 5.3 assemble.1
  120.7 1.8 copy-done
  122.7 2.0 copy-done.1
  127.2 17.4 %project.1 = (bf16[2048,2048]{1,0:T(8,128)(2,1)}, bf16[2048,256]{1,0:T(8,128)(2,1)S(1)}, bf16[2048,256]{1,0:T(8,128)(2,1)S(1)}, bf16[2048,128]{1,0:T(8,128)(2,1)...) custom-call(bf16[2048,2048]{1,0:T(8,128)(2,1)} %bitcast.220, f32[1,2048]{1,0:T(1,128)S(1)} %get-tuple-element.153.gain_ref, ...), custom_call_target="tpu_custom_call" | custom-call | flops 7516192768 | bytes 25165824 | tf_op jit(solution)/shard_map/project/pallas_call | solution.py:786
  147.4 1.3 copy-done.10
  148.8 13.6 %attend.1 = (f32[2048,128]{1,0:T(8,128)}, f32[2048,1]{1,0:T(8,128)}, bf16[2048,2048]{1,0:T(8,128)(2,1)}) custom-call(bf16[2048,256]{1,0:T(8,128)(2,1)} %copy-done.7, bf16[2048,256]{1,0:T(8,128)(2,1)} %copy-done.8, bf16[2048,128]{1,0:T(8,128)(2,1)} %copy-done.9, s32[2048,1]{1,0:T(8,128)} %copy.169.first_ref, bf16[128,2048]{1,0:T(8,128)(2,1)} %bitcast.195), custom_call_target="tpu_custom_call" | custom-call | flops 1342177280 | bytes 4096000 | tf_op jit(solution)/shard_map/attend/pallas_call | solution.py:501
  162.4 73.2 %scatter_ctx.4 = f32[128,2048]{1,0:T(8,128)} custom-call(bf16[16,128,2048]{2,1,0:T(8,128)(2,1)} %bitcast.167), custom_call_target="tpu_custom_call" | custom-call | tf_op jit(solution)/shard_map/scatter_ctx/pallas_call | solution.py:456
  235.6 1.5 multiply_reduce_fusion.3
  238.0 69.3 %gather_ctx.4 = bf16[16,128,2048]{2,1,0:T(8,128)(2,1)} custom-call(bf16[128,2048]{1,0:T(8,128)(2,1)} %multiply_convert_fusion.refs_0_), custom_call_target="tpu_custom_call" | custom-call | tf_op jit(solution)/shard_map/gather_ctx/pallas_call | solution.py:184
  313.5 1.7 select_bitcast_fusion.1
  315.4 1.5 copy.184
  316.9 42.1 %experts.1 = (bf16[2048,2048]{1,0:T(8,128)(2,1)}, bf16[1152,2048]{1,0:T(8,128)(2,1)}, bf16[2048,256]{1,0:T(8,128)(2,1)}, bf16[2048,256]{1,0:T(8,128)(2,1)}, bf16...) custom-call(bf16[2048,2048]{1,0:T(8,128)(2,1)} %bitcast.168, ...), custom_call_target="tpu_custom_call" | custom-call | flops 26373783552 | bytes 31457280 | tf_op jit(solution)/shard_map/experts/pallas_call | solution.py:965
  359.1 68.8 %scatter_ctx.5 = f32[128,2048]{1,0:T(8,128)} custom-call(bf16[16,128,2048]{2,1,0:T(8,128)(2,1)} %bitcast.166), custom_call_target="tpu_custom_call" | custom-call | tf_op jit(solution)/shard_map/scatter_ctx/pallas_call | solution.py:456
  427.9 2.2 fusion.38.refs_0_
  430.1 69.5 %gather_ctx.5 = bf16[16,128,2048]{2,1,0:T(8,128)(2,1)} custom-call(bf16[128,2048]{1,0:T(8,128)(2,1)} %fusion.38.refs_0_), custom_call_target="tpu_custom_call" | custom-call | tf_op jit(solution)/shard_map/gather_ctx/pallas_call | solution.py:184
  499.7 61.2 %experts_back.1 = (bf16[2048,2048]{1,0:T(8,128)(2,1)}, bf16[1152,2048]{1,0:T(8,128)(2,1)}, bf16[2048,512]{1,0:T(8,128)(2,1)}, f32[256,2048]{1,0:T(8,128)}, bf16[...) custom-call(bf16[2048,2048]{1,0:T(8,128)(2,1)} %bitcast.170, ...), custom_call_target="tpu_custom_call" | custom-call | flops 32816234496 | bytes 52428800 | tf_op jit(solution)/shard_map/experts_back/pallas_call | solution.py:1056
  560.9 67.7 %scatter_ctx.6 = f32[128,2048]{1,0:T(8,128)} custom-call(bf16[16,128,2048]{2,1,0:T(8,128)(2,1)} %bitcast.165), custom_call_target="tpu_custom_call" | custom-call | tf_op jit(solution)/shard_map/scatter_ctx/pallas_call | solution.py:456
  628.6 2.5 multiply_reduce_fusion
  631.1 1.8 fusion.39
  632.9 70.9 %gather_multiply.1 = (bf16[16,128,2048]{2,1,0:T(8,128)(2,1)}, bf16[704,2048]{1,0:T(8,128)(2,1)}, bf16[704,2048]{1,0:T(8,128)(2,1)}, bf16[704,2048]{1,0:T(8,128)(2,1)}) custom-call(bf16[128,2048]{1,0:T(8,128)(2,1)} %get-tuple-element.133.x_ref, bf16[1152,2048]{1,0:T(8,128)(2,1)} %get-tuple-element.92.rows_ref, bf16[1152,2048]{1,0:T(8,128)(2,1)} %get-tuple-element.93.dy_ref, ...), custom_call_target="tpu_custom_call" | custom-call | tf_op jit(solution)/shard_map/gather_multiply/pallas_call | solution.py:338
  705.5 2.2 reduce.5
  708.3 1.5 collective-permute-start.8
  709.8 1.3 copy.190.extra_ref
  711.2 1.5 slice.70
  718.2 2.6 fusion.12
  720.8 5.1 all-to-all-start.2
  725.8 19.4 %attend_back.1 = (f32[2048,256]{1,0:T(8,128)}, f32[2048,256]{1,0:T(8,128)}, f32[2048,128]{1,0:T(8,128)}, f32[128,2048]{1,0:T(8,128)}) custom-call(bf16[2048,256]{1,0:T(8,128)(2,1)} %copy-done.7, bf16[2048,256]{1,0:T(8,128)(2,1)} %copy-done.8, bf16[2048,128]{1,0:T(8,128)(2,1)} %copy-done.9, bf16[2048,2048]{1,0:T(8,128)(2,1)} %bitcast.219, ...), custom_call_target="tpu_custom_call" | custom-call | flops 3489660928 | bytes 8192000 | tf_op jit(solution)/shard_map/attend_back/pallas_call | solution.py:571
  746.6 3.7 bitcast_convert_fusion
  751.4 5.9 convert_bitcast_fusion
  757.3 31.5 %project_back.1 = (bf16[2048,2048]{1,0:T(8,128)(2,1)}, f32[2048,896]{1,0:T(8,128)}, f32[512,256]{1,0:T(8,128)}) custom-call(f32[2048,256]{1,0:T(8,128)} %get-tuple-element.105.dq_ref, f32[2048,256]{1,0:T(8,128)} %get-tuple-element.106.dk_ref, f32[2048,128]{1,0:T(8,128)} %get-tuple-element.107.dv_ref, f32[2048,512]{1,0:T(8,128)} %get-tuple-element.108.raw_ref, ...), custom_call_target="tpu_custom_call" | custom-call | flops 15032385536 | bytes 25165824 | tf_op jit(solution)/shard_map/project_back/pallas_call | solution.py:868
  788.8 8.3 finish.1
  797.1 2.7 dynamic-slice_bitcast_fusion
  802.0 1.9 bitcast_add_fusion
  805.3 2.0 fusion.15
  807.3 6.8 all-to-all-start.3
  814.1 3.2 fusion.refs_1_
  817.3 88.0 %scatter_ctx.7 = (f32[128,2048]{1,0:T(8,128)}, f32[64,640]{1,0:T(8,128)}) custom-call(bf16[16,128,2048]{2,1,0:T(8,128)(2,1)} %bitcast.164, bf16[16,64,640]{2,1,0:T(8,128)(2,1)} %fusion.refs_1_), custom_call_target="tpu_custom_call" | custom-call | tf_op jit(solution)/shard_map/scatter_ctx/pallas_call | solution.py:456
  906.3 1.5 slice_reduce_fusion
  908.3 1.5 fusion.5
  910.4 2.6 fusion.9
  913.0 1.9 spread.1
  (178 shorter events, 38.8 us)
Async XLA Ops:
  0.6 103.7 %collective-permute-start.2 = (bf16[64,2048]{1,0:T(8,128)(2,1)}, bf16[64,2048]{1,0:T(8,128)(2,1)S(1)}, u32[]{:S(2)}, u32[]{:S(2)}) collective-permute-start(bf16[64,2048]{1,0:T(8,128)(2,1)} %param.28), channel_id=1, source_target_pairs={{0,1},{1,0},{2,3},{3,2},{4,5},{5,4},{6,7},{7,6},{8,9},{9,8},{10,11... | collective-permute-start | bytes 786440 | tf_op jit(solution)/shard_map/ppermute | solution.py:1091
  1.2 111.6 %collective-permute-start.7 = (bf16[88,2048]{1,0:T(8,128)(2,1)}, bf16[88,2048]{1,0:T(8,128)(2,1)}, u32[]{:S(2)}, u32[]{:S(2)}) collective-permute-start(bf16[88,2048]{1,0:T(8,128)(2,1)} %param.32), channel_id=1, source_target_pairs={{0,1},{1,0},{2,3},{3,2},{4,5},{5,4},{6,7},{7,6},{8,9},{9,8},{10,11... | collective-permute-start | bytes 1081352 | tf_op jit(solution)/shard_map/ppermute | solution.py:1091
  2.3 11.8 %copy-start.29 = (f32[1,128,6]{1,0,2:T(1,128)S(1)}, f32[1,128,6]{1,0,2:T(1,128)}, u32[]{:S(2)}) copy-start(f32[1,128,6]{1,0,2:T(1,128)} %param.22) | copy-start | bytes 9220
  2.3 11.8 %copy-start.30 = (s32[1,128,6]{1,0,2:T(1,128)S(1)}, s32[1,128,6]{1,0,2:T(1,128)}, u32[]{:S(2)}) copy-start(s32[1,128,6]{1,0,2:T(1,128)} %param.21) | copy-start | bytes 9220
  2.3 11.9 %copy-start.31 = (s32[1,4]{1,0:T(1,128)S(1)}, s32[1,4]{1,0:T(1,128)}, u32[]{:S(2)}) copy-start(s32[1,4]{1,0:T(1,128)} %param.20) | copy-start | bytes 52
  3.9 11.4 %copy-start.22 = (bf16[64,2816]{1,0:T(8,128)(2,1)S(1)}, bf16[64,2816]{1,0:T(8,128)(2,1)}, u32[]{:S(2)}) copy-start(bf16[64,2816]{1,0:T(8,128)(2,1)} %param.30) | copy-start | bytes 1081348
  5.1 101.9 %all-to-all-start = ((bf16[16,64,256]{2,1,0:T(8,128)(2,1)}), bf16[16,64,256]{2,1,0:T(8,128)(2,1)S(1)}, u32[]{:S(2)}, u32[]{:S(2)}) async-start(bf16[16,64,256]{2,1,0:T(8,128)(2,1)} %maximum_maximum_fusion), calls=%async_computation | async-start | bytes 1048576 | tf_op jit(solution)/shard_map/all_to_all | solution.py:1152
  13.4 303.5 %collective-permute-start.3 = (bf16[704,2048]{1,0:T(8,128)(2,1)}, bf16[704,2048]{1,0:T(8,128)(2,1)}, u32[]{:S(2)}, u32[]{:S(2)}) collective-permute-start(bf16[704,2048]{1,0:T(8,128)(2,1)} %bitcast.221), channel_id=1, source_target_pairs={{0,1},{1,0},{2,3},{3,2},{4,5},{5,4},{6,7},{7,6},{8,9},{9,8},{10,11... | collective-permute-start | bytes 8650760 | tf_op jit(solution)/shard_map/ppermute | solution.py:1091
  13.5 303.5 %collective-permute-start.4 = (bf16[704,2048]{1,0:T(8,128)(2,1)}, bf16[704,2048]{1,0:T(8,128)(2,1)}, u32[]{:S(2)}, u32[]{:S(2)}) collective-permute-start(bf16[704,2048]{1,0:T(8,128)(2,1)} %bitcast.224), channel_id=1, source_target_pairs={{0,1},{1,0},{2,3},{3,2},{4,5},{5,4},{6,7},{7,6},{8,9},{9,8},{10,11... | collective-permute-start | bytes 8650760 | tf_op jit(solution)/shard_map/ppermute | solution.py:1091
  14.0 303.0 %collective-permute-start.5 = (bf16[704,2048]{1,0:T(8,128)(2,1)}, bf16[704,2048]{1,0:T(8,128)(2,1)}, u32[]{:S(2)}, u32[]{:S(2)}) collective-permute-start(bf16[704,2048]{1,0:T(8,128)(2,1)} %bitcast.227), channel_id=1, source_target_pairs={{0,1},{1,0},{2,3},{3,2},{4,5},{5,4},{6,7},{7,6},{8,9},{9,8},{10,11... | collective-permute-start | bytes 8650760 | tf_op jit(solution)/shard_map/ppermute | solution.py:1091
  14.3 7.8 copy-start.28
  14.6 3.1 copy-start.34
  14.6 3.2 copy-start.32
  14.6 3.3 copy-start.33
  14.7 3.4 copy-start.23
  20.7 2.8 copy-start.27
  103.2 1.8 copy-start.2
  105.0 8.0 copy-start.24
  105.0 10.3 %collective-permute-start.1 = (bf16[16,64,640]{2,1,0:T(8,128)(2,1)S(1)}, bf16[16,64,640]{2,1,0:T(8,128)(2,1)S(1)}, u32[]{:S(2)}, u32[]{:S(2)}) collective-permute-start(bf16[16,64,640]{2,1,0:T(8,128)(2,1)S(1)} %copy-done.2), channel_id=1, source_target_pairs={{0,1},{1,0},{2,3},{3,2},{4,5},{5,4},{6,7},{7,6},{8,9},{9,8},{10,11... | collective-permute-start | bytes 3932168 | tf_op jit(solution)/shard_map/ppermute | solution.py:1091
  107.0 200.3 %all-to-all-start.1 = ((bf16[16,64,512]{2,1,0:T(8,128)(2,1)}), bf16[16,64,512]{2,1,0:T(8,128)(2,1)}, u32[]{:S(2)}, u32[]{:S(2)}) async-start(bf16[16,64,512]{2,1,0:T(8,128)(2,1)} %fusion.11), calls=%async_computation.1 | async-start | bytes 2097152 | tf_op jit(solution)/shard_map/all_to_all | solution.py:1152
  112.8 2.5 collective-permute-start
  120.7 1.8 copy-start
  122.5 22.1 %copy-start.5 = (bf16[512,256]{1,0:T(8,128)(2,1)}, bf16[512,256]{1,0:T(8,128)(2,1)S(1)}, u32[]{:S(2)}) copy-start(bf16[512,256]{1,0:T(8,128)(2,1)S(1)} %get-tuple-element.76.we_ref) | copy-start | bytes 786436
  122.7 22.0 %copy-start.6 = (f32[1,512]{1,0:T(1,128)}, f32[1,512]{1,0:T(1,128)S(1)}, u32[]{:S(2)}) copy-start(f32[1,512]{1,0:T(1,128)S(1)} %broadcast_in_dim_reshape.2.gain_l_ref) | copy-start | bytes 6148
  122.7 2.0 copy-start.1
  147.4 1.3 copy-start.10
  162.4 73.2 %copy-start.13 = (bf16[1,128,2048]{2,1,0:T(8,128)(2,1)S(1)}, bf16[1,128,2048]{2,1,0:T(8,128)(2,1)}, u32[]{:S(2)}) copy-start(bf16[1,128,2048]{2,1,0:T(8,128)(2,1)} %param.18) | copy-start | bytes 1572868
  309.9 3.6 collective-permute-start.6
  359.1 68.8 %copy-start.14 = (bf16[1,128,2048]{2,1,0:T(8,128)(2,1)S(1)}, bf16[1,128,2048]{2,1,0:T(8,128)(2,1)}, u32[]{:S(2)}) copy-start(bf16[1,128,2048]{2,1,0:T(8,128)(2,1)} %param.19) | copy-start | bytes 1572868
  560.9 67.7 %copy-start.11 = (f32[128,2048]{1,0:T(8,128)S(1)}, f32[128,2048]{1,0:T(8,128)}, u32[]{:S(2)}) copy-start(f32[128,2048]{1,0:T(8,128)} %scatter_ctx.5) | copy-start | bytes 3145732
  628.6 2.5 copy-start.12
  632.9 70.9 %copy-start.19 = (bf16[2048,512]{1,0:T(8,128)(2,1)S(1)}, bf16[2048,512]{1,0:T(8,128)(2,1)}, u32[]{:S(2)}) copy-start(bf16[2048,512]{1,0:T(8,128)(2,1)} %get-tuple-element.101) | copy-start | bytes 6291460
  704.9 13.2 %collective-permute-start.9 = (bf16[16,64,512]{2,1,0:T(8,128)(2,1)}, bf16[16,64,512]{2,1,0:T(8,128)(2,1)S(1)}, u32[]{:S(2)}, u32[]{:S(2)}) collective-permute-start(bf16[16,64,512]{2,1,0:T(8,128)(2,1)} %dynamic-slice_bitcast_fusion.1), channel_id=1, source_target_pairs={{0,1},{1,0},{2,3},{3,2},{4,5},{5,4},{6,7},{7,6},{8,9},{9,8},{10,11... | collective-permute-start | bytes 3145736 | tf_op jit(solution)/shard_map/ppermute | solution.py:1091
  708.3 5.1 collective-permute-start.8
  713.4 88.6 %collective-permute-start.13 = (bf16[88,2048]{1,0:T(8,128)(2,1)}, bf16[88,2048]{1,0:T(8,128)(2,1)}, u32[]{:S(2)}, u32[]{:S(2)}) collective-permute-start(bf16[88,2048]{1,0:T(8,128)(2,1)} %fusion.18), channel_id=1, source_target_pairs={{0,1},{1,0},{2,3},{3,2},{4,5},{5,4},{6,7},{7,6},{8,9},{9,8},{10,11... | collective-permute-start | bytes 1081352 | tf_op jit(solution)/shard_map/ppermute | solution.py:1091
  720.8 36.5 %all-to-all-start.2 = ((bf16[16,64,512]{2,1,0:T(8,128)(2,1)}), bf16[16,64,512]{2,1,0:T(8,128)(2,1)S(1)}, u32[]{:S(2)}, u32[]{:S(2)}) async-start(bf16[16,64,512]{2,1,0:T(8,128)(2,1)} %fusion.12), calls=%async_computation.2 | async-start | bytes 2097152 | tf_op jit(solution)/shard_map/all_to_all | solution.py:1152
  725.8 20.7 %copy-start.16 = (bf16[704,2048]{1,0:T(8,128)(2,1)S(1)}, bf16[704,2048]{1,0:T(8,128)(2,1)}, u32[]{:S(2)}) copy-start(bf16[704,2048]{1,0:T(8,128)(2,1)} %get-tuple-element.127) | copy-start | bytes 8650756
  746.3 53.8 %collective-permute-start.12 = (bf16[64,2048]{1,0:T(8,128)(2,1)S(1)}, bf16[64,2048]{1,0:T(8,128)(2,1)S(1)}, u32[]{:S(2)}, u32[]{:S(2)}) collective-permute-start(bf16[64,2048]{1,0:T(8,128)(2,1)S(1)} %fusion.19), channel_id=1, source_target_pairs={{0,1},{1,0},{2,3},{3,2},{4,5},{5,4},{6,7},{7,6},{8,9},{9,8},{10,11... | collective-permute-start | bytes 786440 | tf_op jit(solution)/shard_map/ppermute | solution.py:1091
  746.6 3.7 copy-start.17
  746.6 4.8 copy-start.18
  797.1 3.0 copy-start.21
  797.1 3.8 copy-start.20
  799.8 14.3 %collective-permute-start.10 = (bf16[16,64,640]{2,1,0:T(8,128)(2,1)}, bf16[16,64,640]{2,1,0:T(8,128)(2,1)}, u32[]{:S(2)}, u32[]{:S(2)}) collective-permute-start(bf16[16,64,640]{2,1,0:T(8,128)(2,1)} %dynamic-slice_bitcast_fusion), channel_id=1, source_target_pairs={{0,1},{1,0},{2,3},{3,2},{4,5},{5,4},{6,7},{7,6},{8,9},{9,8},{10,11... | collective-permute-start | bytes 3932168 | tf_op jit(solution)/shard_map/ppermute | solution.py:1091
  801.8 3.5 collective-permute-start.11
  807.3 105.7 %all-to-all-start.3 = ((bf16[16,64,256]{2,1,0:T(8,128)(2,1)}), bf16[16,64,256]{2,1,0:T(8,128)(2,1)S(1)}, u32[]{:S(2)}, u32[]{:S(2)}) async-start(bf16[16,64,256]{2,1,0:T(8,128)(2,1)} %fusion.15), calls=%async_computation.3 | async-start | bytes 1048576 | tf_op jit(solution)/shard_map/all_to_all | solution.py:1152
  817.3 90.5 %copy-start.35 = (bf16[16]{0:T(256)(128)(2,1)S(1)}, bf16[16]{0:T(256)(128)(2,1)}, u32[]{:S(2)}) copy-start(bf16[16]{0:T(256)(128)(2,1)} %param.26) | copy-start | bytes 100
  905.3 5.1 copy-start.15
  910.4 4.5 copy-start.25
  (6 other events, 6.0 us)

commit v3 on v2

--- a/solution.py
+++ b/solution.py
@@ -519,7 +519,7 @@
             pl.BlockSpec((block, 1), lambda i: (i, 0)),
             pl.BlockSpec((block, D), lambda i: (i, 0)),
         ),
-        compiler_params=pltpu.CompilerParams(vmem_limit_bytes=56 << 20),
+        compiler_params=pltpu.CompilerParams(vmem_limit_bytes=60 << 20),
         cost_estimate=pl.CostEstimate(
             flops=length * length * (DN + DR + DV),
             bytes_accessed=length * 2000,
@@ -589,7 +589,7 @@
             row(),
         ],
         out_specs=(part(WIDE), whole(length, WIDE), whole(length, DV), whole(DV, D)),
-        compiler_params=pltpu.CompilerParams(vmem_limit_bytes=56 << 20),
+        compiler_params=pltpu.CompilerParams(vmem_limit_bytes=60 << 20),
         cost_estimate=pl.CostEstimate(
             flops=length * length * (3 * (DN + DR) + 2 * DV),
             bytes_accessed=length * 4000,
@@ -650,7 +650,7 @@
             jax.ShapeDtypeStruct((8, D), f32),
         ),
         scratch_shapes=[pltpu.VMEM((D, DN), f32), pltpu.VMEM((KVR, DN + DV), f32)],
-        compiler_params=pltpu.CompilerParams(vmem_limit_bytes=40 << 20),
+        compiler_params=pltpu.CompilerParams(vmem_limit_bytes=60 << 20),
     )(mine, other, mine_n, other_n)
 
 
@@ -692,7 +692,7 @@
             jax.ShapeDtypeStruct((D, 256), bf16),
             jax.ShapeDtypeStruct((D, KVR + DN), bf16),
         ),
-        compiler_params=pltpu.CompilerParams(vmem_limit_bytes=56 << 20),
+        compiler_params=pltpu.CompilerParams(vmem_limit_bytes=60 << 20),
     )(grad_w, grad_we, w_cat, w_expand, extra)
 
 
@@ -742,7 +742,7 @@
             jax.ShapeDtypeStruct((slab, widths[2]), f32),
             jax.ShapeDtypeStruct((slab, widths[3]), f32),
         ),
-        compiler_params=pltpu.CompilerParams(vmem_limit_bytes=40 << 20),
+        compiler_params=pltpu.CompilerParams(vmem_limit_bytes=60 << 20),
     )(packed, packed_s)
 
 
@@ -812,7 +812,7 @@
             by_rows(block, KVR),
             by_rows(block, KVR),
         ),
-        compiler_params=pltpu.CompilerParams(vmem_limit_bytes=40 << 20),
+        compiler_params=pltpu.CompilerParams(vmem_limit_bytes=60 << 20),
         cost_estimate=pl.CostEstimate(
             flops=2 * length * D * width, bytes_accessed=length * D * 6, transcendentals=0
         ),
@@ -894,7 +894,7 @@
             pl.BlockSpec((D, width), lambda i: (0, 0)),
             pl.BlockSpec((KVR, DN + DV), lambda i: (0, 0)),
         ),
-        compiler_params=pltpu.CompilerParams(vmem_limit_bytes=56 << 20),
+        compiler_params=pltpu.CompilerParams(vmem_limit_bytes=60 << 20),
         cost_estimate=pl.CostEstimate(
             flops=4 * length * D * width, bytes_accessed=length * D * 6, transcendentals=0
         ),
@@ -904,187 +904,530 @@
     )
 
 
-def choose(shape, dim, place):
-    return (lax.broadcasted_iota(jnp.int32, shape, dim) == place).astype(f32).astype(bf16)
-
-
-def experts_kernel(shares, unit, capacity, tokens, *refs):
-    x_ref, row_ref, col_ref, prob_ref = refs[:4]
-    weights = refs[4 : 4 + 3 * shares]
-    wgs_ref, wus_ref, wds_ref = refs[4 + 3 * shares : 7 + 3 * shares]
-    outs = refs[7 + 3 * shares :]
-    part_ref, rows_ref, gs_ref, us_ref, hs_ref = outs[:5]
-    kept = outs[5:]
-    tall, short = unit * tokens, unit * capacity
-    count = x_ref.shape[0] // tall
-    for j in range(count):
-        inside = slice(j * tall, (j + 1) * tall)
-        pick = choose((short, tall), 0, row_ref[:, inside])
-        rows_ref[j * short : (j + 1) * short, :] = dot(pick, x_ref[inside, :]).astype(bf16)
-    rows = rows_ref[...]
-    total = 0.0
-    for s in range(shares):
-        wg_ref, wu_ref, wd_ref = weights[3 * s : 3 * s + 3]
-        gate = dot_last(rows, wg_ref[...])
-        up = dot_last(rows, wu_ref[...])
-        hidden = (gate * jax.nn.sigmoid(gate) * up).astype(bf16)
-        for ref, value in zip(kept[3 * s : 3 * s + 3], (gate, up, hidden)):
-            ref[...] = value.astype(bf16)
-        total = total + dot(hidden, wd_ref[...])
-    total = (total * prob_ref[...]).astype(bf16)
-    gate = dot(x_ref[...], wgs_ref[...])
-    up = dot(x_ref[...], wus_ref[...])
-    hidden = (gate * jax.nn.sigmoid(gate) * up).astype(bf16)
-    gs_ref[...] = gate.astype(bf16)
-    us_ref[...] = up.astype(bf16)
-    hs_ref[...] = hidden
-    for j in range(count):
-        inside = slice(j * tall, (j + 1) * tall)
-        put = choose((tall, short), 1, col_ref[inside, :])
-        part_ref[inside, :] = (
-            dot(put, total[j * short : (j + 1) * short, :])
-            + dot(hidden[inside, :], wds_ref[...])
-        ).astype(bf16)
-
-
-def expert_sizes(capacity, tokens, length):
+class Gather:
+    def __init__(self, parts, bits, events, x_ref, o_ref, send_sem, recv_sem, own_sem):
+        self.parts, self.bits, self.events = parts, bits, events
+        self.x_ref, self.o_ref = x_ref, o_ref
+        self.send_sem, self.recv_sem = send_sem, recv_sem
+        self.me = lax.axis_index("ctx")
+        self.own = pltpu.make_async_copy(x_ref, o_ref.at[self.me], own_sem)
+        self.seen = set()
+        self.started = []
+
+    def send(self, index):
+        _, _, p, slot, bit = self.events[index]
+        if slot:
+            self.arrived(p, slot)
+        _, start, size, _ = self.parts[p]
+        rows = pl.ds(start, size)
+        block = flip(self.me, slot)
+        item = pltpu.make_async_remote_copy(
+            src_ref=self.x_ref.at[rows] if slot == 0 else self.o_ref.at[block, rows],
+            dst_ref=self.o_ref.at[block, rows],
+            send_sem=self.send_sem.at[index],
+            recv_sem=self.recv_sem.at[p, slot ^ bit],
+            device_id={"ctx": flip(self.me, bit)},
+            device_id_type=MESH,
+        )
+        item.start()
+        self.started.append(item)
+
+    def arrived(self, p, slot):
+        if (p, slot) in self.seen:
+            return
+        self.seen.add((p, slot))
+        _, start, size, order = self.parts[p]
+        rows = pl.ds(start, size)
+        bit = [b for b in order if slot & b][-1]
+        pltpu.make_async_remote_copy(
+            src_ref=self.x_ref.at[rows],
+            dst_ref=self.o_ref.at[flip(self.me, slot), rows],
+            send_sem=self.send_sem.at[0],
+            recv_sem=self.recv_sem.at[p, slot],
+            device_id={"ctx": flip(self.me, bit)},
+            device_id_type=MESH,
+        ).wait_recv()
+
+    def block(self, slot):
+        if slot == 0:
+            return self.x_ref
+        for p in range(len(self.parts)):
+            self.arrived(p, slot)
+        return self.o_ref.at[flip(self.me, slot)]
+
+    def finish(self):
+        for slot in range(1, 1 << self.bits):
+            self.block(slot)
+        for item in self.started:
+            item.wait_send()
+        self.own.wait()
+
+
+def gather_order(parts, bits, events, span):
+    at = {}
+    for index, (_, _, p, slot, bit) in enumerate(events):
+        at[p, slot ^ bit] = span * (index + 1) / len(events)
+    whole = {0: 0.0}
+    for slot in range(1, 1 << bits):
+        whole[slot] = max(at[p, slot] for p in range(len(parts)))
+    return whole, at
+
+
+def gather_plan(parts, bits, events, span, size, pieces, cost):
+    whole, at = gather_order(parts, bits, events, span)
+    slots = sorted(whole, key=lambda slot: (whole[slot], slot))
+    groups = [slots[i : i + size] for i in range(0, len(slots), size)]
+    ready = [max(whole[slot] for slot in group) for group in groups]
+    work = [(g, k) for g in range(len(groups)) for k in range(pieces)]
+    plan, now, e, w = [], 0.0, 0, 0
+    while e < len(events) or w < len(work):
+        _, _, p, slot, _ = events[e] if e < len(events) else (0, 0, 0, 0, 0)
+        when = (at[p, slot] if slot else 0.0) if e < len(events) else math.inf
+        then = ready[work[w][0]] if w < len(work) else math.inf
+        if when <= now or when <= then:
+            plan.append(("send", e))
+            now = max(now, when) + 0.1
+            e += 1
+        else:
+            plan.append(("work", work[w]))
+            now = max(now, then) + cost / pieces
+            w += 1
+    return groups, plan
+
+
+def expert_sizes(capacity, tokens, cycle):
     unit = 1
     while unit * capacity % 16:
         unit *= 2
     blocks = max(4, unit)
-    return unit, blocks * tokens, blocks * capacity, length // (blocks * tokens)
-
-
-def experts(x, place_row, place_col, prob, weights, shared, capacity, tokens):
-    length = x.shape[0]
-    unit, tall, short, steps = expert_sizes(capacity, tokens, length)
+    return unit, blocks
+
+
+def pick_rows(me, slots, unit, capacity, row_ref):
+    tokens = row_ref.shape[2]
+    places = []
+    for q, slot in enumerate(slots):
+        place = row_ref[flip(me, slot)]
+        places.append(jnp.where(place >= 0, place + q * capacity, -1))
+    place = jnp.concatenate(places, axis=1)
+    shape = (unit * capacity, unit * tokens)
+    return lax.broadcasted_iota(jnp.int32, shape, 0) == place
+
+
+def as_bf16(mask):
+    return mask.astype(f32).astype(bf16)
+
+
+def experts_kernel(
+    groups, plan, parts, bits, events, shares, unit, capacity, x_ref, row_ref, prob_ref, *refs
+):
+    weights, both_ref, down_ref = refs[: 3 * shares], refs[3 * shares], refs[3 * shares + 1]
+    refs = refs[3 * shares + 2 :]
+    o_ref, part_out, rows_out, gs_out, us_out, hs_out = refs[:6]
+    kept_out, refs = refs[6 : 6 + 3 * shares], refs[6 + 3 * shares :]
+    w, wb, wd, xg, rows, part, shared, kept = refs[:8]
+    send_sem, recv_sem, own_sem, w_sem, x_sem, out_sem, part_sem = refs[8:]
+    me = lax.axis_index("ctx")
+    tokens = x_ref.shape[0]
+    size = len(groups[0])
+    tall, short = unit * tokens, unit * capacity
+    width = wd.shape[0]
+    gather = Gather(parts, bits, events, x_ref, o_ref, send_sem, recv_sem, own_sem)
+    gather.own.start()
+    loads = [pltpu.make_async_copy(weights[i], w.at[i], w_sem.at[i]) for i in range(3 * shares)]
+    loads.append(pltpu.make_async_copy(both_ref, wb, w_sem.at[3 * shares]))
+    loads.append(pltpu.make_async_copy(down_ref, wd, w_sem.at[3 * shares + 1]))
+    greet(bits)
+    ready = set()
+
+    def need(i):
+        if i not in ready:
+            loads[i].wait()
+            ready.add(i)
+        return w[i] if i < 3 * shares else (wb if i == 3 * shares else wd)
+
+    def outs(g):
+        span = pl.ds(g * size * capacity, size * capacity)
+        wide = pl.ds(g * size * tokens, size * tokens)
+        items = [pltpu.make_async_copy(rows, rows_out.at[span], out_sem.at[0])]
+        for i, ref in enumerate((gs_out, us_out, hs_out)):
+            items.append(pltpu.make_async_copy(shared.at[i], ref.at[wide], out_sem.at[1 + i]))
+        for i in range(3 * shares):
+            items.append(
+                pltpu.make_async_copy(kept.at[i], kept_out[i].at[span], out_sem.at[4 + i])
+            )
+        return items
+
+    def part_outs(g, first=0, count=size):
+        return [
+            pltpu.make_async_copy(
+                part.at[pl.ds(q * tokens, tokens)],
+                part_out.at[flip(me, groups[g][q])],
+                part_sem.at[q],
+            )
+            for q in range(first, first + count)
+        ]
+
+    state = {}
+
+    def begin(g):
+        copies = [
+            pltpu.make_async_copy(
+                gather.block(slot), xg.at[pl.ds(q * tokens, tokens)], x_sem.at[q]
+            )
+            for q, slot in enumerate(groups[g])
+        ]
+        for item in copies:
+            item.start()
+        if g:
+            for item in outs(g - 1):
+                item.wait()
+        picks, scales = [], []
+        for j in range(size // unit):
+            slots = groups[g][j * unit : (j + 1) * unit]
+            mask = pick_rows(me, slots, unit, capacity, row_ref)
+            prob = jnp.concatenate([prob_ref[flip(me, slot)] for slot in slots], axis=1)
+            scales.append(jnp.sum(jnp.where(mask, prob, 0.0), axis=1, keepdims=True))
+            picks.append(as_bf16(mask))
+        for item in copies:
+            item.wait()
+        for j, pick in enumerate(picks):
+            chosen = dot(pick, xg[j * tall : (j + 1) * tall, :]).astype(bf16)
+            rows[j * short : (j + 1) * short, :] = chosen
+        state.update(picks=picks, scale=jnp.concatenate(scales, axis=0), total=0.0)
+
+    def gate(s):
+        state["gate"] = dot_last(rows[...], need(3 * s))
+
+    def up(s):
+        gated, upper = state["gate"], dot_last(rows[...], need(3 * s + 1))
+        hidden = (gated * jax.nn.sigmoid(gated) * upper).astype(bf16)
+        for i, value in enumerate((gated, upper, hidden)):
+            kept[3 * s + i] = value.astype(bf16)
+
+    def down(s):
+        state["total"] = state["total"] + dot(kept[3 * s + 2], need(3 * s + 2))
+
+    def shared_hidden(g):
+        gated = dot(xg[...], need(3 * shares)[:, :width])
+        upper = dot(xg[...], need(3 * shares)[:, width:])
+        hidden = (gated * jax.nn.sigmoid(gated) * upper).astype(bf16)
+        for i, value in enumerate((gated, upper, hidden)):
+            shared[i] = value.astype(bf16)
+        state["rows"] = (state["total"] * state["scale"]).astype(bf16)
+        for item in outs(g):
+            item.start()
+        if g:
+            for item in part_outs(g - 1):
+                item.wait()
+
+    def combine(g, j):
+        inside = slice(j * tall, (j + 1) * tall)
+        part[inside, :] = (
+            dot_first(state["picks"][j], state["rows"][j * short : (j + 1) * short, :])
+            + dot(shared[2, inside, :], need(3 * shares + 1)[...])
+        ).astype(bf16)
+        for item in part_outs(g, j * unit, unit):
+            item.start()
+
+    def piece(g, k):
+        if k == 0:
+            begin(g)
+        elif k <= 3 * shares:
+            (gate, up, down)[(k - 1) % 3]((k - 1) // 3)
+        elif k == 3 * shares + 1:
+            shared_hidden(g)
+        else:
+            combine(g, k - 3 * shares - 2)
+
+    sent = 0
+    for kind, item in plan:
+        if kind == "send":
+            gather.send(item)
+            sent += 1
+            if sent == bits * len(parts):
+                for load in loads:
+                    load.start()
+        else:
+            piece(*item)
+    gather.finish()
+    for item in outs(len(groups) - 1) + part_outs(len(groups) - 1):
+        item.wait()
+
+
+def experts(x, place, prob, weights, shared, capacity, bits, collective):
+    tokens = x.shape[0]
+    cycle = 1 << bits
+    unit, size = expert_sizes(capacity, tokens, cycle)
+    parts = all_parts([x.shape], bits)
+    events = gather_events(parts, bits)
     shares = len(weights) // 3
     half = weights[0].shape[0]
-    width = shared[2].shape[0]
-    wide = [fixed((half, D))] * (3 * shares)
+    width = shared[1].shape[0]
+    pieces = 3 * shares + 2 + size // unit
+    groups, plan = gather_plan(parts, bits, events, 66.0, size, pieces, 10.5)
+    anywhere = pl.BlockSpec(memory_space=pl.ANY)
+    inside = pl.BlockSpec(memory_space=pltpu.VMEM)
     return pl.pallas_call(
-        functools.partial(experts_kernel, shares, unit, capacity, tokens),
+        functools.partial(
+            experts_kernel, groups, plan, parts, bits, events, shares, unit, capacity
+        ),
         name="experts",
-        grid=(steps,),
         out_shape=[
-            jax.ShapeDtypeStruct((length, D), bf16),
-            jax.ShapeDtypeStruct((steps * short, D), bf16),
+            jax.ShapeDtypeStruct((cycle, tokens, D), bf16),
+            jax.ShapeDtypeStruct((cycle, tokens, D), bf16),
+            jax.ShapeDtypeStruct((cycle * capacity, D), bf16),
         ]
-        + [jax.ShapeDtypeStruct((length, width), bf16)] * 3
-        + [jax.ShapeDtypeStruct((steps * short, half), bf16)] * (3 * shares),
-        in_specs=[
-            by_rows(tall, D),
-            pl.BlockSpec((1, tall), lambda i: (0, i)),
-            by_rows(tall, 1),
-            by_rows(short, 1),
+        + [jax.ShapeDtypeStruct((cycle * tokens, width), bf16)] * 3
+        + [jax.ShapeDtypeStruct((cycle * capacity, half), bf16)] * (3 * shares),
+        in_specs=[anywhere, inside, inside] + [anywhere] * (3 * shares + 2),
+        out_specs=[anywhere] * (6 + 3 * shares),
+        scratch_shapes=[
+            pltpu.VMEM((3 * shares, half, D), bf16),
+            pltpu.VMEM((D, 2 * width), bf16),
+            pltpu.VMEM((width, D), bf16),
+            pltpu.VMEM((size * tokens, D), bf16),
+            pltpu.VMEM((size * capacity, D), bf16),
+            pltpu.VMEM((size * tokens, D), bf16),
+            pltpu.VMEM((3, size * tokens, width), bf16),
+            pltpu.VMEM((3 * shares, size * capacity, half), bf16),
+            pltpu.SemaphoreType.DMA((len(events),)),
+            pltpu.SemaphoreType.DMA((len(parts), cycle)),
+            pltpu.SemaphoreType.DMA,
+            pltpu.SemaphoreType.DMA((3 * shares + 2,)),
+            pltpu.SemaphoreType.DMA((size,)),
+            pltpu.SemaphoreType.DMA((4 + 3 * shares,)),
+            pltpu.SemaphoreType.DMA((size,)),
+        ],
+        compiler_params=pltpu.CompilerParams(
+            collective_id=collective, has_side_effects=True, vmem_limit_bytes=60 << 20
+        ),
+    )(x, place, prob, *weights, *shared)
+
+
+def experts_back_kernel(
+    groups, plan, parts, bits, events, shares, unit, capacity, x_ref, act_ref, row_ref, prob_ref,
+    gs_in, us_in, hs_in, *refs,
+):
+    kept_in, refs = refs[: 2 * shares], refs[2 * shares :]
+    weights, both_ref, down_ref = refs[: 3 * shares], refs[3 * shares], refs[3 * shares + 1]
+    refs = refs[3 * shares + 2 :]
+    o_ref, part_out, dy_out = refs[:3]
+    grads_out, refs = refs[3 : 3 + 2 * shares], refs[3 + 2 * shares :]
+    gws_ref, gwd_ref = refs[:2]
+    w, wb, wd, dg, ag, dy, part, shared, kept, grads, gwg, gwu = refs[2:14]
+    send_sem, recv_sem, own_sem, w_sem, x_sem, a_sem, k_sem, out_sem, part_sem = refs[14:]
+    me = lax.axis_index("ctx")
+    tokens = x_ref.shape[0]
+    size = len(groups[0])
+    tall, short = unit * tokens, unit * capacity
+    width = wd.shape[0]
+    gather = Gather(parts, bits, events, x_ref, o_ref, send_sem, recv_sem, own_sem)
+    gather.own.start()
+    loads = [pltpu.make_async_copy(weights[i], w.at[i], w_sem.at[i]) for i in range(3 * shares)]
+    loads.append(pltpu.make_async_copy(both_ref, wb, w_sem.at[3 * shares]))
+    loads.append(pltpu.make_async_copy(down_ref, wd, w_sem.at[3 * shares + 1]))
+    greet(bits)
+    for ref in (gwg, gwu, gwd_ref):
+        ref[...] = jnp.zeros_like(ref)
+    ready = set()
+
+    def need(i):
+        if i not in ready:
+            loads[i].wait()
+            ready.add(i)
+        return w[i] if i < 3 * shares else (wb if i == 3 * shares else wd)
+
+    def old(g):
+        span = pl.ds(g * size * capacity, size * capacity)
+        wide = pl.ds(g * size * tokens, size * tokens)
+        items = [
+            pltpu.make_async_copy(
+                act_ref.at[flip(me, slot)], ag.at[pl.ds(q * tokens, tokens)], a_sem.at[q]
+            )
+            for q, slot in enumerate(groups[g])
         ]
-        + wide
-        + [fixed((D, width)), second((D, width)), fixed((width, D))],
-        out_specs=[by_rows(tall, D), by_rows(short, D)]
-        + [by_rows(tall, width)] * 3
-        + [by_rows(short, half)] * (3 * shares),
-        compiler_params=pltpu.CompilerParams(vmem_limit_bytes=58 << 20),
-        cost_estimate=pl.CostEstimate(
-            flops=6 * D * (steps * short * half * shares + length * width),
-            bytes_accessed=30 << 20,
-            transcendentals=0,
-        ),
-    )(x, place_row, place_col, prob, *weights, *shared)
-
-
-def experts_back_kernel(shares, unit, capacity, tokens, *refs):
-    d_ref, x_ref, row_ref, col_ref, prob_ref, gs_ref, us_ref, hs_ref = refs[:8]
-    refs = refs[8:]
-    kept, refs = refs[: 2 * shares], refs[2 * shares :]
-    weights, refs = refs[: 3 * shares], refs[3 * shares :]
-    wgs_ref, wus_ref, wds_ref = refs[:3]
-    part_ref, dy_ref, gws_ref, gwd_ref = refs[3:7]
-    grads, (gwg_ref, gwu_ref) = refs[7:-2], refs[-2:]
-
-    @pl.when(pl.program_id(0) == 0)
-    def _():
-        for ref in (gwg_ref, gwu_ref, gwd_ref):
-            ref[...] = jnp.zeros_like(ref)
-
-    tall, short = unit * tokens, unit * capacity
-    count = x_ref.shape[0] // tall
-    for j in range(count):
+        for i, ref in enumerate((gs_in, us_in, hs_in)):
+            items.append(pltpu.make_async_copy(ref.at[wide], shared.at[i], k_sem.at[i]))
+        for i in range(2 * shares):
+            items.append(pltpu.make_async_copy(kept_in[i].at[span], kept.at[i], k_sem.at[3 + i]))
+        return items
+
+    def outs(g):
+        span = pl.ds(g * size * capacity, size * capacity)
+        items = [pltpu.make_async_copy(dy, dy_out.at[span], out_sem.at[0])]
+        for i in range(2 * shares):
+            items.append(
+                pltpu.make_async_copy(grads.at[i], grads_out[i].at[span], out_sem.at[1 + i])
+            )
+        return items
+
+    def part_outs(g, first=0, count=size):
+        return [
+            pltpu.make_async_copy(
+                part.at[pl.ds(q * tokens, tokens)],
+                part_out.at[flip(me, groups[g][q])],
+                part_sem.at[q],
+            )
+            for q in range(first, first + count)
+        ]
+
+    state = {}
+
+    def begin(g):
+        copies = [
+            pltpu.make_async_copy(
+                gather.block(slot), dg.at[pl.ds(q * tokens, tokens)], x_sem.at[q]
+            )
+            for q, slot in enumerate(groups[g])
+        ]
+        for item in copies:
+            item.start()
+        if g:
+            for item in outs(g - 1):
+                item.wait()
+        picks, scales = [], []
+        for j in range(size // unit):
+            slots = groups[g][j * unit : (j + 1) * unit]
+            mask = pick_rows(me, slots, unit, capacity, row_ref)
+            prob = jnp.concatenate([prob_ref[flip(me, slot)] for slot in slots], axis=1)
+            scales.append(jnp.sum(jnp.where(mask, prob, 0.0), axis=1, keepdims=True))
+            picks.append(as_bf16(mask))
+        for item in copies:
+            item.wait()
+        for j, pick in enumerate(picks):
+            chosen = dot(pick, dg[j * tall : (j + 1) * tall, :]) * scales[j]
+            dy[j * short : (j + 1) * short, :] = chosen.astype(bf16)
+        for item in old(g):
+            item.wait()
+        state.update(picks=picks, total=0.0)
+
+    def hidden_back(s):
+        grad_hidden = dot_last(dy[...], need(3 * s + 2))
+        grad_gate, grad_up = silu_grads(
+            kept[2 * s].astype(f32), kept[2 * s + 1].astype(f32), grad_hidden
+        )
+        grads[2 * s] = grad_gate
+        grads[2 * s + 1] = grad_up
+
+    def rows_back(s, i):
+        state["total"] = state["total"] + dot(grads[2 * s + i], need(3 * s + i))
+
+    def shared_back(g):
+        for item in outs(g):
+            item.start()
+        grad_hidden = dot_last(dg[...], need(3 * shares + 1)[...])
+        grad_gate, grad_up = silu_grads(
+            shared[0].astype(f32), shared[1].astype(f32), grad_hidden
+        )
+        gwg[...] += dot_first(grad_gate, ag[...])
+        state.update(gate=grad_gate, up=grad_up, rows=state["total"].astype(bf16))
+
+    def shared_more(g):
+        gwu[...] += dot_first(state["up"], ag[...])
+        gwd_ref[...] += dot_first(shared[2], dg[...])
+        if g + 1 < len(groups):
+            for item in old(g + 1):
+                item.start()
+        if g:
+            for item in part_outs(g - 1):
+                item.wait()
+
+    def combine(g, j):
         inside = slice(j * tall, (j + 1) * tall)
-        taken = slice(j * short, (j + 1) * short)
-        pick = choose((short, tall), 0, row_ref[:, inside])
-        dy_ref[taken, :] = (dot(pick, d_ref[inside, :]) * prob_ref[taken, :]).astype(bf16)
-    total = 0.0
-    for s in range(shares):
-        wg_ref, wu_ref, wd_ref = weights[3 * s : 3 * s + 3]
-        grad_hidden = dot_last(dy_ref[...], wd_ref[...])
-        gate, up = (ref[...].astype(f32) for ref in kept[2 * s : 2 * s + 2])
-        grad_gate, grad_up = silu_grads(gate, up, grad_hidden)
-        grads[2 * s][...] = grad_gate
-        grads[2 * s + 1][...] = grad_up
-        total = total + dot(grad_gate, wg_ref[...]) + dot(grad_up, wu_ref[...])
-    total = total.astype(bf16)
-    grad_hidden = dot_last(d_ref[...], wds_ref[...])
-    grad_gate, grad_up = silu_grads(
-        gs_ref[...].astype(f32), us_ref[...].astype(f32), grad_hidden
-    )
-    gwg_ref[...] += dot_first(grad_gate, x_ref[...])
-    gwu_ref[...] += dot_first(grad_up, x_ref[...])
-    gwd_ref[...] += dot_first(hs_ref[...], d_ref[...])
-    for j in range(count):
-        inside = slice(j * tall, (j + 1) * tall)
-        put = choose((tall, short), 1, col_ref[inside, :])
-        part_ref[inside, :] = (
-            dot(put, total[j * short : (j + 1) * short, :])
-            + dot_last(grad_gate[inside, :], wgs_ref[...])
-            + dot_last(grad_up[inside, :], wus_ref[...])
+        both = need(3 * shares)
+        part[inside, :] = (
+            dot_first(state["picks"][j], state["rows"][j * short : (j + 1) * short, :])
+            + dot_last(state["gate"][inside, :], both[:, :width])
+            + dot_last(state["up"][inside, :], both[:, width:])
         ).astype(bf16)
-
-    @pl.when(pl.program_id(0) == pl.num_programs(0) - 1)
-    def _():
-        width = gwg_ref.shape[0]
-        gws_ref[:, :width] = gwg_ref[...].T.astype(bf16)
-        gws_ref[:, width:] = gwu_ref[...].T.astype(bf16)
-
-
-def experts_back(d, x, place_row, place_col, prob, saved, kept, weights, shared, capacity, tokens):
-    length = x.shape[0]
-    unit, tall, short, steps = expert_sizes(capacity, tokens, length)
+        for item in part_outs(g, j * unit, unit):
+            item.start()
+
+    def piece(g, k):
+        if k == 0:
+            begin(g)
+        elif k <= 3 * shares:
+            s, i = (k - 1) // 3, (k - 1) % 3
+            hidden_back(s) if i == 0 else rows_back(s, i - 1)
+        elif k == 3 * shares + 1:
+            shared_back(g)
+        elif k == 3 * shares + 2:
+            shared_more(g)
+        else:
+            combine(g, k - 3 * shares - 3)
+
+    sent = 0
+    for kind, item in plan:
+        if kind == "send":
+            gather.send(item)
+            sent += 1
+            if sent == bits * len(parts):
+                for load in loads + old(0):
+                    load.start()
+        else:
+            piece(*item)
+    gws_ref[:, :width] = gwg[...].T.astype(bf16)
+    gws_ref[:, width:] = gwu[...].T.astype(bf16)
+    gather.finish()
+    for item in outs(len(groups) - 1) + part_outs(len(groups) - 1):
+        item.wait()
+
+
+def experts_back(x, act, place, prob, saved, kept, weights, shared, capacity, bits, collective):
+    tokens = x.shape[0]
+    cycle = 1 << bits
+    unit, size = expert_sizes(capacity, tokens, cycle)
+    parts = all_parts([x.shape], bits)
+    events = gather_events(parts, bits)
     shares = len(weights) // 3
     half = weights[0].shape[0]
-    width = shared[2].shape[0]
-    wide = [fixed((half, D))] * (3 * shares)
+    width = shared[1].shape[0]
+    pieces = 3 * shares + 3 + size // unit
+    groups, plan = gather_plan(parts, bits, events, 66.0, size, pieces, 15.0)
+    anywhere = pl.BlockSpec(memory_space=pl.ANY)
+    inside = pl.BlockSpec(memory_space=pltpu.VMEM)
     return pl.pallas_call(
-        functools.partial(experts_back_kernel, shares, unit, capacity, tokens),
+        functools.partial(
+            experts_back_kernel, groups, plan, parts, bits, events, shares, unit, capacity
+        ),
         name="experts_back",
-        grid=(steps,),
         out_shape=[
-            jax.ShapeDtypeStruct((length, D), bf16),
-            jax.ShapeDtypeStruct((steps * short, D), bf16),
+            jax.ShapeDtypeStruct((cycle, tokens, D), bf16),
+            jax.ShapeDtypeStruct((cycle, tokens, D), bf16),
+            jax.ShapeDtypeStruct((cycle * capacity, D), bf16),
         ]
-        + [jax.ShapeDtypeStruct((D, 2 * width), bf16), jax.ShapeDtypeStruct((width, D), f32)]
-        + [jax.ShapeDtypeStruct((steps * short, half), bf16)] * (2 * shares),
-        in_specs=[
-            by_rows(tall, D),
-            by_rows(tall, D),
-            pl.BlockSpec((1, tall), lambda i: (0, i)),
-            by_rows(tall, 1),
-            by_rows(short, 1),
-        ]
-        + [by_rows(tall, width)] * 3
-        + [by_rows(short, half)] * (2 * shares)
-        + wide
-        + [fixed((D, width)), second((D, width)), fixed((width, D))],
-        out_specs=[by_rows(tall, D), by_rows(short, D)]
-        + [fixed((D, 2 * width)), fixed((width, D))]
-        + [by_rows(short, half)] * (2 * shares),
-        scratch_shapes=[pltpu.VMEM((width, D), f32)] * 2,
-        compiler_params=pltpu.CompilerParams(vmem_limit_bytes=60 << 20),
-        cost_estimate=pl.CostEstimate(
-            flops=6 * D * (steps * short * half * shares + 2 * length * width),
-            bytes_accessed=50 << 20,
-            transcendentals=0,
-        ),
-    )(d, x, place_row, place_col, prob, *saved, *kept, *weights, *shared)
+        + [jax.ShapeDtypeStruct((cycle * capacity, half), bf16)] * (2 * shares)
+        + [jax.ShapeDtypeStruct((D, 2 * width), bf16), jax.ShapeDtypeStruct((width, D), f32)],
+        in_specs=[anywhere, anywhere, inside, inside] + [anywhere] * (5 + 5 * shares),
+        out_specs=[anywhere] * (3 + 2 * shares) + [inside, inside],
+        scratch_shapes=[
+            pltpu.VMEM((3 * shares, half, D), bf16),
+            pltpu.VMEM((D, 2 * width), bf16),
+            pltpu.VMEM((width, D), bf16),
+            pltpu.VMEM((size * tokens, D), bf16),
+            pltpu.VMEM((size * tokens, D), bf16),
+            pltpu.VMEM((size * capacity, D), bf16),
+            pltpu.VMEM((size * tokens, D), bf16),
+            pltpu.VMEM((3, size * tokens, width), bf16),
+            pltpu.VMEM((2 * shares, size * capacity, half), bf16),
+            pltpu.VMEM((2 * shares, size * capacity, half), bf16),
+            pltpu.VMEM((width, D), f32),
+            pltpu.VMEM((width, D), f32),
+            pltpu.SemaphoreType.DMA((len(events),)),
+            pltpu.SemaphoreType.DMA((len(parts), cycle)),
+            pltpu.SemaphoreType.DMA,
+            pltpu.SemaphoreType.DMA((3 * shares + 2,)),
+            pltpu.SemaphoreType.DMA((size,)),
+            pltpu.SemaphoreType.DMA((size,)),
+            pltpu.SemaphoreType.DMA((3 + 2 * shares,)),
+            pltpu.SemaphoreType.DMA((1 + 2 * shares,)),
+            pltpu.SemaphoreType.DMA((size,)),
+        ],
+        compiler_params=pltpu.CompilerParams(
+            collective_id=collective, has_side_effects=True, vmem_limit_bytes=61 << 20
+        ),
+    )(x, act, place, prob, *saved, *kept, *weights, *shared)
 
 
 def shift_fsdp(x, groups, by):
@@ -1273,30 +1616,21 @@
     mixed = residual + mixing
 
     normed_two, factor_two = norm_forward(mixed, gain_two)
-    (all_act,) = gather_ctx([normed_two.astype(bf16)], bits, 2)
-    all_act = all_act.reshape(length, D)
     used = my_probs > 0.0
     place = jnp.cumsum(used.astype(jnp.int32), axis=1) - 1
-    slots = jnp.arange(capacity, dtype=jnp.int32)
-    select = (place[:, None, :] == slots[None, :, None]) & used[:, None, :]
-    slot_probs = jnp.sum(jnp.where(select, my_probs[:, None, :], 0.0), axis=-1).reshape(-1, 1)
-    unit = expert_sizes(capacity, tokens, length)[0]
-    turn = jnp.arange(cycle, dtype=jnp.int32)[:, None] % unit
-    place = jnp.where(used, place + capacity * turn, -1).reshape(-1)
-    routing = (place[None, :], place[:, None], slot_probs)
-    shared = [w_both_s, w_both_s, w_down_s]
-    partial, rows, gate_s, up_s, hidden_s, *kept = experts(
-        all_act, *routing, weights, shared, capacity, tokens
+    routing = (jnp.where(used, place, -1)[:, None, :], my_probs[:, None, :])
+    shared = [w_both_s, w_down_s]
+    all_act, partial, rows, gate_s, up_s, hidden_s, *kept = experts(
+        normed_two.astype(bf16), *routing, weights, shared, capacity, bits, 2
     )
-    (routed,) = scatter_ctx([partial.reshape(cycle, tokens, D)], bits, 3)
+    (routed,) = scatter_ctx([partial], bits, 3)
     result = mixed + routed
     diff = result - teacher[0].astype(f32)
     share = jnp.sum(gather_fsdp(0.5 * jnp.sum(diff * diff, keepdims=True), groups))
 
-    (all_diff,) = gather_ctx([diff.astype(bf16)], bits, 2)
     gates = [item for s in range(groups) for item in kept[3 * s : 3 * s + 2]]
-    partial, grad_rows, grad_shared, grad_w_down, *grads = experts_back(
-        all_diff.reshape(length, D),
+    _, partial, grad_rows, *grads, grad_shared, grad_w_down = experts_back(
+        diff.astype(bf16),
         all_act,
         *routing,
         [gate_s, up_s, hidden_s],
@@ -1304,9 +1638,10 @@
         weights,
         shared,
         capacity,
-        tokens,
+        bits,
+        6,
     )
-    (grad_act_two,) = scatter_ctx([partial.reshape(cycle, tokens, D)], bits, 3)
+    (grad_act_two,) = scatter_ctx([partial], bits, 3)
     grad_w_down = scatter_fsdp(grad_w_down[:part_s].reshape(groups, -1, D), groups)
 
     grad_gain_two = jnp.sum(grad_act_two * mixed * factor_two, axis=0)

time: 924 us -> 843 us (0.912)
  Pallas kernels: 787 us -> 716 us
  local copies, waits for them, and re-layouts: 42.4 us -> 31.1 us
    pallas_call x3 -> x1, Pallas kernels: 218 us -> 79 us  [gather_ctx(): pl.pallas_call(functools.partial(gather_kernel, parts, bits, events, coun...]
    pallas_call x2, Pallas kernels: 103 us -> 184 us  [the longest x1 98.8 us: experts_back(): pl.pallas_call(functools.partial(experts_back_kernel, groups, plan, parts...]
    pallas_call x4, Pallas kernels: 298 us -> 280 us  [scatter_ctx(): pl.pallas_call(functools.partial(scatter_kernel, parts, bits, events, cou...]
    unnamed x78 -> x66, local copies, waits for them, and re-layouts: 13.8 us -> 3.91 us
  transfers between devices with their start and end apart: 18 -> 18, of which waited for: 0 -> 1; matrix products, arithmetic and copies ran while one was open for 8% -> 8% of each run, Pallas kernels for 44% -> 41%
where the time goes in v3:
time: 843 us; the launch traced here: 834 us
  Pallas kernels  716 us (85%)
  other arithmetic  48.5 us (6%)
  local copies, waits for them, and re-layouts  31.1 us (4%)
  starting transfers between devices  29.9 us (4%)
  between operations  8.95 us (1%)
    pallas_call x4, Pallas kernels, scatter_ctx(): pl.pallas_call(functools.partial(scatter_kernel, parts, bits, events, cou...  280 us
    pallas_call x1, Pallas kernels, experts_back(): pl.pallas_call(functools.partial(experts_back_kernel, groups, plan, parts...  98.8 us
    pallas_call x1, Pallas kernels, experts(): pl.pallas_call(functools.partial(experts_kernel, groups, plan, parts, bit...  85.2 us
    pallas_call x1, Pallas kernels, gather_ctx(): pl.pallas_call(functools.partial(gather_kernel, parts, bits, events, coun...  79 us
    pallas_call x1, Pallas kernels, gather_multiply(): pl.pallas_call(functools.partial(gather_multiply_kernel, parts, bits, eve...  68.9 us
    pallas_call x1, Pallas kernels, project_back(): pl.pallas_call(functools.partial(project_back_kernel, scale, copies), nam...  31.6 us
    all_to_all x4, starting transfers between devices, exchange(): lax.all_to_all(packed, 'ctx', split_axis=0, concat_axis=0, tiled=True)  25.9 us
    pallas_call x1, Pallas kernels, attend_back(): pl.pallas_call(functools.partial(attend_back_kernel, block, count), name=...  19.3 us
  transfers between devices with their start and end apart: 18, of which 1 were waited for; matrix products, arithmetic and copies ran while one was open for 8% of the time, Pallas kernels for 41%

profile of v3, /device:TPU:0, one launch (start us, length us, event | category | flops | bytes accessed | tf_op | source)
XLA Modules:
  0.0 834.4 jit_solution(16074517604290245993)
XLA Ops:
  2.3 1.6 reshape.347
  5.1 8.4 %all-to-all-start = ((bf16[16,64,256]{2,1,0:T(8,128)(2,1)}), bf16[16,64,256]{2,1,0:T(8,128)(2,1)S(1)}, u32[]{:S(2)}, u32[]{:S(2)}) async-start(bf16[16,64,256]{2,1,0:T(8,128)(2,1)} %maximum_maximum_fusion), calls=%async_computation | async-start | bytes 1048576 | tf_op jit(solution)/shard_map/all_to_all | solution.py:1495
  19.3 1.3 copy.155.sin_ref
  20.7 1.3 copy.154.cos_ref
  22.0 1.4 copy.156.first_ref
  24.1 79.0 %gather_ctx.1 = (bf16[16,128,2048]{2,1,0:T(8,128)(2,1)}, bf16[16,64,640]{2,1,0:T(8,128)(2,1)}) custom-call(bf16[128,2048]{1,0:T(8,128)(2,1)} %bitcast.146, bf16[64,640]{1,0:T(8,128)(2,1)} %concatenate.28.refs_1_), custom_call_target="tpu_custom_call" | custom-call | tf_op jit(solution)/shard_map/gather_ctx/pallas_call | solution.py:184
  103.3 1.1 fusion.11
  106.3 5.4 all-to-all-start.1
  113.2 1.1 pad.15.refs_7_.refs_11_
  114.2 1.0 copy-done.11
  116.1 9.0 %assemble.1 = (bf16[2048,896]{1,0:T(8,128)(2,1)}, bf16[512,256]{1,0:T(8,128)(2,1)}, f32[8,2048]{1,0:T(8,128)}) custom-call(bf16[16,64,256]{2,1,0:T(8,128)(2,1)} %copy-done.8, bf16[16,64,256]{2,1,0:T(8,128)(2,1)} %copy-done.14, bf16[16,64,640]{2,1,0:T(8,128)(2,1)} %get-tuple-element.74.mine_n_ref, bf16[16,64,640]{2,1,0:T(8,128)(2,1)} %copy-done.11), custom_call_target="tpu_custom_call" | custom-call | tf_op jit(solution)/shard_map/assemble/pallas_call | solution.py:644
  125.1 1.6 fusion.39
  127.4 18.6 %project.1 = (bf16[2048,2048]{1,0:T(8,128)(2,1)}, bf16[2048,256]{1,0:T(8,128)(2,1)}, bf16[2048,256]{1,0:T(8,128)(2,1)}, bf16[2048,128]{1,0:T(8,128)(2,1)}, bf16[...) custom-call(bf16[2048,2048]{1,0:T(8,128)(2,1)} %bitcast.188, f32[1,2048]{1,0:T(1,128)} %get-tuple-element.157.gain_ref, ...), custom_call_target="tpu_custom_call" | custom-call | flops 7516192768 | bytes 25165824 | tf_op jit(solution)/shard_map/project/pallas_call | solution.py:786
  146.0 13.6 %attend.1 = (f32[2048,128]{1,0:T(8,128)}, f32[2048,1]{1,0:T(8,128)}, bf16[2048,2048]{1,0:T(8,128)(2,1)}) custom-call(bf16[2048,256]{1,0:T(8,128)(2,1)} %get-tuple-element.78.q_ref, bf16[2048,256]{1,0:T(8,128)(2,1)} %get-tuple-element.79.k_ref, bf16[2048,128]{1,0:T(8,128)(2,1)} %get-tuple-element.80.v_ref, s32[2048,1]{1,0:T(8,128)} %copy.156.first_ref, ...), custom_call_target="tpu_custom_call" | custom-call | flops 1342177280 | bytes 4096000 | tf_op jit(solution)/shard_map/attend/pallas_call | solution.py:501
  159.7 73.2 %scatter_ctx.4 = f32[128,2048]{1,0:T(8,128)} custom-call(bf16[16,128,2048]{2,1,0:T(8,128)(2,1)} %bitcast.145), custom_call_target="tpu_custom_call" | custom-call | tf_op jit(solution)/shard_map/scatter_ctx/pallas_call | solution.py:456
  232.9 1.5 multiply_reduce_fusion.3
  237.3 1.4 select_bitcast_fusion.1
  238.9 1.5 copy.169
  240.5 85.2 %experts.1 = (bf16[16,128,2048]{2,1,0:T(8,128)(2,1)}, bf16[16,128,2048]{2,1,0:T(8,128)(2,1)}, bf16[1152,2048]{1,0:T(8,128)(2,1)}, bf16[2048,256]{1,0:T(8,128)(2,...) custom-call(bf16[128,2048]{1,0:T(8,128)(2,1)} %multiply_convert_fusi, ...), custom_call_target="tpu_custom_call" | custom-call | tf_op jit(solution)/shard_map/experts/pallas_call | solution.py:1171
  325.7 63.7 %scatter_ctx.5 = f32[128,2048]{1,0:T(8,128)} custom-call(bf16[16,128,2048]{2,1,0:T(8,128)(2,1)} %get-tuple-element.83.refs_0_), custom_call_target="tpu_custom_call" | custom-call | tf_op jit(solution)/shard_map/scatter_ctx/pallas_call | solution.py:456
  389.4 2.2 fusion.35.x_ref
  391.6 98.8 %experts_back.1 = (bf16[16,128,2048]{2,1,0:T(8,128)(2,1)}, bf16[16,128,2048]{2,1,0:T(8,128)(2,1)}, bf16[1152,2048]{1,0:T(8,128)(2,1)}, bf16[1152,704]{1,0:T(8,12...) custom-call(bf16[128,2048]{1,0:T(8,128)(2,1)} %fusion.35.x_ref, ...), custom_call_target="tpu_custom_call" | custom-call | tf_op jit(solution)/shard_map/experts_back/pallas_call | solution.py:1390
  490.4 55.4 %scatter_ctx.6 = f32[128,2048]{1,0:T(8,128)} custom-call(bf16[16,128,2048]{2,1,0:T(8,128)(2,1)} %get-tuple-element.93.refs_0_), custom_call_target="tpu_custom_call" | custom-call | tf_op jit(solution)/shard_map/scatter_ctx/pallas_call | solution.py:456
  545.9 2.4 multiply_reduce_fusion
  548.3 1.7 fusion.36
  550.0 68.9 %gather_multiply.1 = (bf16[16,128,2048]{2,1,0:T(8,128)(2,1)}, bf16[704,2048]{1,0:T(8,128)(2,1)}, bf16[704,2048]{1,0:T(8,128)(2,1)}, bf16[704,2048]{1,0:T(8,128)(2,1)}) custom-call(bf16[128,2048]{1,0:T(8,128)(2,1)} %get-tuple-element.135.x_ref, bf16[1152,2048]{1,0:T(8,128)(2,1)} %get-tuple-element.94.rows_ref, bf16[1152,2048]{1,0:T(8,128)(2,1)} %get-tuple-element.95.dy_ref, ...), custom_call_target="tpu_custom_call" | custom-call | tf_op jit(solution)/shard_map/gather_multiply/pallas_call | solution.py:338
  619.7 2.2 reduce.5
  622.6 1.5 collective-permute-start.8
  624.1 1.4 copy.173.extra_ref
  625.5 1.5 slice.70
  632.5 2.9 fusion.12
  635.4 5.2 all-to-all-start.2
  640.6 19.3 %attend_back.1 = (f32[2048,256]{1,0:T(8,128)}, f32[2048,256]{1,0:T(8,128)}, f32[2048,128]{1,0:T(8,128)}, f32[128,2048]{1,0:T(8,128)}) custom-call(bf16[2048,256]{1,0:T(8,128)(2,1)} %get-tuple-element.78.q_ref, bf16[2048,256]{1,0:T(8,128)(2,1)} %get-tuple-element.79.k_ref, bf16[2048,128]{1,0:T(8,128)(2,1)} %get-tuple-element.80.v_ref, ...), custom_call_target="tpu_custom_call" | custom-call | flops 3489660928 | bytes 8192000 | tf_op jit(solution)/shard_map/attend_back/pallas_call | solution.py:571
  660.0 1.1 fusion.18
  661.3 5.3 bitcast_convert_fusion
  666.6 5.9 convert_bitcast_fusion
  672.5 31.6 %project_back.1 = (bf16[2048,2048]{1,0:T(8,128)(2,1)}, f32[2048,896]{1,0:T(8,128)}, f32[512,256]{1,0:T(8,128)}) custom-call(f32[2048,256]{1,0:T(8,128)} %get-tuple-element.107.dq_ref, f32[2048,256]{1,0:T(8,128)} %get-tuple-element.108.dk_ref, f32[2048,128]{1,0:T(8,128)} %get-tuple-element.109.dv_ref, f32[2048,512]{1,0:T(8,128)} %get-tuple-element.110.raw_ref, ...), custom_call_target="tpu_custom_call" | custom-call | flops 15032385536 | bytes 25165824 | tf_op jit(solution)/shard_map/project_back/pallas_call | solution.py:868
  704.1 8.3 finish.1
  712.4 2.7 dynamic-slice_bitcast_fusion
  717.3 1.9 bitcast_add_fusion
  720.6 2.0 fusion.15
  722.6 6.8 all-to-all-start.3
  729.4 3.2 fusion.refs_1_
  732.6 88.0 %scatter_ctx.7 = (f32[128,2048]{1,0:T(8,128)}, f32[64,640]{1,0:T(8,128)}) custom-call(bf16[16,128,2048]{2,1,0:T(8,128)(2,1)} %bitcast.144, bf16[16,64,640]{2,1,0:T(8,128)(2,1)} %fusion.refs_1_), custom_call_target="tpu_custom_call" | custom-call | tf_op jit(solution)/shard_map/scatter_ctx/pallas_call | solution.py:456
  821.6 1.5 slice_reduce_fusion
  823.7 1.5 fusion.5
  825.7 2.6 fusion.9
  829.2 3.0 spread.1
  (157 shorter events, 25.5 us)
Async XLA Ops:
  0.6 103.8 %collective-permute-start.2 = (bf16[64,2048]{1,0:T(8,128)(2,1)}, bf16[64,2048]{1,0:T(8,128)(2,1)}, u32[]{:S(2)}, u32[]{:S(2)}) collective-permute-start(bf16[64,2048]{1,0:T(8,128)(2,1)} %param.28), channel_id=1, source_target_pairs={{0,1},{1,0},{2,3},{3,2},{4,5},{5,4},{6,7},{7,6},{8,9},{9,8},{10,11... | collective-permute-start | bytes 786440 | tf_op jit(solution)/shard_map/ppermute | solution.py:1434
  1.2 110.6 %collective-permute-start.7 = (bf16[88,2048]{1,0:T(8,128)(2,1)}, bf16[88,2048]{1,0:T(8,128)(2,1)}, u32[]{:S(2)}, u32[]{:S(2)}) collective-permute-start(bf16[88,2048]{1,0:T(8,128)(2,1)} %param.32), channel_id=1, source_target_pairs={{0,1},{1,0},{2,3},{3,2},{4,5},{5,4},{6,7},{7,6},{8,9},{9,8},{10,11... | collective-permute-start | bytes 1081352 | tf_op jit(solution)/shard_map/ppermute | solution.py:1434
  2.3 12.0 %copy-start.24 = (f32[1,128,6]{1,0,2:T(1,128)S(1)}, f32[1,128,6]{1,0,2:T(1,128)}, u32[]{:S(2)}) copy-start(f32[1,128,6]{1,0,2:T(1,128)} %param.22) | copy-start | bytes 9220
  2.3 12.0 %copy-start.25 = (s32[1,128,6]{1,0,2:T(1,128)S(1)}, s32[1,128,6]{1,0,2:T(1,128)}, u32[]{:S(2)}) copy-start(s32[1,128,6]{1,0,2:T(1,128)} %param.21) | copy-start | bytes 9220
  2.3 12.0 %copy-start.26 = (s32[1,4]{1,0:T(1,128)S(1)}, s32[1,4]{1,0:T(1,128)}, u32[]{:S(2)}) copy-start(s32[1,4]{1,0:T(1,128)} %param.20) | copy-start | bytes 52
  3.9 11.8 %copy-start.29 = (bf16[16]{0:T(256)(128)(2,1)S(1)}, bf16[16]{0:T(256)(128)(2,1)}, u32[]{:S(2)}) copy-start(bf16[16]{0:T(256)(128)(2,1)} %param.26) | copy-start | bytes 100
  4.0 12.0 %copy-start.27 = (bf16[64]{0:T(256)(128)(2,1)S(1)}, bf16[64]{0:T(256)(128)(2,1)}, u32[]{:S(2)}) copy-start(bf16[64]{0:T(256)(128)(2,1)} %param.29) | copy-start | bytes 388
  4.0 12.1 %copy-start.28 = (bf16[64]{0:T(256)(128)(2,1)S(1)}, bf16[64]{0:T(256)(128)(2,1)}, u32[]{:S(2)}) copy-start(bf16[64]{0:T(256)(128)(2,1)} %param.23) | copy-start | bytes 388
  4.0 12.8 %copy-start.15 = (bf16[64,2816]{1,0:T(8,128)(2,1)S(1)}, bf16[64,2816]{1,0:T(8,128)(2,1)}, u32[]{:S(2)}) copy-start(bf16[64,2816]{1,0:T(8,128)(2,1)} %param.30) | copy-start | bytes 1081348
  5.1 12.8 %copy-start.16 = (bf16[64,2816]{1,0:T(8,128)(2,1)S(1)}, bf16[64,2816]{1,0:T(8,128)(2,1)}, u32[]{:S(2)}) copy-start(bf16[64,2816]{1,0:T(8,128)(2,1)} %param.31) | copy-start | bytes 1081348
  5.1 101.2 %all-to-all-start = ((bf16[16,64,256]{2,1,0:T(8,128)(2,1)}), bf16[16,64,256]{2,1,0:T(8,128)(2,1)S(1)}, u32[]{:S(2)}, u32[]{:S(2)}) async-start(bf16[16,64,256]{2,1,0:T(8,128)(2,1)} %maximum_maximum_fusion), calls=%async_computation | async-start | bytes 1048576 | tf_op jit(solution)/shard_map/all_to_all | solution.py:1495
  13.6 226.9 %collective-permute-start.3 = (bf16[704,2048]{1,0:T(8,128)(2,1)}, bf16[704,2048]{1,0:T(8,128)(2,1)}, u32[]{:S(2)}, u32[]{:S(2)}) collective-permute-start(bf16[704,2048]{1,0:T(8,128)(2,1)} %bitcast.25.refs_0_.refs_4_), channel_id=1, source_target_pairs={{0,1},{1,0},{2,3},{3,2},{4,5},{5,4},{6,7},{7,6},{8,9},{9,8},{10,11... | collective-permute-start | bytes 8650760 | tf_op jit(solution)/shard_map/ppermute | solution.py:1434
  13.6 226.8 %collective-permute-start.4 = (bf16[704,2048]{1,0:T(8,128)(2,1)}, bf16[704,2048]{1,0:T(8,128)(2,1)}, u32[]{:S(2)}, u32[]{:S(2)}) collective-permute-start(bf16[704,2048]{1,0:T(8,128)(2,1)} %bitcast.27.refs_1_.refs_5_), channel_id=1, source_target_pairs={{0,1},{1,0},{2,3},{3,2},{4,5},{5,4},{6,7},{7,6},{8,9},{9,8},{10,11... | collective-permute-start | bytes 8650760 | tf_op jit(solution)/shard_map/ppermute | solution.py:1434
  14.1 226.3 %collective-permute-start.5 = (bf16[704,2048]{1,0:T(8,128)(2,1)}, bf16[704,2048]{1,0:T(8,128)(2,1)}, u32[]{:S(2)}, u32[]{:S(2)}) collective-permute-start(bf16[704,2048]{1,0:T(8,128)(2,1)} %bitcast.28.refs_2_.refs_6_), channel_id=1, source_target_pairs={{0,1},{1,0},{2,3},{3,2},{4,5},{5,4},{6,7},{7,6},{8,9},{9,8},{10,11... | collective-permute-start | bytes 8650760 | tf_op jit(solution)/shard_map/ppermute | solution.py:1434
  14.5 7.5 copy-start.23
  20.6 2.8 copy-start.21
  23.4 81.1 %copy-start.19 = (bf16[64,2048]{1,0:T(8,128)(2,1)S(1)}, bf16[64,2048]{1,0:T(8,128)(2,1)}, u32[]{:S(2)}) copy-start(bf16[64,2048]{1,0:T(8,128)(2,1)} %param.28) | copy-start | bytes 786436
  104.4 7.6 copy-start.17
  104.4 9.8 %collective-permute-start.1 = (bf16[16,64,640]{2,1,0:T(8,128)(2,1)}, bf16[16,64,640]{2,1,0:T(8,128)(2,1)S(1)}, u32[]{:S(2)}, u32[]{:S(2)}) collective-permute-start(bf16[16,64,640]{2,1,0:T(8,128)(2,1)} %get-tuple-element.74.mine_n_ref), channel_id=1, source_target_pairs={{0,1},{1,0},{2,3},{3,2},{4,5},{5,4},{6,7},{7,6},{8,9},{9,8},{10,11... | collective-permute-start | bytes 3932168 | tf_op jit(solution)/shard_map/ppermute | solution.py:1434
  106.3 6.8 copy-start.8
  106.3 128.1 %all-to-all-start.1 = ((bf16[16,64,512]{2,1,0:T(8,128)(2,1)}), bf16[16,64,512]{2,1,0:T(8,128)(2,1)S(1)}, u32[]{:S(2)}, u32[]{:S(2)}) async-start(bf16[16,64,512]{2,1,0:T(8,128)(2,1)} %fusion.11), calls=%async_computation.1 | async-start | bytes 2097152 | tf_op jit(solution)/shard_map/all_to_all | solution.py:1495
  111.8 2.4 collective-permute-start
  114.2 1.1 copy-start.11
  115.3 0.8 copy-start.14
  159.7 73.3 %copy-start.2 = (bf16[1,128,2048]{2,1,0:T(8,128)(2,1)S(1)}, bf16[1,128,2048]{2,1,0:T(8,128)(2,1)}, u32[]{:S(2)}) copy-start(bf16[1,128,2048]{2,1,0:T(8,128)(2,1)} %param.18) | copy-start | bytes 1572868
  234.5 2.9 collective-permute-start.6
  236.1 2.6 copy-start.20
  325.7 63.7 %copy-start.3 = (bf16[1,128,2048]{2,1,0:T(8,128)(2,1)S(1)}, bf16[1,128,2048]{2,1,0:T(8,128)(2,1)}, u32[]{:S(2)}) copy-start(bf16[1,128,2048]{2,1,0:T(8,128)(2,1)} %param.19) | copy-start | bytes 1572868
  490.4 55.4 %copy-start = (f32[128,2048]{1,0:T(8,128)S(1)}, f32[128,2048]{1,0:T(8,128)}, u32[]{:S(2)}) copy-start(f32[128,2048]{1,0:T(8,128)} %scatter_ctx.5) | copy-start | bytes 3145732
  545.8 2.4 copy-start.1
  550.0 69.0 %copy-start.10 = (bf16[2048,512]{1,0:T(8,128)(2,1)S(1)}, bf16[2048,512]{1,0:T(8,128)(2,1)}, u32[]{:S(2)}) copy-start(bf16[2048,512]{1,0:T(8,128)(2,1)} %get-tuple-element.103) | copy-start | bytes 6291460
  619.0 13.5 %collective-permute-start.9 = (bf16[16,64,512]{2,1,0:T(8,128)(2,1)S(1)}, bf16[16,64,512]{2,1,0:T(8,128)(2,1)}, u32[]{:S(2)}, u32[]{:S(2)}) collective-permute-start(bf16[16,64,512]{2,1,0:T(8,128)(2,1)S(1)} %dynamic-slice_bitcast_fusion.1), channel_id=1, source_target_pairs={{0,1},{1,0},{2,3},{3,2},{4,5},{5,4},{6,7},{7,6},{8,9},{9,8},{10,11... | collective-permute-start | bytes 3145736 | tf_op jit(solution)/shard_map/ppermute | solution.py:1434
  622.6 5.2 collective-permute-start.8
  627.7 89.6 %collective-permute-start.13 = (bf16[88,2048]{1,0:T(8,128)(2,1)}, bf16[88,2048]{1,0:T(8,128)(2,1)}, u32[]{:S(2)}, u32[]{:S(2)}) collective-permute-start(bf16[88,2048]{1,0:T(8,128)(2,1)} %fusion.17), channel_id=1, source_target_pairs={{0,1},{1,0},{2,3},{3,2},{4,5},{5,4},{6,7},{7,6},{8,9},{9,8},{10,11... | collective-permute-start | bytes 1081352 | tf_op jit(solution)/shard_map/ppermute | solution.py:1434
  635.4 37.1 %all-to-all-start.2 = ((bf16[16,64,512]{2,1,0:T(8,128)(2,1)}), bf16[16,64,512]{2,1,0:T(8,128)(2,1)S(1)}, u32[]{:S(2)}, u32[]{:S(2)}) async-start(bf16[16,64,512]{2,1,0:T(8,128)(2,1)} %fusion.12), calls=%async_computation.2 | async-start | bytes 2097152 | tf_op jit(solution)/shard_map/all_to_all | solution.py:1495
  661.0 54.4 %collective-permute-start.12 = (bf16[64,2048]{1,0:T(8,128)(2,1)S(1)}, bf16[64,2048]{1,0:T(8,128)(2,1)S(1)}, u32[]{:S(2)}, u32[]{:S(2)}) collective-permute-start(bf16[64,2048]{1,0:T(8,128)(2,1)S(1)} %fusion.18), channel_id=1, source_target_pairs={{0,1},{1,0},{2,3},{3,2},{4,5},{5,4},{6,7},{7,6},{8,9},{9,8},{10,11... | collective-permute-start | bytes 786440 | tf_op jit(solution)/shard_map/ppermute | solution.py:1434
  661.3 5.3 copy-start.6
  661.3 5.3 copy-start.7
  672.5 46.7 %copy-start.4 = (bf16[16,64,512]{2,1,0:T(8,128)(2,1)}, bf16[16,64,512]{2,1,0:T(8,128)(2,1)S(1)}, u32[]{:S(2)}) copy-start(bf16[16,64,512]{2,1,0:T(8,128)(2,1)S(1)} %all-to-all-done.2.pack_s_ref) | copy-start | bytes 3145732
  712.4 3.0 copy-start.13
  712.4 3.8 copy-start.12
  715.1 14.3 %collective-permute-start.10 = (bf16[16,64,640]{2,1,0:T(8,128)(2,1)}, bf16[16,64,640]{2,1,0:T(8,128)(2,1)}, u32[]{:S(2)}, u32[]{:S(2)}) collective-permute-start(bf16[16,64,640]{2,1,0:T(8,128)(2,1)} %dynamic-slice_bitcast_fusion), channel_id=1, source_target_pairs={{0,1},{1,0},{2,3},{3,2},{4,5},{5,4},{6,7},{7,6},{8,9},{9,8},{10,11... | collective-permute-start | bytes 3932168 | tf_op jit(solution)/shard_map/ppermute | solution.py:1434
  717.1 3.5 collective-permute-start.11
  722.6 105.8 %all-to-all-start.3 = ((bf16[16,64,256]{2,1,0:T(8,128)(2,1)}), bf16[16,64,256]{2,1,0:T(8,128)(2,1)S(1)}, u32[]{:S(2)}, u32[]{:S(2)}) async-start(bf16[16,64,256]{2,1,0:T(8,128)(2,1)} %fusion.15), calls=%async_computation.3 | async-start | bytes 1048576 | tf_op jit(solution)/shard_map/all_to_all | solution.py:1495
  732.6 91.1 %copy-start.22 = (f32[1,2048]{1,0:T(1,128)S(1)}, f32[1,2048]{1,0:T(1,128)}, u32[]{:S(2)}) copy-start(f32[1,2048]{1,0:T(1,128)} %get-tuple-element.157.gain_ref) | copy-start | bytes 24580
  820.6 5.1 copy-start.5
  825.7 6.4 copy-start.18
  828.3 0.8 copy-start.9

commit v4 on v3

--- a/solution.py
+++ b/solution.py
@@ -45,7 +45,8 @@
 
 
 def rope_tables(offsets):
-    freqs = 10000.0 ** (-(jnp.arange(DR // 2, dtype=f32) * 2.0) / DR)
+    spot = (jnp.arange(2 * DR, dtype=jnp.int32) % (DR // 2)).astype(f32)
+    freqs = 10000.0 ** (-(spot * 2.0) / DR)
     angle = offsets.astype(f32)[:, None] * freqs[None, :]
     return (jnp.cos(angle), jnp.sin(angle))
 
@@ -490,7 +491,8 @@
             total = jnp.sum(weights, axis=-1, keepdims=True)
             summed = dot(weights.astype(bf16), v_ref[:extent, :])
             o_ref[...] = summed / total
-            log_ref[...] = top + jnp.log(total)
+            column = jnp.broadcast_to(top + jnp.log(total), (block, 128))
+            log_ref[...] = column.T[:1, :]
             part_ref[...] = dot((summed / total).astype(bf16), wo_ref[...]).astype(bf16)
 
 
@@ -504,7 +506,7 @@
         grid=(count,),
         out_shape=(
             jax.ShapeDtypeStruct((length, DV), f32),
-            jax.ShapeDtypeStruct((length, 1), f32),
+            jax.ShapeDtypeStruct((1, length), f32),
             jax.ShapeDtypeStruct((length, D), bf16),
         ),
         in_specs=[
@@ -516,7 +518,7 @@
         ],
         out_specs=(
             pl.BlockSpec((block, DV), lambda i: (i, 0)),
-            pl.BlockSpec((block, 1), lambda i: (i, 0)),
+            pl.BlockSpec((1, block), lambda i: (0, i)),
             pl.BlockSpec((block, D), lambda i: (i, 0)),
         ),
         compiler_params=pltpu.CompilerParams(vmem_limit_bytes=60 << 20),
@@ -530,9 +532,12 @@
 
 def attend_back_kernel(
     block, count, q_ref, k_ref, v_ref, m_ref, att_ref, wo_ref, first_ref, log_ref,
-    dq_ref, dk_ref, dv_ref, gwo_ref,
+    *refs,
 ):
+    lows, (dq_ref, dk_ref, dv_ref, gwo_ref), wides = refs[:3], refs[3:7], refs[7:]
     step = pl.program_id(0)
+    for low_ref, wide_ref in zip(lows, wides):
+        wide_ref[...] = low_ref[...].astype(f32)
 
     @pl.when(step == 0)
     def _():
@@ -561,13 +566,17 @@
             dq_ref[...] = dot_first(grad_scores, keys)
 
 
-def attend_back(queries, keys, values, grad_mixed, attended, w_output, first, log_total):
+def attend_back(queries, keys, values, grad_mixed, attended, w_output, first, log_total, lows):
     length = queries.shape[0]
     block = min(256, length)
     count = length // block
     row = lambda: pl.BlockSpec((1, block), lambda i: (0, i))
     whole = lambda height, width: pl.BlockSpec((height, width), lambda i: (0, 0))
     part = lambda width: pl.BlockSpec((block, width), lambda i: (i, 0))
+    tall, wide = lows[0].shape
+    piece = 176 if tall % 176 == 0 else tall
+    steps = tall // piece
+    some = pl.BlockSpec((piece, wide), lambda i: (i * steps // count, 0))
     return pl.pallas_call(
         functools.partial(attend_back_kernel, block, count),
         name="attend_back",
@@ -577,7 +586,8 @@
             jax.ShapeDtypeStruct((length, WIDE), f32),
             jax.ShapeDtypeStruct((length, DV), f32),
             jax.ShapeDtypeStruct((DV, D), f32),
-        ),
+        )
+        + tuple(jax.ShapeDtypeStruct((tall, wide), f32) for _ in lows),
         in_specs=[
             part(WIDE),
             whole(length, WIDE),
@@ -587,15 +597,16 @@
             whole(DV, D),
             row(),
             row(),
-        ],
-        out_specs=(part(WIDE), whole(length, WIDE), whole(length, DV), whole(DV, D)),
+        ]
+        + [some] * 3,
+        out_specs=(part(WIDE), whole(length, WIDE), whole(length, DV), whole(DV, D)) + (some,) * 3,
         compiler_params=pltpu.CompilerParams(vmem_limit_bytes=60 << 20),
         cost_estimate=pl.CostEstimate(
             flops=length * length * (3 * (DN + DR) + 2 * DV),
             bytes_accessed=length * 4000,
             transcendentals=length * length // 2,
         ),
-    )(queries, keys, values, grad_mixed, attended, w_output, first, log_total)
+    )(queries, keys, values, grad_mixed, attended, w_output, first, log_total, *lows)
 
 
 def lanes_of(value):
@@ -654,45 +665,82 @@
     )(mine, other, mine_n, other_n)
 
 
-def finish_kernel(cycle, slab, gw_ref, gwe_ref, w_ref, we_ref, extra_ref, first_ref, slim_ref):
+def finish_kernel(
+    cycle, slab, gw_ref, gwe_ref, w_ref, we_ref, extra_ref, first_ref, slim_ref,
+    away_first, away_slim, got_first, got_slim, send_sem, recv_sem,
+):
+    me = lax.axis_index("fsdp")
     quarter = slab // 4
-    turned = gw_ref[:, 2 * DN : 3 * DN]
-    ropes = gw_ref[:, DN : 2 * DN] - swap_lanes(turned)
-    gain_one = jnp.sum(gw_ref[...] * w_ref[...].astype(f32), axis=1, keepdims=True)
-    gain_latent = jnp.sum(gwe_ref[...] * we_ref[...].astype(f32), axis=1, keepdims=True)
-    lanes = lanes_of(ropes)
-    first_ref[:, :DN] = gw_ref[:, :DN].astype(bf16)
-    slim_ref[:, :KVR] = gw_ref[:, 3 * DN :].astype(bf16)
-    tail = jnp.where(lanes < DR, pltpu.roll(ropes, DR, 1), 0.0)
-    tail = jnp.where(lanes == DR, gain_one, tail)
-    tail = jnp.where(lanes == DR + 1, extra_ref[...], tail)
-    for part in range(cycle * 2):
-        rows = slice(part * slab, (part + 1) * slab)
-        some = slice(part * quarter, (part + 1) * quarter)
-        expand = gwe_ref[some, :]
-        pieces = [
-            pltpu.roll(expand[:, :DN], DR, 1),
-            expand[:, :DN],
-            pltpu.roll(expand[:, DN:], DR, 1),
-            expand[:, DN:],
-        ]
-        pieces = jnp.concatenate(pieces, axis=0)
-        first_ref[rows, DN:] = jnp.where(lanes[rows] < DR, ropes[rows], pieces).astype(bf16)
-        column = jnp.concatenate(
-            [gain_latent[some], jnp.zeros((slab - quarter, 1), f32)], axis=0
-        )
-        slim_ref[rows, KVR:] = jnp.where(lanes[rows] == DR + 2, column, tail[rows]).astype(bf16)
-
-
-def finish(grad_w, grad_we, w_cat, w_expand, extra, cycle, slab):
+    barrier = pltpu.get_barrier_semaphore()
+    pl.semaphore_signal(barrier, inc=1, device_id={"fsdp": 1 - me}, device_id_type=MESH)
+
+    def by_slab(owner, first_out, slim_out):
+        @pl.loop(0, cycle)
+        def _(c):
+            rows = pl.ds(pl.multiple_of((c * 2 + owner) * slab, slab), slab)
+            some = pl.ds(pl.multiple_of((c * 2 + owner) * quarter, quarter), quarter)
+            grad, expand = gw_ref[rows, :], gwe_ref[some, :]
+            ropes = grad[:, DN : 2 * DN] - swap_lanes(grad[:, 2 * DN : 3 * DN])
+            gain_one = jnp.sum(grad * w_ref[rows, :].astype(f32), axis=1, keepdims=True)
+            gain_latent = jnp.sum(expand * we_ref[some, :].astype(f32), axis=1, keepdims=True)
+            lanes = lanes_of(ropes)
+            tail = jnp.where(lanes < DR, pltpu.roll(ropes, DR, 1), 0.0)
+            tail = jnp.where(lanes == DR, gain_one, tail)
+            tail = jnp.where(lanes == DR + 1, extra_ref[rows, :], tail)
+            column = jnp.concatenate([gain_latent, jnp.zeros((slab - quarter, 1), f32)], axis=0)
+            tail = jnp.where(lanes == DR + 2, column, tail)
+            pieces = jnp.concatenate(
+                [
+                    pltpu.roll(expand[:, :DN], DR, 1),
+                    expand[:, :DN],
+                    pltpu.roll(expand[:, DN:], DR, 1),
+                    expand[:, DN:],
+                ],
+                axis=0,
+            )
+            first_out[c, :, :DN] = grad[:, :DN].astype(bf16)
+            first_out[c, :, DN:] = jnp.where(lanes < DR, ropes, pieces).astype(bf16)
+            slim_out[c, :, :KVR] = grad[:, 3 * DN :].astype(bf16)
+            slim_out[c, :, KVR:] = tail.astype(bf16)
+
+    by_slab(1 - me, away_first, away_slim)
+    pl.semaphore_wait(barrier, 1)
+    copies = [
+        pltpu.make_async_remote_copy(
+            src_ref=src,
+            dst_ref=dst,
+            send_sem=send_sem.at[i],
+            recv_sem=recv_sem.at[i],
+            device_id={"fsdp": 1 - me},
+            device_id_type=MESH,
+        )
+        for i, (src, dst) in enumerate(((away_first, got_first), (away_slim, got_slim)))
+    ]
+    for item in copies:
+        item.start()
+    by_slab(me, first_ref, slim_ref)
+    for item in copies:
+        item.wait()
+
+    @pl.loop(0, cycle)
+    def _(c):
+        first_ref[c] = (first_ref[c].astype(f32) + got_first[c].astype(f32)).astype(bf16)
+        slim_ref[c] = (slim_ref[c].astype(f32) + got_slim[c].astype(f32)).astype(bf16)
+
+
+def finish(grad_w, grad_we, w_cat, w_expand, extra, cycle, slab, collective):
+    shapes = [(cycle, slab, 256), (cycle, slab, KVR + DN)]
     return pl.pallas_call(
         functools.partial(finish_kernel, cycle, slab),
         name="finish",
-        out_shape=(
-            jax.ShapeDtypeStruct((D, 256), bf16),
-            jax.ShapeDtypeStruct((D, KVR + DN), bf16),
-        ),
-        compiler_params=pltpu.CompilerParams(vmem_limit_bytes=60 << 20),
+        out_shape=tuple(jax.ShapeDtypeStruct(shape, bf16) for shape in shapes),
+        in_specs=[pl.BlockSpec(memory_space=pltpu.VMEM)] * 5,
+        out_specs=(pl.BlockSpec(memory_space=pltpu.VMEM),) * 2,
+        scratch_shapes=[pltpu.VMEM(shape, bf16) for shape in shapes * 2]
+        + [pltpu.SemaphoreType.DMA((2,)), pltpu.SemaphoreType.DMA((2,))],
+        compiler_params=pltpu.CompilerParams(
+            collective_id=collective, has_side_effects=True, vmem_limit_bytes=60 << 20
+        ),
     )(grad_w, grad_we, w_cat, w_expand, extra)
 
 
@@ -781,7 +829,7 @@
 
 def project(x, gain, w_cat, gain_latent, w_expand, cosine, sine, scale):
     length = x.shape[0]
-    block = min(256, length)
+    block = min(512, length)
     width = w_cat.shape[1]
     return pl.pallas_call(
         functools.partial(project_kernel, scale),
@@ -821,7 +869,7 @@
 
 def project_back_kernel(
     scale, copies, dq_ref, dk_ref, dv_ref, raw_ref, latent_ref, act_ref, cos_ref, sin_ref,
-    w_ref, we_ref, gain_l_ref, keep_q_ref, keep_e_ref, part_ref, gw_ref, gwe_ref,
+    we_ref, gain_l_ref, keep_q_ref, keep_e_ref, grads_ref, gw_ref, gwe_ref,
 ):
     @pl.when(pl.program_id(0) == 0)
     def _():
@@ -853,24 +901,24 @@
         ],
         axis=-1,
     )
-    part_ref[...] = dot_last(grads, w_ref[...]).astype(bf16)
+    grads_ref[...] = grads
     gw_ref[...] += dot_first(act_ref[...], grads)
     gwe_ref[...] += dot_first(latent_ref[...], expanded)
 
 
 def project_back(
-    grad_q, grad_k, grad_v, raw, latent, act, cosine, sine, w_cat, w_expand, gain_latent, keep_q,
+    grad_q, grad_k, grad_v, raw, latent, act, cosine, sine, w_expand, gain_latent, keep_q,
     keep_e, scale, copies,
 ):
     length = act.shape[0]
-    block = min(256, length)
-    width = w_cat.shape[1]
+    block = min(512, length)
+    width = 3 * DN + KVR
     return pl.pallas_call(
         functools.partial(project_back_kernel, scale, copies),
         name="project_back",
         grid=(length // block,),
         out_shape=(
-            jax.ShapeDtypeStruct((length, D), bf16),
+            jax.ShapeDtypeStruct((length, width), bf16),
             jax.ShapeDtypeStruct((D, width), f32),
             jax.ShapeDtypeStruct((KVR, DN + DV), f32),
         ),
@@ -883,14 +931,13 @@
             by_rows(block, D),
             by_rows(block, DN),
             by_rows(block, DN),
-            fixed((D, width)),
             fixed((KVR, DN + DV)),
             fixed((1, KVR)),
             fixed((1, WIDE)),
             fixed((1, DN + DV)),
         ],
         out_specs=(
-            by_rows(block, D),
+            by_rows(block, width),
             pl.BlockSpec((D, width), lambda i: (0, 0)),
             pl.BlockSpec((KVR, DN + DV), lambda i: (0, 0)),
         ),
@@ -899,9 +946,30 @@
             flops=4 * length * D * width, bytes_accessed=length * D * 6, transcendentals=0
         ),
     )(
-        grad_q, grad_k, grad_v, raw, latent, act, cosine, sine, w_cat, w_expand,
-        gain_latent[None, :], keep_q, keep_e,
+        grad_q, grad_k, grad_v, raw, latent, act, cosine, sine, w_expand, gain_latent[None, :],
+        keep_q, keep_e,
     )
+
+
+def rows_kernel(grads_ref, w_ref, part_ref):
+    part_ref[...] = dot_last(grads_ref[...], w_ref[...]).astype(bf16)
+
+
+def project_back_rows(grads, w_cat):
+    length, width = grads.shape
+    block = min(512, length)
+    return pl.pallas_call(
+        rows_kernel,
+        name="project_back_rows",
+        grid=(length // block,),
+        out_shape=jax.ShapeDtypeStruct((length, D), bf16),
+        in_specs=[by_rows(block, width), fixed((D, width))],
+        out_specs=by_rows(block, D),
+        compiler_params=pltpu.CompilerParams(vmem_limit_bytes=60 << 20),
+        cost_estimate=pl.CostEstimate(
+            flops=2 * length * D * width, bytes_accessed=length * D * 4, transcendentals=0
+        ),
+    )(grads, w_cat)
 
 
 class Gather:
@@ -1165,7 +1233,7 @@
     half = weights[0].shape[0]
     width = shared[1].shape[0]
     pieces = 3 * shares + 2 + size // unit
-    groups, plan = gather_plan(parts, bits, events, 66.0, size, pieces, 10.5)
+    groups, plan = gather_plan(parts, bits, events, 90.0, size, pieces, 10.5)
     anywhere = pl.BlockSpec(memory_space=pl.ANY)
     inside = pl.BlockSpec(memory_space=pltpu.VMEM)
     return pl.pallas_call(
@@ -1384,7 +1452,7 @@
     half = weights[0].shape[0]
     width = shared[1].shape[0]
     pieces = 3 * shares + 3 + size // unit
-    groups, plan = gather_plan(parts, bits, events, 66.0, size, pieces, 15.0)
+    groups, plan = gather_plan(parts, bits, events, 90.0, size, pieces, 15.0)
     anywhere = pl.BlockSpec(memory_space=pl.ANY)
     inside = pl.BlockSpec(memory_space=pltpu.VMEM)
     return pl.pallas_call(
@@ -1574,10 +1642,12 @@
     inside = starts[None, :] <= positions[:, None]
     first_pos = jnp.max(jnp.where(inside, starts[None, :], 0), axis=1)
     cosine, sine = rope_tables(positions - first_pos)
-    cosine = jnp.tile(cosine, (1, 4))
-    sine = jnp.tile(sine, (1, 4))
-
-    all_hidden, narrow = gather_ctx([hidden_in[0], narrow], bits, 1)
+    first_col = first_pos[:, None]
+
+    own_hidden, cosine, sine, first_col = lax.optimization_barrier(
+        (hidden_in[0], cosine, sine, first_col)
+    )
+    all_hidden, narrow = gather_ctx([own_hidden, narrow], bits, 1)
     packed_s, _ = lax.optimization_barrier((packed_s, all_hidden))
     packed_s = exchange(packed_s)
     my_probs = packed_s[:, :, part_s : part_s + prob_width]
@@ -1610,7 +1680,7 @@
         all_hidden.reshape(length, D), gain_one, w_cat, gain_latent, w_expand, cosine, sine, scale
     )
     attended, log_total, partial = attend(
-        queries, keys, values, first_pos[:, None], own_output
+        queries, keys, values, first_col, own_output
     )
     (mixing,) = scatter_ctx([partial.reshape(cycle, tokens, D)], bits, 3)
     mixed = residual + mixing
@@ -1646,17 +1716,10 @@
 
     grad_gain_two = jnp.sum(grad_act_two * mixed * factor_two, axis=0)
     grad_mixed = diff + norm_back_rows(mixed, factor_two, gain_two, grad_act_two)
-    lefts = []
-    for r in range(groups):
-        lefts += [grads[2 * r], grads[2 * r + 1], kept[3 * r + 2]]
-    all_mixed, *expert_grads = gather_multiply(
-        grad_mixed.astype(bf16), rows, grad_rows, lefts, bits, 5
-    )
     def by_owner(grad):
         cut = jnp.transpose(grad.reshape(cycle, groups, slab, -1), (1, 0, 2, 3))
         return scatter_fsdp(cut, groups).astype(bf16)
 
-    grad_shared, _ = lax.optimization_barrier((grad_shared, all_mixed))
     grad_shared = by_owner(grad_shared)
     high = lax.reduce_precision(share, 8, 7)
     mid = lax.reduce_precision(share - high, 8, 7)
@@ -1664,10 +1727,17 @@
     spot = jnp.arange(grad_shared.shape[2], dtype=jnp.int32) - part_s
     loss_row = sum(jnp.where(spot == i, loss_parts[i], bf16(0)) for i in range(3))
     grad_shared = jnp.where(((spot >= 0) & (spot < 3))[None, None, :], loss_row, grad_shared)
+    lefts = []
+    for r in range(groups):
+        lefts += [grads[2 * r], grads[2 * r + 1], kept[3 * r + 2]]
+    all_mixed, *expert_grads = gather_multiply(
+        grad_mixed.astype(bf16), rows, grad_rows, lefts, bits, 5
+    )
+    grad_shared, all_mixed = lax.optimization_barrier((grad_shared, all_mixed))
     packed_s = exchange(grad_shared)
     loss_parts = packed_s[:, 0, part_s : part_s + 3].astype(f32)
     loss_value = jnp.sum(loss_parts) / (length * groups * D)
-    grad_query, grad_keys, grad_values, grad_w_output = attend_back(
+    grad_query, grad_keys, grad_values, grad_w_output, *expert_grads = attend_back(
         queries,
         keys,
         values,
@@ -1675,7 +1745,8 @@
         attended,
         w_output,
         first_pos[None, :],
-        log_total.reshape(1, length),
+        log_total,
+        expert_grads,
     )
     grad_query, packed_s = lax.optimization_barrier((grad_query, packed_s))
     grad_w_output = own_part(grad_w_output, 0).reshape(groups, slab, D)
@@ -1683,7 +1754,7 @@
     lanes = jnp.arange(WIDE, dtype=jnp.int32)
     keep_q = (lanes // ((DN + DR) // copies) == copy_index).astype(f32)[None, :]
     keep_e = (lanes // ((DN + DV) // copies) == copy_index).astype(f32)[None, :]
-    partial, grad_w_cat, grad_w_expand = project_back(
+    grads_cat, grad_w_cat, grad_w_expand = project_back(
         grad_query,
         grad_keys,
         grad_values,
@@ -1692,7 +1763,6 @@
         act_one,
         cosine,
         sine,
-        w_cat,
         w_expand,
         gain_latent,
         keep_q,
@@ -1702,7 +1772,7 @@
     )
     if fast:
         first, slim = finish(
-            grad_w_cat, grad_w_expand, w_cat, w_expand, grad_gain_two[:, None], cycle, slab
+            grad_w_cat, grad_w_expand, w_cat, w_expand, grad_gain_two[:, None], cycle, slab, 7
         )
     else:
         grad_gain_one = jnp.sum(grad_w_cat * w_cat.astype(f32), axis=1)
@@ -1731,10 +1801,10 @@
             ],
             axis=1,
         ).astype(bf16)
-
-    slim = by_owner(slim)
-    first = padded(by_owner(first), block_q)
+        slim, first = by_owner(slim), padded(by_owner(first), block_q)
     packed = exchange(first)
+    partial = project_back_rows(grads_cat, w_cat)
+    partial, packed = lax.optimization_barrier((partial, packed))
     grad_act_one, grad_narrow = scatter_ctx(
         [partial.reshape(cycle, tokens, D), slim], bits, 4
     )
@@ -1771,9 +1841,9 @@
         own_grads[2],
         own_grads[3],
         grad_w_down,
-        expert_grads[0].astype(f32).T[None],
-        expert_grads[1].astype(f32).T[None],
-        expert_grads[2].astype(f32)[None],
+        expert_grads[0].T[None],
+        expert_grads[1].T[None],
+        expert_grads[2][None],
     )
 
 

time: 843 us -> 829 us (0.983)
  other arithmetic: 48.5 us -> 33.8 us
  local copies, waits for them, and re-layouts: 31.1 us -> 22.5 us
    pallas_call x0 -> x1, Pallas kernels: none -> 13.3 us  [project_back_rows(): pl.pallas_call(rows_kernel, name='project_back_rows', grid=(length // blo...]
    pallas_call x1, Pallas kernels: 31.6 us -> 20 us  [project_back(): pl.pallas_call(functools.partial(project_back_kernel, scale, copies), nam...]
    broadcast_in_dim x2 -> x0, other arithmetic: 11.2 us -> none  [the longest x1 5.94 us: shards(): expert_grads[1].astype(f32).T[None]]
  transfers between devices with their start and end apart: 18 -> 16, of which waited for: 1 -> 2; matrix products, arithmetic and copies ran while one was open for 8% -> 4% of each run, Pallas kernels for 41% -> 31%
where the time goes in v4:
time: 829 us; the launch traced here: 822 us
  Pallas kernels  723 us (87%)
  other arithmetic  33.8 us (4%)
  starting transfers between devices  26.5 us (3%)
  local copies, waits for them, and re-layouts  22.5 us (3%)
  between operations  8.74 us (1%)
    pallas_call x4, Pallas kernels, scatter_ctx(): pl.pallas_call(functools.partial(scatter_kernel, parts, bits, events, cou...  278 us
    pallas_call x1, Pallas kernels, experts_back(): pl.pallas_call(functools.partial(experts_back_kernel, groups, plan, parts...  97.7 us
    pallas_call x1, Pallas kernels, experts(): pl.pallas_call(functools.partial(experts_kernel, groups, plan, parts, bit...  85.3 us
    pallas_call x1, Pallas kernels, gather_ctx(): pl.pallas_call(functools.partial(gather_kernel, parts, bits, events, coun...  79.2 us
    pallas_call x1, Pallas kernels, gather_multiply(): pl.pallas_call(functools.partial(gather_multiply_kernel, parts, bits, eve...  68.9 us
    pallas_call x1, Pallas kernels, attend_back(): pl.pallas_call(functools.partial(attend_back_kernel, block, count), name=...  24.3 us
    all_to_all x4, starting transfers between devices, exchange(): lax.all_to_all(packed, 'ctx', split_axis=0, concat_axis=0, tiled=True)  22.8 us
    pallas_call x1, Pallas kernels, project_back(): pl.pallas_call(functools.partial(project_back_kernel, scale, copies), nam...  20 us
  transfers between devices with their start and end apart: 16, of which 2 were waited for; matrix products, arithmetic and copies ran while one was open for 4% of the time, Pallas kernels for 31%

profile of v4, /device:TPU:0, one launch (start us, length us, event | category | flops | bytes accessed | tf_op | source)
XLA Modules:
  0.0 821.7 jit_solution(17814342762256379296)
XLA Ops:
  1.6 5.5 multiply_sine_fusion
  8.2 79.2 %gather_ctx.1 = (bf16[16,128,2048]{2,1,0:T(8,128)(2,1)}, bf16[16,64,640]{2,1,0:T(8,128)(2,1)}) custom-call(bf16[128,2048]{1,0:T(8,128)(2,1)} %bitcast.124, bf16[64,640]{1,0:T(8,128)(2,1)} %concatenate.28.refs_1_), custom_call_target="tpu_custom_call" | custom-call | tf_op jit(solution)/shard_map/gather_ctx/pallas_call | solution.py:185
  88.5 1.0 maximum_maximum_fusion
  89.5 6.4 all-to-all-start
  98.1 1.0 reshape.278
  99.4 1.3 copy.130.first_ref
  100.8 1.0 reshape.279
  102.0 1.1 fusion.10
  104.2 7.1 all-to-all-done.mine_ref
  111.3 4.4 all-to-all-start.1
  115.8 1.0 select_bitcast_fusion.3
  117.0 1.1 pad.15.refs_7_.refs_11_
  118.8 9.0 %assemble.1 = (bf16[2048,896]{1,0:T(8,128)(2,1)}, bf16[512,256]{1,0:T(8,128)(2,1)}, f32[8,2048]{1,0:T(8,128)}) custom-call(bf16[16,64,256]{2,1,0:T(8,128)(2,1)} %copy-done.8, bf16[16,64,256]{2,1,0:T(8,128)(2,1)} %copy-done.11, bf16[16,64,640]{2,1,0:T(8,128)(2,1)} %get-tuple-element.85.mine_n_ref, bf16[16,64,640]{2,1,0:T(8,128)(2,1)} %collective-permute-done.1.other_n_ref), custom_call_target="tpu_custom_call" | custom-call | tf_op jit(solution)/shard_map/assemble/pallas_call | solution.py:655
  127.8 1.6 fusion.42
  130.1 17.2 %project.1 = (bf16[2048,2048]{1,0:T(8,128)(2,1)}, bf16[2048,256]{1,0:T(8,128)(2,1)}, bf16[2048,256]{1,0:T(8,128)(2,1)}, bf16[2048,128]{1,0:T(8,128)(2,1)}, bf16[...) custom-call(bf16[2048,2048]{1,0:T(8,128)(2,1)} %bitcast.158, f32[1,2048]{1,0:T(1,128)} %get-tuple-element.177.gain_ref, ...), custom_call_target="tpu_custom_call" | custom-call | flops 7516192768 | bytes 25165824 | tf_op jit(solution)/shard_map/project/pallas_call | solution.py:834
  147.4 13.6 %attend.1 = (f32[2048,128]{1,0:T(8,128)}, f32[1,2048]{1,0:T(1,128)}, bf16[2048,2048]{1,0:T(8,128)(2,1)}) custom-call(bf16[2048,256]{1,0:T(8,128)(2,1)} %get-tuple-element.91.q_ref, bf16[2048,256]{1,0:T(8,128)(2,1)} %get-tuple-element.92.k_ref, bf16[2048,128]{1,0:T(8,128)(2,1)} %get-tuple-element.93.v_ref, s32[2048,1]{1,0:T(8,128)} %copy.130.first_ref, ...), custom_call_target="tpu_custom_call" | custom-call | flops 1342177280 | bytes 4096000 | tf_op jit(solution)/shard_map/attend/pallas_call | solution.py:503
  160.9 73.6 %scatter_ctx.4 = f32[128,2048]{1,0:T(8,128)} custom-call(bf16[16,128,2048]{2,1,0:T(8,128)(2,1)} %bitcast.122), custom_call_target="tpu_custom_call" | custom-call | tf_op jit(solution)/shard_map/scatter_ctx/pallas_call | solution.py:457
  234.5 1.5 multiply_reduce_fusion.3
  236.1 0.9 multiply_convert_fusion.x_ref
  238.9 1.4 select_bitcast_fusion.1
  240.5 1.5 copy.143
  242.1 85.3 %experts.1 = (bf16[16,128,2048]{2,1,0:T(8,128)(2,1)}, bf16[16,128,2048]{2,1,0:T(8,128)(2,1)}, bf16[1152,2048]{1,0:T(8,128)(2,1)}, bf16[2048,256]{1,0:T(8,128)(2,...) custom-call(bf16[128,2048]{1,0:T(8,128)(2,1)} %multiply_convert_fusi, ...), custom_call_target="tpu_custom_call" | custom-call | tf_op jit(solution)/shard_map/experts/pallas_call | solution.py:1239
  327.4 62.9 %scatter_ctx.5 = f32[128,2048]{1,0:T(8,128)} custom-call(bf16[16,128,2048]{2,1,0:T(8,128)(2,1)} %get-tuple-element.97.refs_0_), custom_call_target="tpu_custom_call" | custom-call | tf_op jit(solution)/shard_map/scatter_ctx/pallas_call | solution.py:457
  390.3 2.2 fusion.38.x_ref
  392.5 97.7 %experts_back.1 = (bf16[16,128,2048]{2,1,0:T(8,128)(2,1)}, bf16[16,128,2048]{2,1,0:T(8,128)(2,1)}, bf16[1152,2048]{1,0:T(8,128)(2,1)}, bf16[1152,704]{1,0:T(8,12...) custom-call(bf16[128,2048]{1,0:T(8,128)(2,1)} %fusion.38.x_ref, ...), custom_call_target="tpu_custom_call" | custom-call | tf_op jit(solution)/shard_map/experts_back/pallas_call | solution.py:1458
  490.3 58.2 %scatter_ctx.6 = f32[128,2048]{1,0:T(8,128)} custom-call(bf16[16,128,2048]{2,1,0:T(8,128)(2,1)} %get-tuple-element.107.refs_0_), custom_call_target="tpu_custom_call" | custom-call | tf_op jit(solution)/shard_map/scatter_ctx/pallas_call | solution.py:457
  548.5 2.4 dynamic-slice_bitcast_fusion
  551.0 1.2 multiply_reduce_fusion
  552.9 1.5 collective-permute-start.8
  554.4 3.1 fusion.39
  557.4 68.9 %gather_multiply.1 = (bf16[16,128,2048]{2,1,0:T(8,128)(2,1)}, bf16[704,2048]{1,0:T(8,128)(2,1)}, bf16[704,2048]{1,0:T(8,128)(2,1)}, bf16[704,2048]{1,0:T(8,128)(2,1)}) custom-call(bf16[128,2048]{1,0:T(8,128)(2,1)} %get-tuple-element.155.x_ref, bf16[1152,2048]{1,0:T(8,128)(2,1)} %get-tuple-element.108.rows_ref, bf16[1152,2048]{1,0:T(8,128)(2,1)} %get-tuple-element.109.dy_ref, ...), custom_call_target="tpu_custom_call" | custom-call | tf_op jit(solution)/shard_map/gather_multiply/pallas_call | solution.py:339
  631.1 2.5 fusion.11
  633.6 5.0 all-to-all-start.2
  638.6 1.5 slice.70
  640.9 1.3 copy.145.extra_ref
  642.2 1.9 bitcast_add_fusion
  644.1 24.3 %attend_back.1 = (f32[2048,256]{1,0:T(8,128)}, f32[2048,256]{1,0:T(8,128)}, f32[2048,128]{1,0:T(8,128)}, f32[128,2048]{1,0:T(8,128)}, f32[704,2048]{1,0:T(8,128)...) custom-call(bf16[2048,256]{1,0:T(8,128)(2,1)} %get-tuple-element.91.q_ref, bf16[2048,256]{1,0:T(8,128)(2,1)} %get-tuple-element.92.k_ref, ...), custom_call_target="tpu_custom_call" | custom-call | flops 3489660928 | bytes 8192000 | tf_op jit(solution)/shard_map/attend_back/pallas_call | solution.py:580
  668.4 1.1 fusion.16
  670.1 20.0 %project_back.1 = (bf16[2048,896]{1,0:T(8,128)(2,1)}, f32[2048,896]{1,0:T(8,128)}, f32[512,256]{1,0:T(8,128)}) custom-call(f32[2048,256]{1,0:T(8,128)} %get-tuple-element.125.dq_ref, f32[2048,256]{1,0:T(8,128)} %get-tuple-element.126.dk_ref, f32[2048,128]{1,0:T(8,128)} %get-tuple-element.127.dv_ref, f32[2048,512]{1,0:T(8,128)} %get-tuple-element.128.raw_ref, ...), custom_call_target="tpu_custom_call" | custom-call | flops 15032385536 | bytes 25165824 | tf_op jit(solution)/shard_map/project_back/pallas_call | solution.py:916
  690.0 13.1 %finish.1 = (bf16[16,64,256]{2,1,0:T(8,128)(2,1)}, bf16[16,64,640]{2,1,0:T(8,128)(2,1)}) custom-call(f32[2048,896]{1,0:T(8,128)} %get-tuple-element.132.gw_ref, f32[512,256]{1,0:T(8,128)} %get-tuple-element.133.gwe_ref, bf16[2048,896]{1,0:T(8,128)(2,1)} %get-tuple-element.87.w_ref, bf16[512,256]{1,0:T(8,128)(2,1)} %get-tuple-element.88.we_ref, ...), custom_call_target="tpu_custom_call" | custom-call | tf_op jit(solution)/shard_map/finish/pallas_call | solution.py:733
  703.1 7.0 all-to-all-start.3
  710.1 1.9 bitcast_add_fusion.1
  713.4 13.3 %project_back_rows.1 = bf16[2048,2048]{1,0:T(8,128)(2,1)} custom-call(bf16[2048,896]{1,0:T(8,128)(2,1)} %get-tuple-element.131.grads_ref, bf16[2048,896]{1,0:T(8,128)(2,1)} %get-tuple-element.87.w_ref), custom_call_target="tpu_custom_call" | custom-call | flops 7516192768 | bytes 16777216 | tf_op jit(solution)/shard_map/project_back_rows/pallas_call | solution.py:961
  726.6 83.6 %scatter_ctx.7 = (f32[128,2048]{1,0:T(8,128)}, f32[64,640]{1,0:T(8,128)}) custom-call(bf16[16,128,2048]{2,1,0:T(8,128)(2,1)} %bitcast.121, bf16[16,64,640]{2,1,0:T(8,128)(2,1)} %get-tuple-element.136.refs_1_), custom_call_target="tpu_custom_call" | custom-call | tf_op jit(solution)/shard_map/scatter_ctx/pallas_call | solution.py:457
  810.2 1.6 slice_reduce_fusion
  812.8 1.5 fusion.4
  815.3 3.0 spread.1
  818.4 1.3 fusion.8
  (139 shorter events, 15.1 us)
Async XLA Ops:
  0.6 6.5 copy-start.27
  0.7 6.6 copy-start.26
  0.7 6.7 copy-start.25
  0.7 6.8 copy-start.21
  0.7 86.9 %copy-start.20 = (bf16[16,4096]{1,0:T(8,128)(2,1)S(1)}, bf16[16,4096]{1,0:T(8,128)(2,1)}, u32[]{:S(2)}) copy-start(bf16[16,4096]{1,0:T(8,128)(2,1)} %param.27) | copy-start | bytes 393220
  0.7 87.0 %copy-start.12 = (bf16[64,3072]{1,0:T(8,128)(2,1)S(1)}, bf16[64,3072]{1,0:T(8,128)(2,1)}, u32[]{:S(2)}) copy-start(bf16[64,3072]{1,0:T(8,128)(2,1)} %param.24) | copy-start | bytes 1179652
  1.6 97.9 %copy-start.18 = (s32[2048]{0:T(1024)}, s32[2048]{0:T(1024)S(1)}, u32[]{:S(2)}) copy-start(s32[2048]{0:T(1024)S(1)} %select_reduce_fusion.1) | copy-start | bytes 24580
  87.5 30.6 %collective-permute-start.1 = (bf16[16,64,640]{2,1,0:T(8,128)(2,1)}, bf16[16,64,640]{2,1,0:T(8,128)(2,1)}, u32[]{:S(2)}, u32[]{:S(2)}) collective-permute-start(bf16[16,64,640]{2,1,0:T(8,128)(2,1)} %get-tuple-element.85.mine_n_ref), channel_id=1, source_target_pairs={{0,1},{1,0},{2,3},{3,2},{4,5},{5,4},{6,7},{7,6},{8,9},{9,8},{10,11... | collective-permute-start | bytes 3932168 | tf_op jit(solution)/shard_map/ppermute | solution.py:1502
  87.7 8.2 copy-start.17
  87.7 8.4 %copy-start.15 = (bf16[88,2048]{1,0:T(8,128)(2,1)S(1)}, bf16[88,2048]{1,0:T(8,128)(2,1)}, u32[]{:S(2)}) copy-start(bf16[88,2048]{1,0:T(8,128)(2,1)} %param.32) | copy-start | bytes 1081348
  87.7 9.2 %copy-start.23 = (f32[1,128,6]{1,0,2:T(1,128)S(1)}, f32[1,128,6]{1,0,2:T(1,128)}, u32[]{:S(2)}) copy-start(f32[1,128,6]{1,0,2:T(1,128)} %param.22) | copy-start | bytes 9220
  87.7 9.3 %copy-start.24 = (s32[1,128,6]{1,0,2:T(1,128)S(1)}, s32[1,128,6]{1,0,2:T(1,128)}, u32[]{:S(2)}) copy-start(s32[1,128,6]{1,0,2:T(1,128)} %param.21) | copy-start | bytes 9220
  88.4 9.7 %copy-start.13 = (bf16[64,2816]{1,0:T(8,128)(2,1)S(1)}, bf16[64,2816]{1,0:T(8,128)(2,1)}, u32[]{:S(2)}) copy-start(bf16[64,2816]{1,0:T(8,128)(2,1)} %param.30) | copy-start | bytes 1081348
  89.5 21.8 %all-to-all-start = ((bf16[16,64,256]{2,1,0:T(8,128)(2,1)}), bf16[16,64,256]{2,1,0:T(8,128)(2,1)S(1)}, u32[]{:S(2)}, u32[]{:S(2)}) async-start(bf16[16,64,256]{2,1,0:T(8,128)(2,1)} %maximum_maximum_fusion), calls=%async_computation | async-start | bytes 1048576 | tf_op jit(solution)/shard_map/all_to_all | solution.py:1563
  95.9 7.2 collective-permute-start.2
  96.2 19.6 %collective-permute-start.7 = (bf16[88,2048]{1,0:T(8,128)(2,1)S(1)}, bf16[88,2048]{1,0:T(8,128)(2,1)}, u32[]{:S(2)}, u32[]{:S(2)}) collective-permute-start(bf16[88,2048]{1,0:T(8,128)(2,1)S(1)} %copy-done.15), channel_id=1, source_target_pairs={{0,1},{1,0},{2,3},{3,2},{4,5},{5,4},{6,7},{7,6},{8,9},{9,8},{10,11... | collective-permute-start | bytes 1081352 | tf_op jit(solution)/shard_map/ppermute | solution.py:1502
  96.5 145.6 %collective-permute-start.3 = (bf16[704,2048]{1,0:T(8,128)(2,1)}, bf16[704,2048]{1,0:T(8,128)(2,1)}, u32[]{:S(2)}, u32[]{:S(2)}) collective-permute-start(bf16[704,2048]{1,0:T(8,128)(2,1)} %bitcast.23.refs_0_.refs_4_), channel_id=1, source_target_pairs={{0,1},{1,0},{2,3},{3,2},{4,5},{5,4},{6,7},{7,6},{8,9},{9,8},{10,11... | collective-permute-start | bytes 8650760 | tf_op jit(solution)/shard_map/ppermute | solution.py:1502
  96.7 145.4 %collective-permute-start.4 = (bf16[704,2048]{1,0:T(8,128)(2,1)}, bf16[704,2048]{1,0:T(8,128)(2,1)}, u32[]{:S(2)}, u32[]{:S(2)}) collective-permute-start(bf16[704,2048]{1,0:T(8,128)(2,1)} %bitcast.25.refs_1_.refs_5_), channel_id=1, source_target_pairs={{0,1},{1,0},{2,3},{3,2},{4,5},{5,4},{6,7},{7,6},{8,9},{9,8},{10,11... | collective-permute-start | bytes 8650760 | tf_op jit(solution)/shard_map/ppermute | solution.py:1502
  98.0 2.8 copy-start.14
  103.1 139.0 %collective-permute-start.5 = (bf16[704,2048]{1,0:T(8,128)(2,1)}, bf16[704,2048]{1,0:T(8,128)(2,1)}, u32[]{:S(2)}, u32[]{:S(2)}) collective-permute-start(bf16[704,2048]{1,0:T(8,128)(2,1)} %bitcast.26.refs_2_.refs_6_), channel_id=1, source_target_pairs={{0,1},{1,0},{2,3},{3,2},{4,5},{5,4},{6,7},{7,6},{8,9},{9,8},{10,11... | collective-permute-start | bytes 8650760 | tf_op jit(solution)/shard_map/ppermute | solution.py:1502
  111.3 5.6 copy-start.8
  111.3 124.7 %all-to-all-start.1 = ((bf16[16,64,512]{2,1,0:T(8,128)(2,1)}), bf16[16,64,512]{2,1,0:T(8,128)(2,1)S(1)}, u32[]{:S(2)}, u32[]{:S(2)}) async-start(bf16[16,64,512]{2,1,0:T(8,128)(2,1)} %fusion.10), calls=%async_computation.1 | async-start | bytes 2097152 | tf_op jit(solution)/shard_map/all_to_all | solution.py:1563
  115.8 2.3 collective-permute-start
  118.0 0.8 copy-start.11
  160.9 73.6 %copy-start.2 = (bf16[1,128,2048]{2,1,0:T(8,128)(2,1)S(1)}, bf16[1,128,2048]{2,1,0:T(8,128)(2,1)}, u32[]{:S(2)}) copy-start(bf16[1,128,2048]{2,1,0:T(8,128)(2,1)} %param.18) | copy-start | bytes 1572868
  236.1 2.9 collective-permute-start.6
  237.7 2.6 copy-start.19
  327.4 63.0 %copy-start.3 = (bf16[1,128,2048]{2,1,0:T(8,128)(2,1)S(1)}, bf16[1,128,2048]{2,1,0:T(8,128)(2,1)}, u32[]{:S(2)}) copy-start(bf16[1,128,2048]{2,1,0:T(8,128)(2,1)} %param.19) | copy-start | bytes 1572868
  490.3 60.7 %copy-start.4 = (bf16[1,128,2048]{2,1,0:T(8,128)(2,1)S(1)}, bf16[1,128,2048]{2,1,0:T(8,128)(2,1)}, u32[]{:S(2)}) copy-start(bf16[1,128,2048]{2,1,0:T(8,128)(2,1)} %param.19) | copy-start | bytes 1572868
  548.5 2.5 copy-start
  548.5 2.5 copy-start.1
  551.0 80.1 %collective-permute-start.9 = (bf16[16,64,512]{2,1,0:T(8,128)(2,1)}, bf16[16,64,512]{2,1,0:T(8,128)(2,1)}, u32[]{:S(2)}, u32[]{:S(2)}) collective-permute-start(bf16[16,64,512]{2,1,0:T(8,128)(2,1)} %dynamic-slice_bitcast_fusion), channel_id=1, source_target_pairs={{0,1},{1,0},{2,3},{3,2},{4,5},{5,4},{6,7},{7,6},{8,9},{9,8},{10,11... | collective-permute-start | bytes 3145736 | tf_op jit(solution)/shard_map/ppermute | solution.py:1502
  552.9 73.5 %collective-permute-start.8 = (f32[1,1]{1,0:T(1,128)}, f32[1,1]{1,0:T(1,128)}, u32[]{:S(2)}, u32[]{:S(2)}) collective-permute-start(f32[1,1]{1,0:T(1,128)} %bitcast.39), channel_id=1, source_target_pairs={{0,1},{1,0},{2,3},{3,2},{4,5},{5,4},{6,7},{7,6},{8,9},{9,8},{10,11... | collective-permute-start | bytes 20 | tf_op jit(solution)/shard_map/ppermute | solution.py:1502
  557.4 73.6 %copy-start.10 = (bf16[2048,512]{1,0:T(8,128)(2,1)S(1)}, bf16[2048,512]{1,0:T(8,128)(2,1)}, u32[]{:S(2)}) copy-start(bf16[2048,512]{1,0:T(8,128)(2,1)} %get-tuple-element.106) | copy-start | bytes 6291460
  633.6 36.4 %all-to-all-start.2 = ((bf16[16,64,512]{2,1,0:T(8,128)(2,1)}), bf16[16,64,512]{2,1,0:T(8,128)(2,1)S(1)}, u32[]{:S(2)}, u32[]{:S(2)}) async-start(bf16[16,64,512]{2,1,0:T(8,128)(2,1)} %fusion.11), calls=%async_computation.2 | async-start | bytes 2097152 | tf_op jit(solution)/shard_map/all_to_all | solution.py:1563
  640.2 2.0 collective-permute-start.11
  669.5 40.6 %collective-permute-start.10 = (bf16[64,2048]{1,0:T(8,128)(2,1)S(1)}, bf16[64,2048]{1,0:T(8,128)(2,1)S(1)}, u32[]{:S(2)}, u32[]{:S(2)}) collective-permute-start(bf16[64,2048]{1,0:T(8,128)(2,1)S(1)} %fusion.16), channel_id=1, source_target_pairs={{0,1},{1,0},{2,3},{3,2},{4,5},{5,4},{6,7},{7,6},{8,9},{9,8},{10,11... | collective-permute-start | bytes 786440 | tf_op jit(solution)/shard_map/ppermute | solution.py:1502
  670.1 42.0 %copy-start.5 = (bf16[16,64,512]{2,1,0:T(8,128)(2,1)}, bf16[16,64,512]{2,1,0:T(8,128)(2,1)S(1)}, u32[]{:S(2)}) copy-start(bf16[16,64,512]{2,1,0:T(8,128)(2,1)S(1)} %all-to-all-done.2.pack_s_ref) | copy-start | bytes 3145732
  703.1 23.5 %all-to-all-start.3 = ((bf16[16,64,256]{2,1,0:T(8,128)(2,1)}), bf16[16,64,256]{2,1,0:T(8,128)(2,1)S(1)}, u32[]{:S(2)}, u32[]{:S(2)}) async-start(bf16[16,64,256]{2,1,0:T(8,128)(2,1)} %get-tuple-element.134), calls=%async_computation.3 | async-start | bytes 1048576 | tf_op jit(solution)/shard_map/all_to_all | solution.py:1563
  726.6 83.6 %copy-start.9 = (bf16[16,64,256]{2,1,0:T(8,128)(2,1)}, bf16[16,64,256]{2,1,0:T(8,128)(2,1)S(1)}, u32[]{:S(2)}) copy-start(bf16[16,64,256]{2,1,0:T(8,128)(2,1)S(1)} %all-to-all-done.3.pack_ref) | copy-start | bytes 1572868
  726.6 86.1 %copy-start.22 = (f32[1,2048]{1,0:T(1,128)S(1)}, f32[1,2048]{1,0:T(1,128)}, u32[]{:S(2)}) copy-start(f32[1,2048]{1,0:T(1,128)} %get-tuple-element.177.gain_ref) | copy-start | bytes 24580
  810.2 8.1 copy-start.6
  810.2 8.1 copy-start.7
  818.4 1.3 copy-start.16

commit v5 on v4

--- a/solution.py
+++ b/solution.py
@@ -534,7 +534,9 @@
     block, count, q_ref, k_ref, v_ref, m_ref, att_ref, wo_ref, first_ref, log_ref,
     *refs,
 ):
-    lows, (dq_ref, dk_ref, dv_ref, gwo_ref), wides = refs[:3], refs[3:7], refs[7:]
+    few = (len(refs) - 4) // 2
+    lows, (dq_ref, dk_ref, dv_ref, gwo_ref) = refs[:few], refs[few : few + 4]
+    wides = refs[few + 4 :]
     step = pl.program_id(0)
     for low_ref, wide_ref in zip(lows, wides):
         wide_ref[...] = low_ref[...].astype(f32)
@@ -598,8 +600,9 @@
             row(),
             row(),
         ]
-        + [some] * 3,
-        out_specs=(part(WIDE), whole(length, WIDE), whole(length, DV), whole(DV, D)) + (some,) * 3,
+        + [some] * len(lows),
+        out_specs=(part(WIDE), whole(length, WIDE), whole(length, DV), whole(DV, D))
+        + (some,) * len(lows),
         compiler_params=pltpu.CompilerParams(vmem_limit_bytes=60 << 20),
         cost_estimate=pl.CostEstimate(
             flops=length * length * (3 * (DN + DR) + 2 * DV),
@@ -951,25 +954,34 @@
     )
 
 
-def rows_kernel(grads_ref, w_ref, part_ref):
+def rows_kernel(grads_ref, w_ref, low_ref, part_ref, wide_ref):
+    wide_ref[...] = low_ref[...].astype(f32)
     part_ref[...] = dot_last(grads_ref[...], w_ref[...]).astype(bf16)
 
 
-def project_back_rows(grads, w_cat):
+def project_back_rows(grads, w_cat, low):
     length, width = grads.shape
     block = min(512, length)
+    count = length // block
+    tall, wide = low.shape
+    piece = 176 if tall % 176 == 0 else tall
+    steps = tall // piece
+    some = pl.BlockSpec((piece, wide), lambda i: (i * steps // count, 0))
     return pl.pallas_call(
         rows_kernel,
         name="project_back_rows",
         grid=(length // block,),
-        out_shape=jax.ShapeDtypeStruct((length, D), bf16),
-        in_specs=[by_rows(block, width), fixed((D, width))],
-        out_specs=by_rows(block, D),
+        out_shape=(
+            jax.ShapeDtypeStruct((length, D), bf16),
+            jax.ShapeDtypeStruct((tall, wide), f32),
+        ),
+        in_specs=[by_rows(block, width), fixed((D, width)), some],
+        out_specs=(by_rows(block, D), some),
         compiler_params=pltpu.CompilerParams(vmem_limit_bytes=60 << 20),
         cost_estimate=pl.CostEstimate(
             flops=2 * length * D * width, bytes_accessed=length * D * 4, transcendentals=0
         ),
-    )(grads, w_cat)
+    )(grads, w_cat, low)
 
 
 class Gather:
@@ -1452,7 +1464,7 @@
     half = weights[0].shape[0]
     width = shared[1].shape[0]
     pieces = 3 * shares + 3 + size // unit
-    groups, plan = gather_plan(parts, bits, events, 90.0, size, pieces, 15.0)
+    groups, plan = gather_plan(parts, bits, events, 150.0, size, pieces, 15.0)
     anywhere = pl.BlockSpec(memory_space=pl.ANY)
     inside = pl.BlockSpec(memory_space=pltpu.VMEM)
     return pl.pallas_call(
@@ -1737,7 +1749,7 @@
     packed_s = exchange(grad_shared)
     loss_parts = packed_s[:, 0, part_s : part_s + 3].astype(f32)
     loss_value = jnp.sum(loss_parts) / (length * groups * D)
-    grad_query, grad_keys, grad_values, grad_w_output, *expert_grads = attend_back(
+    grad_query, grad_keys, grad_values, grad_w_output, *wide_grads = attend_back(
         queries,
         keys,
         values,
@@ -1746,7 +1758,7 @@
         w_output,
         first_pos[None, :],
         log_total,
-        expert_grads,
+        expert_grads[:2],
     )
     grad_query, packed_s = lax.optimization_barrier((grad_query, packed_s))
     grad_w_output = own_part(grad_w_output, 0).reshape(groups, slab, D)
@@ -1803,7 +1815,7 @@
         ).astype(bf16)
         slim, first = by_owner(slim), padded(by_owner(first), block_q)
     packed = exchange(first)
-    partial = project_back_rows(grads_cat, w_cat)
+    partial, last_grad = project_back_rows(grads_cat, w_cat, expert_grads[2])
     partial, packed = lax.optimization_barrier((partial, packed))
     grad_act_one, grad_narrow = scatter_ctx(
         [partial.reshape(cycle, tokens, D), slim], bits, 4
@@ -1841,9 +1853,9 @@
         own_grads[2],
         own_grads[3],
         grad_w_down,
-        expert_grads[0].T[None],
-        expert_grads[1].T[None],
-        expert_grads[2][None],
+        wide_grads[0].T[None],
+        wide_grads[1].T[None],
+        last_grad[None],
     )
 
 

time: 829 us -> 824 us (level)
  no operation moved by 1% of the time
where the time goes in v5:
time: 824 us; the launch traced here: 817 us
  Pallas kernels  719 us (87%)
  other arithmetic  33.7 us (4%)
  starting transfers between devices  25.4 us (3%)
  local copies, waits for them, and re-layouts  22.5 us (3%)
  between operations  9.02 us (1%)
    pallas_call x4, Pallas kernels, scatter_ctx(): pl.pallas_call(functools.partial(scatter_kernel, parts, bits, events, cou...  276 us
    pallas_call x1, Pallas kernels, experts_back(): pl.pallas_call(functools.partial(experts_back_kernel, groups, plan, parts...  95.2 us
    pallas_call x1, Pallas kernels, experts(): pl.pallas_call(functools.partial(experts_kernel, groups, plan, parts, bit...  85.1 us
    pallas_call x1, Pallas kernels, gather_ctx(): pl.pallas_call(functools.partial(gather_kernel, parts, bits, events, coun...  79.2 us
    pallas_call x1, Pallas kernels, gather_multiply(): pl.pallas_call(functools.partial(gather_multiply_kernel, parts, bits, eve...  70.4 us
    pallas_call x1, Pallas kernels, attend_back(): pl.pallas_call(functools.partial(attend_back_kernel, block, count), name=...  23 us
    all_to_all x4, starting transfers between devices, exchange(): lax.all_to_all(packed, 'ctx', split_axis=0, concat_axis=0, tiled=True)  21.8 us
    pallas_call x1, Pallas kernels, project_back(): pl.pallas_call(functools.partial(project_back_kernel, scale, copies), nam...  20 us
  transfers between devices with their start and end apart: 16, of which 2 were waited for; matrix products, arithmetic and copies ran while one was open for 4% of the time, Pallas kernels for 31%

profile of v5, /device:TPU:0, one launch (start us, length us, event | category | flops | bytes accessed | tf_op | source)
XLA Modules:
  0.0 816.8 jit_solution(1207349335785886675)
XLA Ops:
  1.6 5.5 multiply_sine_fusion
  8.2 79.2 %gather_ctx.1 = (bf16[16,128,2048]{2,1,0:T(8,128)(2,1)}, bf16[16,64,640]{2,1,0:T(8,128)(2,1)}) custom-call(bf16[128,2048]{1,0:T(8,128)(2,1)} %bitcast.123, bf16[64,640]{1,0:T(8,128)(2,1)} %concatenate.28.refs_1_), custom_call_target="tpu_custom_call" | custom-call | tf_op jit(solution)/shard_map/gather_ctx/pallas_call | solution.py:185
  88.5 1.0 maximum_maximum_fusion
  89.5 6.4 all-to-all-start
  98.0 1.0 reshape.278
  99.4 1.3 copy.130.first_ref
  100.8 1.0 reshape.279
  101.9 1.1 fusion.10
  104.2 7.1 all-to-all-done.mine_ref
  111.3 4.4 all-to-all-start.1
  115.8 1.0 select_bitcast_fusion.3
  116.9 1.1 pad.15.refs_7_.refs_11_
  118.8 9.0 %assemble.1 = (bf16[2048,896]{1,0:T(8,128)(2,1)}, bf16[512,256]{1,0:T(8,128)(2,1)}, f32[8,2048]{1,0:T(8,128)}) custom-call(bf16[16,64,256]{2,1,0:T(8,128)(2,1)} %copy-done.8, bf16[16,64,256]{2,1,0:T(8,128)(2,1)} %copy-done.11, bf16[16,64,640]{2,1,0:T(8,128)(2,1)} %get-tuple-element.86.mine_n_ref, bf16[16,64,640]{2,1,0:T(8,128)(2,1)} %collective-permute-done.1.other_n_ref), custom_call_target="tpu_custom_call" | custom-call | tf_op jit(solution)/shard_map/assemble/pallas_call | solution.py:658
  127.8 1.6 fusion.42
  130.1 17.2 %project.1 = (bf16[2048,2048]{1,0:T(8,128)(2,1)}, bf16[2048,256]{1,0:T(8,128)(2,1)}, bf16[2048,256]{1,0:T(8,128)(2,1)}, bf16[2048,128]{1,0:T(8,128)(2,1)}, bf16[...) custom-call(bf16[2048,2048]{1,0:T(8,128)(2,1)} %bitcast.158, f32[1,2048]{1,0:T(1,128)} %get-tuple-element.179.gain_ref, ...), custom_call_target="tpu_custom_call" | custom-call | flops 7516192768 | bytes 25165824 | tf_op jit(solution)/shard_map/project/pallas_call | solution.py:837
  147.3 13.6 %attend.1 = (f32[2048,128]{1,0:T(8,128)}, f32[1,2048]{1,0:T(1,128)}, bf16[2048,2048]{1,0:T(8,128)(2,1)}) custom-call(bf16[2048,256]{1,0:T(8,128)(2,1)} %get-tuple-element.92.q_ref, bf16[2048,256]{1,0:T(8,128)(2,1)} %get-tuple-element.93.k_ref, bf16[2048,128]{1,0:T(8,128)(2,1)} %get-tuple-element.94.v_ref, s32[2048,1]{1,0:T(8,128)} %copy.130.first_ref, ...), custom_call_target="tpu_custom_call" | custom-call | flops 1342177280 | bytes 4096000 | tf_op jit(solution)/shard_map/attend/pallas_call | solution.py:503
  160.9 73.6 %scatter_ctx.4 = f32[128,2048]{1,0:T(8,128)} custom-call(bf16[16,128,2048]{2,1,0:T(8,128)(2,1)} %bitcast.122), custom_call_target="tpu_custom_call" | custom-call | tf_op jit(solution)/shard_map/scatter_ctx/pallas_call | solution.py:457
  234.5 1.5 multiply_reduce_fusion.3
  236.2 0.9 multiply_convert_fusion.x_ref
  238.9 1.4 select_bitcast_fusion.1
  240.5 1.5 copy.143
  242.1 85.1 %experts.1 = (bf16[16,128,2048]{2,1,0:T(8,128)(2,1)}, bf16[16,128,2048]{2,1,0:T(8,128)(2,1)}, bf16[1152,2048]{1,0:T(8,128)(2,1)}, bf16[2048,256]{1,0:T(8,128)(2,...) custom-call(bf16[128,2048]{1,0:T(8,128)(2,1)} %multiply_convert_fusi, ...), custom_call_target="tpu_custom_call" | custom-call | tf_op jit(solution)/shard_map/experts/pallas_call | solution.py:1251
  327.2 63.0 %scatter_ctx.5 = f32[128,2048]{1,0:T(8,128)} custom-call(bf16[16,128,2048]{2,1,0:T(8,128)(2,1)} %get-tuple-element.98.refs_0_), custom_call_target="tpu_custom_call" | custom-call | tf_op jit(solution)/shard_map/scatter_ctx/pallas_call | solution.py:457
  390.2 2.2 fusion.38.x_ref
  392.3 95.2 %experts_back.1 = (bf16[16,128,2048]{2,1,0:T(8,128)(2,1)}, bf16[16,128,2048]{2,1,0:T(8,128)(2,1)}, bf16[1152,2048]{1,0:T(8,128)(2,1)}, bf16[1152,704]{1,0:T(8,12...) custom-call(bf16[128,2048]{1,0:T(8,128)(2,1)} %fusion.38.x_ref, ...), custom_call_target="tpu_custom_call" | custom-call | tf_op jit(solution)/shard_map/experts_back/pallas_call | solution.py:1470
  487.5 55.6 %scatter_ctx.6 = f32[128,2048]{1,0:T(8,128)} custom-call(bf16[16,128,2048]{2,1,0:T(8,128)(2,1)} %get-tuple-element.108.refs_0_), custom_call_target="tpu_custom_call" | custom-call | tf_op jit(solution)/shard_map/scatter_ctx/pallas_call | solution.py:457
  543.2 2.4 dynamic-slice_bitcast_fusion
  545.6 1.2 multiply_reduce_fusion
  547.5 1.4 collective-permute-start.8
  548.9 3.1 fusion.39
  551.9 70.4 %gather_multiply.1 = (bf16[16,128,2048]{2,1,0:T(8,128)(2,1)}, bf16[704,2048]{1,0:T(8,128)(2,1)}, bf16[704,2048]{1,0:T(8,128)(2,1)}, bf16[704,2048]{1,0:T(8,128)(2,1)}) custom-call(bf16[128,2048]{1,0:T(8,128)(2,1)} %get-tuple-element.157.x_ref, bf16[1152,2048]{1,0:T(8,128)(2,1)} %get-tuple-element.109.rows_ref, bf16[1152,2048]{1,0:T(8,128)(2,1)} %get-tuple-element.110.dy_ref, ...), custom_call_target="tpu_custom_call" | custom-call | tf_op jit(solution)/shard_map/gather_multiply/pallas_call | solution.py:339
  627.4 2.5 fusion.11
  629.9 4.1 all-to-all-start.2
  634.0 1.5 slice.70
  636.2 1.4 copy.145.extra_ref
  637.6 1.9 bitcast_add_fusion
  639.5 23.0 %attend_back.1 = (f32[2048,256]{1,0:T(8,128)}, f32[2048,256]{1,0:T(8,128)}, f32[2048,128]{1,0:T(8,128)}, f32[128,2048]{1,0:T(8,128)}, f32[704,2048]{1,0:T(8,128)}, /*index=5*/f32[704,2048]{1,0:T(8,128)}) custom-call(bf16[2048,256]{1,0:T(8,128)(2,1)} %get-tuple-element.92.q_ref, bf16[2048,256]{1,0:T(8,128)(2,1)} %get-tuple-element.93.k_ref, ...), custom_call_target="tpu_custom_call" | custom-call | flops 3489660928 | bytes 8192000 | tf_op jit(solution)/shard_map/attend_back/pallas_call | solution.py:582
  662.4 1.1 fusion.16
  664.1 20.0 %project_back.1 = (bf16[2048,896]{1,0:T(8,128)(2,1)}, f32[2048,896]{1,0:T(8,128)}, f32[512,256]{1,0:T(8,128)}) custom-call(f32[2048,256]{1,0:T(8,128)} %get-tuple-element.125.dq_ref, f32[2048,256]{1,0:T(8,128)} %get-tuple-element.126.dk_ref, f32[2048,128]{1,0:T(8,128)} %get-tuple-element.127.dv_ref, f32[2048,512]{1,0:T(8,128)} %get-tuple-element.128.raw_ref, ...), custom_call_target="tpu_custom_call" | custom-call | flops 15032385536 | bytes 25165824 | tf_op jit(solution)/shard_map/project_back/pallas_call | solution.py:919
  684.0 13.1 %finish.1 = (bf16[16,64,256]{2,1,0:T(8,128)(2,1)}, bf16[16,64,640]{2,1,0:T(8,128)(2,1)}) custom-call(f32[2048,896]{1,0:T(8,128)} %get-tuple-element.134.gw_ref, f32[512,256]{1,0:T(8,128)} %get-tuple-element.135.gwe_ref, bf16[2048,896]{1,0:T(8,128)(2,1)} %get-tuple-element.88.w_ref, bf16[512,256]{1,0:T(8,128)(2,1)} %get-tuple-element.89.we_ref, ...), custom_call_target="tpu_custom_call" | custom-call | tf_op jit(solution)/shard_map/finish/pallas_call | solution.py:736
  697.1 7.0 all-to-all-start.3
  704.1 1.9 bitcast_add_fusion.1
  707.4 14.3 %project_back_rows.1 = (bf16[2048,2048]{1,0:T(8,128)(2,1)}, f32[704,2048]{1,0:T(8,128)}) custom-call(bf16[2048,896]{1,0:T(8,128)(2,1)} %get-tuple-element.131.grads_ref, bf16[2048,896]{1,0:T(8,128)(2,1)} %get-tuple-element.88.w_ref, bf16[704,2048]{1,0:T(8,128)(2,1)} %get-tuple-element.132.low_ref), custom_call_target="tpu_custom_call" | custom-call | flops 7516192768 | bytes 16777216 | tf_op jit(solution)/shard_map/project_back_rows/pallas_call | solution.py:970
  721.7 83.6 %scatter_ctx.7 = (f32[128,2048]{1,0:T(8,128)}, f32[64,640]{1,0:T(8,128)}) custom-call(bf16[16,128,2048]{2,1,0:T(8,128)(2,1)} %bitcast.121, bf16[16,64,640]{2,1,0:T(8,128)(2,1)} %get-tuple-element.138.refs_1_), custom_call_target="tpu_custom_call" | custom-call | tf_op jit(solution)/shard_map/scatter_ctx/pallas_call | solution.py:457
  805.3 1.6 slice_reduce_fusion
  807.9 1.5 fusion.4
  810.4 3.0 spread.1
  813.5 1.3 fusion.8
  (139 shorter events, 15.1 us)
Async XLA Ops:
  0.6 6.5 copy-start.27
  0.7 6.6 copy-start.26
  0.7 6.7 copy-start.25
  0.7 6.8 copy-start.21
  0.7 86.9 %copy-start.20 = (bf16[16,4096]{1,0:T(8,128)(2,1)S(1)}, bf16[16,4096]{1,0:T(8,128)(2,1)}, u32[]{:S(2)}) copy-start(bf16[16,4096]{1,0:T(8,128)(2,1)} %param.27) | copy-start | bytes 393220
  0.7 87.0 %copy-start.12 = (bf16[64,3072]{1,0:T(8,128)(2,1)S(1)}, bf16[64,3072]{1,0:T(8,128)(2,1)}, u32[]{:S(2)}) copy-start(bf16[64,3072]{1,0:T(8,128)(2,1)} %param.24) | copy-start | bytes 1179652
  1.6 97.9 %copy-start.18 = (s32[2048]{0:T(1024)}, s32[2048]{0:T(1024)S(1)}, u32[]{:S(2)}) copy-start(s32[2048]{0:T(1024)S(1)} %select_reduce_fusion.1) | copy-start | bytes 24580
  87.5 30.6 %collective-permute-start.1 = (bf16[16,64,640]{2,1,0:T(8,128)(2,1)}, bf16[16,64,640]{2,1,0:T(8,128)(2,1)}, u32[]{:S(2)}, u32[]{:S(2)}) collective-permute-start(bf16[16,64,640]{2,1,0:T(8,128)(2,1)} %get-tuple-element.86.mine_n_ref), channel_id=1, source_target_pairs={{0,1},{1,0},{2,3},{3,2},{4,5},{5,4},{6,7},{7,6},{8,9},{9,8},{10,11... | collective-permute-start | bytes 3932168 | tf_op jit(solution)/shard_map/ppermute | solution.py:1514
  87.7 8.2 copy-start.17
  87.7 8.4 %copy-start.15 = (bf16[88,2048]{1,0:T(8,128)(2,1)S(1)}, bf16[88,2048]{1,0:T(8,128)(2,1)}, u32[]{:S(2)}) copy-start(bf16[88,2048]{1,0:T(8,128)(2,1)} %param.32) | copy-start | bytes 1081348
  87.7 9.2 %copy-start.23 = (f32[1,128,6]{1,0,2:T(1,128)S(1)}, f32[1,128,6]{1,0,2:T(1,128)}, u32[]{:S(2)}) copy-start(f32[1,128,6]{1,0,2:T(1,128)} %param.22) | copy-start | bytes 9220
  87.7 9.3 %copy-start.24 = (s32[1,128,6]{1,0,2:T(1,128)S(1)}, s32[1,128,6]{1,0,2:T(1,128)}, u32[]{:S(2)}) copy-start(s32[1,128,6]{1,0,2:T(1,128)} %param.21) | copy-start | bytes 9220
  88.3 9.7 %copy-start.13 = (bf16[64,2816]{1,0:T(8,128)(2,1)S(1)}, bf16[64,2816]{1,0:T(8,128)(2,1)}, u32[]{:S(2)}) copy-start(bf16[64,2816]{1,0:T(8,128)(2,1)} %param.30) | copy-start | bytes 1081348
  89.5 21.8 %all-to-all-start = ((bf16[16,64,256]{2,1,0:T(8,128)(2,1)}), bf16[16,64,256]{2,1,0:T(8,128)(2,1)S(1)}, u32[]{:S(2)}, u32[]{:S(2)}) async-start(bf16[16,64,256]{2,1,0:T(8,128)(2,1)} %maximum_maximum_fusion), calls=%async_computation | async-start | bytes 1048576 | tf_op jit(solution)/shard_map/all_to_all | solution.py:1575
  95.9 7.2 collective-permute-start.2
  96.1 19.6 %collective-permute-start.7 = (bf16[88,2048]{1,0:T(8,128)(2,1)S(1)}, bf16[88,2048]{1,0:T(8,128)(2,1)}, u32[]{:S(2)}, u32[]{:S(2)}) collective-permute-start(bf16[88,2048]{1,0:T(8,128)(2,1)S(1)} %copy-done.15), channel_id=1, source_target_pairs={{0,1},{1,0},{2,3},{3,2},{4,5},{5,4},{6,7},{7,6},{8,9},{9,8},{10,11... | collective-permute-start | bytes 1081352 | tf_op jit(solution)/shard_map/ppermute | solution.py:1514
  96.4 145.6 %collective-permute-start.3 = (bf16[704,2048]{1,0:T(8,128)(2,1)}, bf16[704,2048]{1,0:T(8,128)(2,1)}, u32[]{:S(2)}, u32[]{:S(2)}) collective-permute-start(bf16[704,2048]{1,0:T(8,128)(2,1)} %bitcast.23.refs_0_.refs_4_), channel_id=1, source_target_pairs={{0,1},{1,0},{2,3},{3,2},{4,5},{5,4},{6,7},{7,6},{8,9},{9,8},{10,11... | collective-permute-start | bytes 8650760 | tf_op jit(solution)/shard_map/ppermute | solution.py:1514
  96.6 145.4 %collective-permute-start.4 = (bf16[704,2048]{1,0:T(8,128)(2,1)}, bf16[704,2048]{1,0:T(8,128)(2,1)}, u32[]{:S(2)}, u32[]{:S(2)}) collective-permute-start(bf16[704,2048]{1,0:T(8,128)(2,1)} %bitcast.25.refs_1_.refs_5_), channel_id=1, source_target_pairs={{0,1},{1,0},{2,3},{3,2},{4,5},{5,4},{6,7},{7,6},{8,9},{9,8},{10,11... | collective-permute-start | bytes 8650760 | tf_op jit(solution)/shard_map/ppermute | solution.py:1514
  98.0 2.8 copy-start.14
  103.1 139.0 %collective-permute-start.5 = (bf16[704,2048]{1,0:T(8,128)(2,1)}, bf16[704,2048]{1,0:T(8,128)(2,1)}, u32[]{:S(2)}, u32[]{:S(2)}) collective-permute-start(bf16[704,2048]{1,0:T(8,128)(2,1)} %bitcast.26.refs_2_.refs_6_), channel_id=1, source_target_pairs={{0,1},{1,0},{2,3},{3,2},{4,5},{5,4},{6,7},{7,6},{8,9},{9,8},{10,11... | collective-permute-start | bytes 8650760 | tf_op jit(solution)/shard_map/ppermute | solution.py:1514
  111.3 5.6 copy-start.8
  111.3 124.7 %all-to-all-start.1 = ((bf16[16,64,512]{2,1,0:T(8,128)(2,1)}), bf16[16,64,512]{2,1,0:T(8,128)(2,1)S(1)}, u32[]{:S(2)}, u32[]{:S(2)}) async-start(bf16[16,64,512]{2,1,0:T(8,128)(2,1)} %fusion.10), calls=%async_computation.1 | async-start | bytes 2097152 | tf_op jit(solution)/shard_map/all_to_all | solution.py:1575
  115.7 2.3 collective-permute-start
  118.0 0.8 copy-start.11
  160.9 73.7 %copy-start.2 = (bf16[1,128,2048]{2,1,0:T(8,128)(2,1)S(1)}, bf16[1,128,2048]{2,1,0:T(8,128)(2,1)}, u32[]{:S(2)}) copy-start(bf16[1,128,2048]{2,1,0:T(8,128)(2,1)} %param.18) | copy-start | bytes 1572868
  236.1 2.9 collective-permute-start.6
  237.7 2.6 copy-start.19
  327.1 63.0 %copy-start.3 = (bf16[1,128,2048]{2,1,0:T(8,128)(2,1)S(1)}, bf16[1,128,2048]{2,1,0:T(8,128)(2,1)}, u32[]{:S(2)}) copy-start(bf16[1,128,2048]{2,1,0:T(8,128)(2,1)} %param.19) | copy-start | bytes 1572868
  487.5 58.1 %copy-start.4 = (bf16[1,128,2048]{2,1,0:T(8,128)(2,1)S(1)}, bf16[1,128,2048]{2,1,0:T(8,128)(2,1)}, u32[]{:S(2)}) copy-start(bf16[1,128,2048]{2,1,0:T(8,128)(2,1)} %param.19) | copy-start | bytes 1572868
  543.2 2.5 copy-start
  543.2 2.5 copy-start.1
  545.6 81.7 %collective-permute-start.9 = (bf16[16,64,512]{2,1,0:T(8,128)(2,1)}, bf16[16,64,512]{2,1,0:T(8,128)(2,1)}, u32[]{:S(2)}, u32[]{:S(2)}) collective-permute-start(bf16[16,64,512]{2,1,0:T(8,128)(2,1)} %dynamic-slice_bitcast_fusion), channel_id=1, source_target_pairs={{0,1},{1,0},{2,3},{3,2},{4,5},{5,4},{6,7},{7,6},{8,9},{9,8},{10,11... | collective-permute-start | bytes 3145736 | tf_op jit(solution)/shard_map/ppermute | solution.py:1514
  547.5 74.8 %collective-permute-start.8 = (f32[1,1]{1,0:T(1,128)}, f32[1,1]{1,0:T(1,128)}, u32[]{:S(2)}, u32[]{:S(2)}) collective-permute-start(f32[1,1]{1,0:T(1,128)} %bitcast.39), channel_id=1, source_target_pairs={{0,1},{1,0},{2,3},{3,2},{4,5},{5,4},{6,7},{7,6},{8,9},{9,8},{10,11... | collective-permute-start | bytes 20 | tf_op jit(solution)/shard_map/ppermute | solution.py:1514
  551.9 75.4 %copy-start.10 = (bf16[2048,512]{1,0:T(8,128)(2,1)S(1)}, bf16[2048,512]{1,0:T(8,128)(2,1)}, u32[]{:S(2)}) copy-start(bf16[2048,512]{1,0:T(8,128)(2,1)} %get-tuple-element.107) | copy-start | bytes 6291460
  629.9 34.2 %all-to-all-start.2 = ((bf16[16,64,512]{2,1,0:T(8,128)(2,1)}), bf16[16,64,512]{2,1,0:T(8,128)(2,1)S(1)}, u32[]{:S(2)}, u32[]{:S(2)}) async-start(bf16[16,64,512]{2,1,0:T(8,128)(2,1)} %fusion.11), calls=%async_computation.2 | async-start | bytes 2097152 | tf_op jit(solution)/shard_map/all_to_all | solution.py:1575
  635.5 2.1 collective-permute-start.11
  663.5 40.6 %collective-permute-start.10 = (bf16[64,2048]{1,0:T(8,128)(2,1)S(1)}, bf16[64,2048]{1,0:T(8,128)(2,1)S(1)}, u32[]{:S(2)}, u32[]{:S(2)}) collective-permute-start(bf16[64,2048]{1,0:T(8,128)(2,1)S(1)} %fusion.16), channel_id=1, source_target_pairs={{0,1},{1,0},{2,3},{3,2},{4,5},{5,4},{6,7},{7,6},{8,9},{9,8},{10,11... | collective-permute-start | bytes 786440 | tf_op jit(solution)/shard_map/ppermute | solution.py:1514
  664.1 41.9 %copy-start.5 = (bf16[16,64,512]{2,1,0:T(8,128)(2,1)}, bf16[16,64,512]{2,1,0:T(8,128)(2,1)S(1)}, u32[]{:S(2)}) copy-start(bf16[16,64,512]{2,1,0:T(8,128)(2,1)S(1)} %all-to-all-done.2.pack_s_ref) | copy-start | bytes 3145732
  697.1 24.6 %all-to-all-start.3 = ((bf16[16,64,256]{2,1,0:T(8,128)(2,1)}), bf16[16,64,256]{2,1,0:T(8,128)(2,1)S(1)}, u32[]{:S(2)}, u32[]{:S(2)}) async-start(bf16[16,64,256]{2,1,0:T(8,128)(2,1)} %get-tuple-element.136), calls=%async_computation.3 | async-start | bytes 1048576 | tf_op jit(solution)/shard_map/all_to_all | solution.py:1575
  721.7 83.6 %copy-start.9 = (bf16[16,64,256]{2,1,0:T(8,128)(2,1)}, bf16[16,64,256]{2,1,0:T(8,128)(2,1)S(1)}, u32[]{:S(2)}) copy-start(bf16[16,64,256]{2,1,0:T(8,128)(2,1)S(1)} %all-to-all-done.3.pack_ref) | copy-start | bytes 1572868
  721.7 86.1 %copy-start.22 = (f32[1,2048]{1,0:T(1,128)S(1)}, f32[1,2048]{1,0:T(1,128)}, u32[]{:S(2)}) copy-start(f32[1,2048]{1,0:T(1,128)} %get-tuple-element.179.gain_ref) | copy-start | bytes 24580
  805.3 8.1 copy-start.6
  805.3 8.1 copy-start.7
  813.4 1.3 copy-start.16
